TPU v7x, 128 devices: a whole 4x4x4 slice. The times are simulated.
128 devices in a mesh: ctx: 64 (over z, x, y), head: 2 (over core).
Axes of the slice: x: 4, y: 4, z: 4, core: 2. Of those that a mesh axis runs over, the one named last changes fastest.
Arguments:
- teacher_query: bfloat16 [14336, 5120], P('ctx', 'head'), may hold values from -25 to 25
- teacher_key: bfloat16 [14336, 5120], P('ctx', 'head'), may hold values from -25 to 25
- student_hidden: bfloat16 [14336, 2048], P('ctx'), may hold values from -25 to 25
- w_query: bfloat16 [2048, 2048], P(None, 'head'), may hold values from -0.125 to 0.125
- w_key: bfloat16 [2048, 2048], P(None, 'head'), may hold values from -0.125 to 0.125
- segment_ids: int32 [14336], replicated, may hold values from 0 to 3, never falling along the last dimension, each value on 1 to 7168 neighbouring positions
- block_mask: int32 [64, 7], P('ctx'), may hold values 0 or 1
Outputs:
- grad_hidden: bfloat16 [14336, 2048], P('ctx', 'head')
Inputs may be any that keep to these rules, and one draw needn't show every extreme that they name: `segment_ids`: document numbers never fall along the row; no document is longer than 7168 tokens and one is exactly that long.
All inputs are finite; a program needn't handle non-finite values. No bound on the sum of `block_mask` on one device may be relied on, other than what follows from the above.
Results may differ from a plain program's by a relative error of at most 0.0085.
Values may be sent and summed in bfloat16 or wider, within the bound.
No kernel may reach another device: no remote copies, remote signals or barrier semaphores. Data moves between devices by JAX's collectives and lax.ppermute only.
A program may use at most 256 MiB of HBM per device.

v0:
```python
import math

import jax
import jax.numpy as jnp
from jax import lax
from jax.sharding import PartitionSpec as P

DT = 5120
DS = 2048
HEADS = 64
REACH = 8


def from_behind(block, axis, distance):
    devices = range(lax.axis_size(axis))
    route = [(i - distance, i) for i in devices if i - distance in devices]
    return lax.ppermute(block, axis, route)


def relation_probs(scores, visible):
    masked = jnp.where(visible, scores, -jnp.inf)
    highest = jnp.max(masked, axis=-1, keepdims=True)
    weights = jnp.exp(masked - highest)
    return weights / jnp.sum(weights, axis=-1, keepdims=True)


def visibility(block_id, row_count, reach, segment_ids, mask_row):
    margin = (reach - 1) * row_count
    window_rows = reach * row_count
    first_row = block_id * row_count
    key_places = first_row - margin + jnp.arange(window_rows, dtype=jnp.int32)
    query_places = first_row + jnp.arange(row_count, dtype=jnp.int32)
    padded_segments = jnp.concatenate([jnp.full((margin,), -1, jnp.int32), segment_ids])
    key_segments = lax.dynamic_slice_in_dim(padded_segments, first_row, window_rows)
    query_segments = lax.dynamic_slice_in_dim(padded_segments, first_row + margin, row_count)
    opened = jnp.concatenate([jnp.ones((1,), jnp.int32), mask_row])
    block_open = jnp.repeat(opened[::-1], row_count)
    return (
        (key_places[None, :] >= 0)
        & (key_places[None, :] <= query_places[:, None])
        & (key_segments[None, :] == query_segments[:, None])
        & (block_open[None, :] == 1)
    )


def gather_window(pieces):
    received = [pieces]
    current = pieces
    for distance in range(REACH - 1):
        current = from_behind((current[0], current[1], current[2], current[3]), "ctx", 1)
        received.append(current)
    ordered = received[::-1]
    return tuple(
        (jnp.concatenate([blocks[member] for blocks in ordered], axis=0) for member in range(4))
    )


def return_partials(first_terms, second_terms, row_count):
    carried = (first_terms[:row_count], second_terms[:row_count])
    for block_id in range(1, REACH):
        moved = from_behind((carried[0], carried[1]), "ctx", -1)
        low_row = block_id * row_count
        carried = (
            moved[0] + first_terms[low_row : low_row + row_count],
            moved[1] + second_terms[low_row : low_row + row_count],
        )
    return carried


def relation_terms(teacher_rows, teacher_window, student_rows, student_window, visible):
    width_t = DT // HEADS
    width_s = DS // HEADS
    local_heads = student_rows.shape[1] // width_s
    group = min(8, local_heads)
    query_count = student_rows.shape[0]
    key_count = student_window.shape[0]
    shown = visible[None]

    def columns(values, width, group_index):
        sliced = lax.dynamic_slice_in_dim(values, group_index * group * width, group * width, 1)
        return sliced.reshape(sliced.shape[0], group, width)

    def one_group(group_index, totals):
        query_total, key_total = totals
        teacher_scores = jnp.einsum(
            "qhd,khd->hqk",
            columns(teacher_rows, width_t, group_index),
            columns(teacher_window, width_t, group_index),
            preferred_element_type=jnp.float32,
        ) * (1.0 / math.sqrt(width_t))
        student_a = columns(student_rows, width_s, group_index)
        student_b = columns(student_window, width_s, group_index)
        student_scores = jnp.einsum(
            "qhd,khd->hqk", student_a, student_b, preferred_element_type=jnp.float32
        ) * (1.0 / math.sqrt(width_s))
        difference = relation_probs(student_scores, shown) - relation_probs(teacher_scores, shown)
        coupling = jnp.where(shown, difference * (1.0 / math.sqrt(width_s)), 0.0).astype(
            jnp.bfloat16
        )
        query_part = jnp.einsum(
            "hqk,khd->qhd", coupling, student_b, preferred_element_type=jnp.float32
        ).reshape(query_count, group * width_s)
        key_part = jnp.einsum(
            "hqk,qhd->khd", coupling, student_a, preferred_element_type=jnp.float32
        ).reshape(key_count, group * width_s)
        query_total = lax.dynamic_update_slice_in_dim(
            query_total, query_part, group_index * group * width_s, 1
        )
        key_total = lax.dynamic_update_slice_in_dim(
            key_total, key_part, group_index * group * width_s, 1
        )
        return (query_total, key_total)

    start_totals = (
        jnp.zeros((query_count, student_rows.shape[1]), jnp.float32),
        jnp.zeros((key_count, student_rows.shape[1]), jnp.float32),
    )
    return lax.fori_loop(0, local_heads // group, one_group, start_totals)


def shards(teacher_query, teacher_key, student_hidden, w_query, w_key, segment_ids, block_mask):
    row_count = student_hidden.shape[0]
    student_query = jnp.dot(student_hidden, w_query, preferred_element_type=jnp.float32).astype(
        jnp.bfloat16
    )
    student_key = jnp.dot(student_hidden, w_key, preferred_element_type=jnp.float32).astype(
        jnp.bfloat16
    )
    window = gather_window((teacher_query, teacher_key, student_query, student_key))
    block_id = lax.axis_index("ctx")
    visible = visibility(block_id, row_count, REACH, segment_ids, block_mask[0])
    query_first, key_first = relation_terms(
        teacher_query, window[0], student_query, window[2], visible
    )
    query_second, key_second = relation_terms(
        teacher_key, window[1], student_key, window[3], visible
    )
    back_first, back_second = return_partials(key_first, key_second, row_count)
    grad_query = (query_first + back_first).astype(jnp.bfloat16)
    grad_key = (query_second + back_second).astype(jnp.bfloat16)
    partial_sum = jnp.einsum(
        "tc,dc->td", grad_query, w_query, preferred_element_type=jnp.float32
    ) + jnp.einsum("tc,dc->td", grad_key, w_key, preferred_element_type=jnp.float32)
    return lax.psum_scatter(partial_sum, "head", scatter_dimension=1, tiled=True).astype(
        jnp.bfloat16
    )


def solution(mesh):
    placed = (
        P("ctx", "head"),
        P("ctx", "head"),
        P("ctx", None),
        P(None, "head"),
        P(None, "head"),
        P(),
        P("ctx", None),
    )
    return jax.shard_map(
        shards, mesh=mesh, in_specs=placed, out_specs=P("ctx", "head"), check_vma=False
    )
```

profile of v0, /device:TPU:1, one launch (start us, length us, event | category | flops | bytes accessed | tf_op | source)
XLA Modules:
  0.0 1324.5 jit_solution(12009846696978343277)
XLA Ops:
  14.1 20.9 %collective-permute-done.28 = bf16[224,2560]{1,0:T(8,128)(2,1)S(1)} collective-permute-done((bf16[224,2560]{1,0:T(8,128)(2,1)}, bf16[224,2560]{1,0:T(8,128)(2,1)S(1)}, u32[]{:S(2)}, u32[]{:S(2)}) %collective-permute-start.28) | collective-permute-done | bytes 1146912 | tf_op jit(solution)/shard_map/ppermute | solution.py:17
  39.2 20.5 %collective-permute-done.7 = bf16[224,2560]{1,0:T(8,128)(2,1)S(1)} collective-permute-done((bf16[224,2560]{1,0:T(8,128)(2,1)}, bf16[224,2560]{1,0:T(8,128)(2,1)S(1)}, u32[]{:S(2)}, u32[]{:S(2)}) %collective-permute-start.7) | collective-permute-done | bytes 1146912 | tf_op jit(solution)/shard_map/ppermute | solution.py:17
  63.7 20.4 %collective-permute-done.29 = bf16[224,2560]{1,0:T(8,128)(2,1)S(1)} collective-permute-done((bf16[224,2560]{1,0:T(8,128)(2,1)S(1)}, bf16[224,2560]{1,0:T(8,128)(2,1)S(1)}, u32[]{:S(2)}, u32[]{:S(2)}) %collective-permute-start.29) | collective-permute-done | bytes 1146912 | tf_op jit(solution)/shard_map/ppermute | solution.py:17
  99.7 43.6 %collective-permute-done.21 = bf16[224,1024]{1,0:T(8,128)(2,1)S(1)} collective-permute-done((bf16[224,1024]{1,0:T(8,128)(2,1)}, bf16[224,1024]{1,0:T(8,128)(2,1)S(1)}, u32[]{:S(2)}, u32[]{:S(2)}) %collective-permute-start.21) | collective-permute-done | bytes 458784 | tf_op jit(solution)/shard_map/ppermute | solution.py:17
  166.9 54.9 %collective-permute-done.1 = bf16[224,1024]{1,0:T(8,128)(2,1)S(1)} collective-permute-done((bf16[224,1024]{1,0:T(8,128)(2,1)S(1)}, bf16[224,1024]{1,0:T(8,128)(2,1)S(1)}, u32[]{:S(2)}, u32[]{:S(2)}) %collective-permute-start.1) | collective-permute-done | bytes 458784 | tf_op jit(solution)/shard_map/ppermute | solution.py:17
  225.9 5.7 collective-permute-done.23
  251.3 4.9 collective-permute-start.25
  256.1 54.1 %collective-permute-done.3 = bf16[224,1024]{1,0:T(8,128)(2,1)} collective-permute-done((bf16[224,1024]{1,0:T(8,128)(2,1)S(1)}, bf16[224,1024]{1,0:T(8,128)(2,1)}, u32[]{:S(2)}, u32[]{:S(2)}) %collective-permute-start.3) | collective-permute-done | bytes 458784 | tf_op jit(solution)/shard_map/ppermute | solution.py:17
  310.3 5.0 collective-permute-start.4
  315.3 4.8 collective-permute-done.25
  320.1 5.0 collective-permute-start.26
  330.0 4.9 collective-permute-start.5
  334.9 5.0 collective-permute-done.26
  339.9 4.9 collective-permute-start.27
  370.5 13.6 %collective-permute-done.11 = bf16[224,2560]{1,0:T(8,128)(2,1)} collective-permute-done((bf16[224,2560]{1,0:T(8,128)(2,1)}, bf16[224,2560]{1,0:T(8,128)(2,1)}, u32[]{:S(2)}, u32[]{:S(2)}) %collective-permute-start.11) | collective-permute-done | bytes 1146912 | tf_op jit(solution)/shard_map/ppermute | solution.py:17
  384.1 5.1 collective-permute-start.12
  389.2 19.5 %collective-permute-done.33 = bf16[224,2560]{1,0:T(8,128)(2,1)} collective-permute-done((bf16[224,2560]{1,0:T(8,128)(2,1)}, bf16[224,2560]{1,0:T(8,128)(2,1)}, u32[]{:S(2)}, u32[]{:S(2)}) %collective-permute-start.33) | collective-permute-done | bytes 1146912 | tf_op jit(solution)/shard_map/ppermute | solution.py:17
  428.1 15.0 %collective-permute-done.12 = bf16[224,2560]{1,0:T(8,128)(2,1)} collective-permute-done((bf16[224,2560]{1,0:T(8,128)(2,1)}, bf16[224,2560]{1,0:T(8,128)(2,1)}, u32[]{:S(2)}, u32[]{:S(2)}) %collective-permute-start.12) | collective-permute-done | bytes 1146912 | tf_op jit(solution)/shard_map/ppermute | solution.py:17
  443.1 5.1 collective-permute-start.13
  448.2 19.5 %collective-permute-done.34 = bf16[224,2560]{1,0:T(8,128)(2,1)S(1)} collective-permute-done((bf16[224,2560]{1,0:T(8,128)(2,1)}, bf16[224,2560]{1,0:T(8,128)(2,1)S(1)}, u32[]{:S(2)}, u32[]{:S(2)}) %collective-permute-start.34) | collective-permute-done | bytes 1146912 | tf_op jit(solution)/shard_map/ppermute | solution.py:17
  486.5 260.1 %while.37 = (s32[]{:T(128)}, f32[224,1024]{1,0:T(8,128)}, f32[1792,1024]{1,0:T(8,128)}, bf16[1792,1024]{1,0:T(8,128)(2,1)}, bf16[224,1024]{1,0:T(8,128)(2,1)}, /...) while((s32[]{:T(128)}, f32[224,1024]{1,0:T(8,128)}, ...), condition=%wide.region_11.12_spmd.clone, body=%wide.region_6.11_spmd.clone.sunk | while | flops 1694361088 | bytes 118743776 | solution.py:118
  496.5 10.6 subtract_exponential_fusion.7
  507.1 10.4 fusion.152
  518.5 18.7 %select_convert_fusion.5 = bf16[8,224,1792]{2,1,0:T(8,128)(2,1)} fusion(f32[8,224,1792]{2,1,0:T(8,128)} %subtract_exponential_fusion.7, f32[8,224,1792]{2,1,0:T(8,128)} %fusion.152, pred[224,1792]{1,0:T(8,128)(4,1)} %copy-done.8, bf16[224,8,32]{0,2,1:T(8,128)(2,1)S(1)} %bitcast.143, bf16[1792,8,32]{0,2,1:T(8,128)(2,1)S(1)} %bitcast.137), kind=kOutput, calls=%fused_computation.38.clone.1 | convolution fusion | flops 234429440 | bytes 33546240 | tf_op jit(solution)/shard_map/while/body/eval_jaxpr/div | solution.py:24
  561.5 10.6 subtract_exponential_fusion.7
  572.1 10.4 fusion.152
  583.5 18.7 %select_convert_fusion.5 = bf16[8,224,1792]{2,1,0:T(8,128)(2,1)} fusion(f32[8,224,1792]{2,1,0:T(8,128)} %subtract_exponential_fusion.7, f32[8,224,1792]{2,1,0:T(8,128)} %fusion.152, pred[224,1792]{1,0:T(8,128)(4,1)} %copy-done.8, bf16[224,8,32]{0,2,1:T(8,128)(2,1)S(1)} %bitcast.143, bf16[1792,8,32]{0,2,1:T(8,128)(2,1)S(1)} %bitcast.137), kind=kOutput, calls=%fused_computation.38.clone.1 | convolution fusion | flops 234429440 | bytes 33546240 | tf_op jit(solution)/shard_map/while/body/eval_jaxpr/div | solution.py:24
  602.2 4.8 fusion.153
  626.5 10.6 subtract_exponential_fusion.7
  637.1 10.4 fusion.152
  648.5 18.7 %select_convert_fusion.5 = bf16[8,224,1792]{2,1,0:T(8,128)(2,1)} fusion(f32[8,224,1792]{2,1,0:T(8,128)} %subtract_exponential_fusion.7, f32[8,224,1792]{2,1,0:T(8,128)} %fusion.152, pred[224,1792]{1,0:T(8,128)(4,1)} %copy-done.8, bf16[224,8,32]{0,2,1:T(8,128)(2,1)S(1)} %bitcast.143, bf16[1792,8,32]{0,2,1:T(8,128)(2,1)S(1)} %bitcast.137), kind=kOutput, calls=%fused_computation.38.clone.1 | convolution fusion | flops 234429440 | bytes 33546240 | tf_op jit(solution)/shard_map/while/body/eval_jaxpr/div | solution.py:24
  667.1 4.8 fusion.153
  691.5 10.6 subtract_exponential_fusion.7
  702.1 10.4 fusion.152
  713.5 18.7 %select_convert_fusion.5 = bf16[8,224,1792]{2,1,0:T(8,128)(2,1)} fusion(f32[8,224,1792]{2,1,0:T(8,128)} %subtract_exponential_fusion.7, f32[8,224,1792]{2,1,0:T(8,128)} %fusion.152, pred[224,1792]{1,0:T(8,128)(4,1)} %copy-done.8, bf16[224,8,32]{0,2,1:T(8,128)(2,1)S(1)} %bitcast.143, bf16[1792,8,32]{0,2,1:T(8,128)(2,1)S(1)} %bitcast.137), kind=kOutput, calls=%fused_computation.38.clone.1 | convolution fusion | flops 234429440 | bytes 33546240 | tf_op jit(solution)/shard_map/while/body/eval_jaxpr/div | solution.py:24
  770.3 260.2 %while.36 = (s32[]{:T(128)}, f32[224,1024]{1,0:T(8,128)}, f32[1792,1024]{1,0:T(8,128)}, bf16[1792,1024]{1,0:T(8,128)(2,1)}, bf16[224,1024]{1,0:T(8,128)(2,1)}, /...) while((s32[]{:T(128)}, f32[224,1024]{1,0:T(8,128)}, ...), condition=%wide.region_5.6_spmd.clone, body=%wide.region_0.5_spmd.clone.sunk | while | flops 1694361088 | bytes 118743776 | solution.py:118
  780.5 10.6 subtract_exponential_fusion.6
  791.2 10.4 fusion.139
  802.5 18.7 %select_convert_fusion.4 = bf16[8,224,1792]{2,1,0:T(8,128)(2,1)} fusion(f32[8,224,1792]{2,1,0:T(8,128)} %subtract_exponential_fusion.6, f32[8,224,1792]{2,1,0:T(8,128)} %fusion.139, pred[224,1792]{1,0:T(8,128)(4,1)} %copy-done.9, bf16[224,8,32]{0,2,1:T(8,128)(2,1)S(1)} %bitcast.145, bf16[1792,8,32]{0,2,1:T(8,128)(2,1)S(1)} %bitcast.139), kind=kOutput, calls=%fused_computation.6.clone.1 | convolution fusion | flops 234429440 | bytes 33546240 | tf_op jit(solution)/shard_map/while/body/eval_jaxpr/div | solution.py:24
  821.2 4.8 fusion.140
  845.5 10.6 subtract_exponential_fusion.6
  856.1 10.4 fusion.139
  867.5 18.7 %select_convert_fusion.4 = bf16[8,224,1792]{2,1,0:T(8,128)(2,1)} fusion(f32[8,224,1792]{2,1,0:T(8,128)} %subtract_exponential_fusion.6, f32[8,224,1792]{2,1,0:T(8,128)} %fusion.139, pred[224,1792]{1,0:T(8,128)(4,1)} %copy-done.9, bf16[224,8,32]{0,2,1:T(8,128)(2,1)S(1)} %bitcast.145, bf16[1792,8,32]{0,2,1:T(8,128)(2,1)S(1)} %bitcast.139), kind=kOutput, calls=%fused_computation.6.clone.1 | convolution fusion | flops 234429440 | bytes 33546240 | tf_op jit(solution)/shard_map/while/body/eval_jaxpr/div | solution.py:24
  886.2 4.8 fusion.140
  910.4 10.6 subtract_exponential_fusion.6
  921.0 10.4 fusion.139
  932.4 18.7 %select_convert_fusion.4 = bf16[8,224,1792]{2,1,0:T(8,128)(2,1)} fusion(f32[8,224,1792]{2,1,0:T(8,128)} %subtract_exponential_fusion.6, f32[8,224,1792]{2,1,0:T(8,128)} %fusion.139, pred[224,1792]{1,0:T(8,128)(4,1)} %copy-done.9, bf16[224,8,32]{0,2,1:T(8,128)(2,1)S(1)} %bitcast.145, bf16[1792,8,32]{0,2,1:T(8,128)(2,1)S(1)} %bitcast.139), kind=kOutput, calls=%fused_computation.6.clone.1 | convolution fusion | flops 234429440 | bytes 33546240 | tf_op jit(solution)/shard_map/while/body/eval_jaxpr/div | solution.py:24
  975.3 10.6 subtract_exponential_fusion.6
  985.9 10.4 fusion.139
  997.3 18.7 %select_convert_fusion.4 = bf16[8,224,1792]{2,1,0:T(8,128)(2,1)} fusion(f32[8,224,1792]{2,1,0:T(8,128)} %subtract_exponential_fusion.6, f32[8,224,1792]{2,1,0:T(8,128)} %fusion.139, pred[224,1792]{1,0:T(8,128)(4,1)} %copy-done.9, bf16[224,8,32]{0,2,1:T(8,128)(2,1)S(1)} %bitcast.145, bf16[1792,8,32]{0,2,1:T(8,128)(2,1)S(1)} %bitcast.139), kind=kOutput, calls=%fused_computation.6.clone.1 | convolution fusion | flops 234429440 | bytes 33546240 | tf_op jit(solution)/shard_map/while/body/eval_jaxpr/div | solution.py:24
  1037.2 17.8 %collective-permute-done.14 = f32[224,1024]{1,0:T(8,128)S(1)} collective-permute-done((f32[224,1024]{1,0:T(8,128)S(1)}, f32[224,1024]{1,0:T(8,128)S(1)}, u32[]{:S(2)}, u32[]{:S(2)}) %collective-permute-start.14) | collective-permute-done | bytes 917536 | tf_op jit(solution)/shard_map/ppermute | solution.py:17
  1057.5 17.1 %collective-permute-done.36 = f32[224,1024]{1,0:T(8,128)S(1)} collective-permute-done((f32[224,1024]{1,0:T(8,128)S(1)}, f32[224,1024]{1,0:T(8,128)S(1)}, u32[]{:S(2)}, u32[]{:S(2)}) %collective-permute-start.36) | collective-permute-done | bytes 917536 | tf_op jit(solution)/shard_map/ppermute | solution.py:17
  1076.0 18.2 %collective-permute-done.15 = f32[224,1024]{1,0:T(8,128)S(1)} collective-permute-done((f32[224,1024]{1,0:T(8,128)S(1)}, f32[224,1024]{1,0:T(8,128)S(1)}, u32[]{:S(2)}, u32[]{:S(2)}) %collective-permute-start.15) | collective-permute-done | bytes 917536 | tf_op jit(solution)/shard_map/ppermute | solution.py:17
  1096.9 17.1 %collective-permute-done.37 = f32[224,1024]{1,0:T(8,128)S(1)} collective-permute-done((f32[224,1024]{1,0:T(8,128)S(1)}, f32[224,1024]{1,0:T(8,128)S(1)}, u32[]{:S(2)}, u32[]{:S(2)}) %collective-permute-start.37) | collective-permute-done | bytes 917536 | tf_op jit(solution)/shard_map/ppermute | solution.py:17
  1115.4 18.2 %collective-permute-done.16 = f32[224,1024]{1,0:T(8,128)S(1)} collective-permute-done((f32[224,1024]{1,0:T(8,128)S(1)}, f32[224,1024]{1,0:T(8,128)S(1)}, u32[]{:S(2)}, u32[]{:S(2)}) %collective-permute-start.16) | collective-permute-done | bytes 917536 | tf_op jit(solution)/shard_map/ppermute | solution.py:17
  1135.0 18.2 %collective-permute-done.38 = f32[224,1024]{1,0:T(8,128)S(1)} collective-permute-done((f32[224,1024]{1,0:T(8,128)S(1)}, f32[224,1024]{1,0:T(8,128)S(1)}, u32[]{:S(2)}, u32[]{:S(2)}) %collective-permute-start.38) | collective-permute-done | bytes 917536 | tf_op jit(solution)/shard_map/ppermute | solution.py:17
  1155.0 18.0 %collective-permute-done.17 = f32[224,1024]{1,0:T(8,128)S(1)} collective-permute-done((f32[224,1024]{1,0:T(8,128)S(1)}, f32[224,1024]{1,0:T(8,128)S(1)}, u32[]{:S(2)}, u32[]{:S(2)}) %collective-permute-start.17) | collective-permute-done | bytes 917536 | tf_op jit(solution)/shard_map/ppermute | solution.py:17
  1174.3 18.2 %collective-permute-done.39 = f32[224,1024]{1,0:T(8,128)S(1)} collective-permute-done((f32[224,1024]{1,0:T(8,128)S(1)}, f32[224,1024]{1,0:T(8,128)S(1)}, u32[]{:S(2)}, u32[]{:S(2)}) %collective-permute-start.39) | collective-permute-done | bytes 917536 | tf_op jit(solution)/shard_map/ppermute | solution.py:17
  1194.0 18.2 %collective-permute-done.18 = f32[224,1024]{1,0:T(8,128)S(1)} collective-permute-done((f32[224,1024]{1,0:T(8,128)S(1)}, f32[224,1024]{1,0:T(8,128)S(1)}, u32[]{:S(2)}, u32[]{:S(2)}) %collective-permute-start.18) | collective-permute-done | bytes 917536 | tf_op jit(solution)/shard_map/ppermute | solution.py:17
  1213.7 18.2 %collective-permute-done.40 = f32[224,1024]{1,0:T(8,128)S(1)} collective-permute-done((f32[224,1024]{1,0:T(8,128)S(1)}, f32[224,1024]{1,0:T(8,128)S(1)}, u32[]{:S(2)}, u32[]{:S(2)}) %collective-permute-start.40) | collective-permute-done | bytes 917536 | tf_op jit(solution)/shard_map/ppermute | solution.py:17
  1233.6 18.0 %collective-permute-done.19 = f32[224,1024]{1,0:T(8,128)S(1)} collective-permute-done((f32[224,1024]{1,0:T(8,128)S(1)}, f32[224,1024]{1,0:T(8,128)S(1)}, u32[]{:S(2)}, u32[]{:S(2)}) %collective-permute-start.19) | collective-permute-done | bytes 917536 | tf_op jit(solution)/shard_map/ppermute | solution.py:17
  1253.0 18.2 %collective-permute-done.41 = f32[224,1024]{1,0:T(8,128)S(1)} collective-permute-done((f32[224,1024]{1,0:T(8,128)S(1)}, f32[224,1024]{1,0:T(8,128)S(1)}, u32[]{:S(2)}, u32[]{:S(2)}) %collective-permute-start.41) | collective-permute-done | bytes 917536 | tf_op jit(solution)/shard_map/ppermute | solution.py:17
  1272.7 18.2 %collective-permute-done.20 = f32[224,1024]{1,0:T(8,128)S(1)} collective-permute-done((f32[224,1024]{1,0:T(8,128)S(1)}, f32[224,1024]{1,0:T(8,128)S(1)}, u32[]{:S(2)}, u32[]{:S(2)}) %collective-permute-start.20) | collective-permute-done | bytes 917536 | tf_op jit(solution)/shard_map/ppermute | solution.py:17
  1293.6 21.9 %reduce-scatter.2.cloned.1.call-done = f32[224,1024]{1,0:T(8,128)} async-done(((f32[224,2048]{1,0:T(8,128)}), f32[224,1024]{1,0:T(8,128)}) %reduce-scatter.2.cloned.1.call-update) | async-done | bytes 917520 | tf_op jit(solution)/shard_map/reduce_scatter | solution.py:144
  (398 shorter events, 384.7 us)
Async XLA Ops:
  6.5 81.8 %copy-start = (bf16[224,2048]{1,0:T(8,128)(2,1)S(1)}, bf16[224,2048]{1,0:T(8,128)(2,1)}, u32[]{:S(2)}) copy-start(bf16[224,2048]{1,0:T(8,128)(2,1)} %param.13) | copy-start | bytes 2752516
  6.5 318.5 %copy-start.40 = (s32[1,7]{1,0:T(1,128)S(1)}, s32[1,7]{1,0:T(1,128)}, u32[]{:S(2)}) copy-start(s32[1,7]{1,0:T(1,128)} %param.17) | copy-start | bytes 88
  6.5 345.9 %copy-start.35 = (s32[14336]{0:T(1024)S(1)}, s32[14336]{0:T(1024)}, u32[]{:S(2)}) copy-start(s32[14336]{0:T(1024)} %param.16) | copy-start | bytes 172036
  6.5 1308.9 %reduce-scatter.2.cloned.1.call-start = ((), (), s32[]{:S(2)}) async-start(), calls=%async_computation.1 | async-start | bytes 2752512 | tf_op jit(solution)/shard_map/reduce_scatter | solution.py:144
  6.5 89.0 %copy-start.11 = (bf16[2048,1024]{1,0:T(8,128)(2,1)S(1)}, bf16[2048,1024]{1,0:T(8,128)(2,1)}, u32[]{:S(2)}) copy-start(bf16[2048,1024]{1,0:T(8,128)(2,1)} %param.14) | copy-start | bytes 12582916
  6.6 28.5 %collective-permute-start.28 = (bf16[224,2560]{1,0:T(8,128)(2,1)}, bf16[224,2560]{1,0:T(8,128)(2,1)S(1)}, u32[]{:S(2)}, u32[]{:S(2)}) collective-permute-start(bf16[224,2560]{1,0:T(8,128)(2,1)} %param.12), channel_id=1, source_target_pairs={{0,2},{2,4},{4,6},{6,8},{8,10},{10,12},{12,14},{14,16},{16,18},{18... | collective-permute-start | bytes 3440648 | tf_op jit(solution)/shard_map/ppermute | solution.py:17
  10.9 48.7 %collective-permute-start.7 = (bf16[224,2560]{1,0:T(8,128)(2,1)}, bf16[224,2560]{1,0:T(8,128)(2,1)S(1)}, u32[]{:S(2)}, u32[]{:S(2)}) collective-permute-start(bf16[224,2560]{1,0:T(8,128)(2,1)} %param.11), channel_id=1, source_target_pairs={{0,2},{2,4},{4,6},{6,8},{8,10},{10,12},{12,14},{14,16},{16,18},{18... | collective-permute-start | bytes 3440648 | tf_op jit(solution)/shard_map/ppermute | solution.py:17
  35.1 49.0 %collective-permute-start.29 = (bf16[224,2560]{1,0:T(8,128)(2,1)S(1)}, bf16[224,2560]{1,0:T(8,128)(2,1)S(1)}, u32[]{:S(2)}, u32[]{:S(2)}) collective-permute-start(bf16[224,2560]{1,0:T(8,128)(2,1)S(1)} %collective-permute-done.28), channel_id=1, source_target_pairs={{0,2},{2,4},{4,6},{6,8},{8,10},{10,12},{12,14},{14,16},{16,18},{18... | collective-permute-start | bytes 3440648 | tf_op jit(solution)/shard_map/ppermute | solution.py:17
  59.7 37.1 %copy-start.16 = (bf16[224,2560]{1,0:T(8,128)(2,1)}, bf16[224,2560]{1,0:T(8,128)(2,1)S(1)}, u32[]{:S(2)}) copy-start(bf16[224,2560]{1,0:T(8,128)(2,1)S(1)} %collective-permute-done.7) | copy-start | bytes 3440644
  59.7 87.6 %collective-permute-start.8 = (bf16[224,2560]{1,0:T(8,128)(2,1)S(1)}, bf16[224,2560]{1,0:T(8,128)(2,1)S(1)}, u32[]{:S(2)}, u32[]{:S(2)}) collective-permute-start(bf16[224,2560]{1,0:T(8,128)(2,1)S(1)} %collective-permute-done.7), channel_id=1, source_target_pairs={{0,2},{2,4},{4,6},{6,8},{8,10},{10,12},{12,14},{14,16},{16,18},{18... | collective-permute-start | bytes 3440648 | tf_op jit(solution)/shard_map/ppermute | solution.py:17
  84.1 66.4 %collective-permute-start.30 = (bf16[224,2560]{1,0:T(8,128)(2,1)S(1)}, bf16[224,2560]{1,0:T(8,128)(2,1)S(1)}, u32[]{:S(2)}, u32[]{:S(2)}) collective-permute-start(bf16[224,2560]{1,0:T(8,128)(2,1)S(1)} %collective-permute-done.29), channel_id=1, source_target_pairs={{0,2},{2,4},{4,6},{6,8},{8,10},{10,12},{12,14},{14,16},{16,18},{18... | collective-permute-start | bytes 3440648 | tf_op jit(solution)/shard_map/ppermute | solution.py:17
  92.4 50.8 %collective-permute-start.21 = (bf16[224,1024]{1,0:T(8,128)(2,1)}, bf16[224,1024]{1,0:T(8,128)(2,1)S(1)}, u32[]{:S(2)}, u32[]{:S(2)}) collective-permute-start(bf16[224,1024]{1,0:T(8,128)(2,1)} %convolution_convert_fusion), channel_id=1, source_target_pairs={{0,2},{2,4},{4,6},{6,8},{8,10},{10,12},{12,14},{14,16},{16,18},{18... | collective-permute-start | bytes 1376264 | tf_op jit(solution)/shard_map/ppermute | solution.py:17
  96.7 330.5 %copy-start.15 = (bf16[224,1024]{1,0:T(8,128)(2,1)}, bf16[224,1024]{1,0:T(8,128)(2,1)S(1)}, u32[]{:S(2)}) copy-start(bf16[224,1024]{1,0:T(8,128)(2,1)S(1)} %convolution_convert_fusion.1) | copy-start | bytes 1376260
  96.8 57.7 %collective-permute-start = (bf16[224,1024]{1,0:T(8,128)(2,1)S(1)}, bf16[224,1024]{1,0:T(8,128)(2,1)S(1)}, u32[]{:S(2)}, u32[]{:S(2)}) collective-permute-start(bf16[224,1024]{1,0:T(8,128)(2,1)S(1)} %convolution_convert_fusion.1), channel_id=1, source_target_pairs={{0,2},{2,4},{4,6},{6,8},{8,10},{10,12},{12,14},{14,16},{16,18},{18... | collective-permute-start | bytes 1376264 | tf_op jit(solution)/shard_map/ppermute | solution.py:17
  143.2 19.6 %collective-permute-start.22 = (bf16[224,1024]{1,0:T(8,128)(2,1)S(1)}, bf16[224,1024]{1,0:T(8,128)(2,1)S(1)}, u32[]{:S(2)}, u32[]{:S(2)}) collective-permute-start(bf16[224,1024]{1,0:T(8,128)(2,1)S(1)} %collective-permute-done.21), channel_id=1, source_target_pairs={{0,2},{2,4},{4,6},{6,8},{8,10},{10,12},{12,14},{14,16},{16,18},{18... | collective-permute-start | bytes 1376264 | tf_op jit(solution)/shard_map/ppermute | solution.py:17
  147.3 88.5 %collective-permute-start.9 = (bf16[224,2560]{1,0:T(8,128)(2,1)S(1)}, bf16[224,2560]{1,0:T(8,128)(2,1)S(1)}, u32[]{:S(2)}, u32[]{:S(2)}) collective-permute-start(bf16[224,2560]{1,0:T(8,128)(2,1)S(1)} %collective-permute-done.8), channel_id=1, source_target_pairs={{0,2},{2,4},{4,6},{6,8},{8,10},{10,12},{12,14},{14,16},{16,18},{18... | collective-permute-start | bytes 3440648 | tf_op jit(solution)/shard_map/ppermute | solution.py:17
  150.5 85.2 %copy-start.26 = (bf16[224,2560]{1,0:T(8,128)(2,1)}, bf16[224,2560]{1,0:T(8,128)(2,1)S(1)}, u32[]{:S(2)}) copy-start(bf16[224,2560]{1,0:T(8,128)(2,1)S(1)} %collective-permute-done.30) | copy-start | bytes 3440644
  150.6 89.4 %collective-permute-start.31 = (bf16[224,2560]{1,0:T(8,128)(2,1)S(1)}, bf16[224,2560]{1,0:T(8,128)(2,1)}, u32[]{:S(2)}, u32[]{:S(2)}) collective-permute-start(bf16[224,2560]{1,0:T(8,128)(2,1)S(1)} %collective-permute-done.30), channel_id=1, source_target_pairs={{0,2},{2,4},{4,6},{6,8},{8,10},{10,12},{12,14},{14,16},{16,18},{18... | collective-permute-start | bytes 3440648 | tf_op jit(solution)/shard_map/ppermute | solution.py:17
  154.5 67.3 %collective-permute-start.1 = (bf16[224,1024]{1,0:T(8,128)(2,1)S(1)}, bf16[224,1024]{1,0:T(8,128)(2,1)S(1)}, u32[]{:S(2)}, u32[]{:S(2)}) collective-permute-start(bf16[224,1024]{1,0:T(8,128)(2,1)S(1)} %collective-permute-done), channel_id=1, source_target_pairs={{0,2},{2,4},{4,6},{6,8},{8,10},{10,12},{12,14},{14,16},{16,18},{18... | collective-permute-start | bytes 1376264 | tf_op jit(solution)/shard_map/ppermute | solution.py:17
  162.8 147.5 %copy-start.28 = (bf16[224,1024]{1,0:T(8,128)(2,1)}, bf16[224,1024]{1,0:T(8,128)(2,1)S(1)}, u32[]{:S(2)}) copy-start(bf16[224,1024]{1,0:T(8,128)(2,1)S(1)} %collective-permute-done.22) | copy-start | bytes 1376260
  162.8 68.8 %collective-permute-start.23 = (bf16[224,1024]{1,0:T(8,128)(2,1)S(1)}, bf16[224,1024]{1,0:T(8,128)(2,1)S(1)}, u32[]{:S(2)}, u32[]{:S(2)}) collective-permute-start(bf16[224,1024]{1,0:T(8,128)(2,1)S(1)} %collective-permute-done.22), channel_id=1, source_target_pairs={{0,2},{2,4},{4,6},{6,8},{8,10},{10,12},{12,14},{14,16},{16,18},{18... | collective-permute-start | bytes 1376264 | tf_op jit(solution)/shard_map/ppermute | solution.py:17
  221.8 21.1 %collective-permute-start.2 = (bf16[224,1024]{1,0:T(8,128)(2,1)S(1)}, bf16[224,1024]{1,0:T(8,128)(2,1)S(1)}, u32[]{:S(2)}, u32[]{:S(2)}) collective-permute-start(bf16[224,1024]{1,0:T(8,128)(2,1)S(1)} %collective-permute-done.1), channel_id=1, source_target_pairs={{0,2},{2,4},{4,6},{6,8},{8,10},{10,12},{12,14},{14,16},{16,18},{18... | collective-permute-start | bytes 1376264 | tf_op jit(solution)/shard_map/ppermute | solution.py:17
  231.6 83.6 %copy-start.29 = (bf16[224,1024]{1,0:T(8,128)(2,1)}, bf16[224,1024]{1,0:T(8,128)(2,1)S(1)}, u32[]{:S(2)}) copy-start(bf16[224,1024]{1,0:T(8,128)(2,1)S(1)} %collective-permute-done.23) | copy-start | bytes 1376260
  231.6 19.7 %collective-permute-start.24 = (bf16[224,1024]{1,0:T(8,128)(2,1)S(1)}, bf16[224,1024]{1,0:T(8,128)(2,1)S(1)}, u32[]{:S(2)}, u32[]{:S(2)}) collective-permute-start(bf16[224,1024]{1,0:T(8,128)(2,1)S(1)} %collective-permute-done.23), channel_id=1, source_target_pairs={{0,2},{2,4},{4,6},{6,8},{8,10},{10,12},{12,14},{14,16},{16,18},{18... | collective-permute-start | bytes 1376264 | tf_op jit(solution)/shard_map/ppermute | solution.py:17
  235.8 190.7 %copy-start.20 = (bf16[224,2560]{1,0:T(8,128)(2,1)}, bf16[224,2560]{1,0:T(8,128)(2,1)S(1)}, u32[]{:S(2)}) copy-start(bf16[224,2560]{1,0:T(8,128)(2,1)S(1)} %collective-permute-done.9) | copy-start | bytes 3440644
  235.8 109.0 %collective-permute-start.10 = (bf16[224,2560]{1,0:T(8,128)(2,1)S(1)}, bf16[224,2560]{1,0:T(8,128)(2,1)}, u32[]{:S(2)}, u32[]{:S(2)}) collective-permute-start(bf16[224,2560]{1,0:T(8,128)(2,1)S(1)} %collective-permute-done.9), channel_id=1, source_target_pairs={{0,2},{2,4},{4,6},{6,8},{8,10},{10,12},{12,14},{14,16},{16,18},{18... | collective-permute-start | bytes 3440648 | tf_op jit(solution)/shard_map/ppermute | solution.py:17
  240.0 108.2 %collective-permute-start.32 = (bf16[224,2560]{1,0:T(8,128)(2,1)}, bf16[224,2560]{1,0:T(8,128)(2,1)}, u32[]{:S(2)}, u32[]{:S(2)}) collective-permute-start(bf16[224,2560]{1,0:T(8,128)(2,1)} %collective-permute-done.31), channel_id=1, source_target_pairs={{0,2},{2,4},{4,6},{6,8},{8,10},{10,12},{12,14},{14,16},{16,18},{18... | collective-permute-start | bytes 3440648 | tf_op jit(solution)/shard_map/ppermute | solution.py:17
  242.9 67.3 %collective-permute-start.3 = (bf16[224,1024]{1,0:T(8,128)(2,1)S(1)}, bf16[224,1024]{1,0:T(8,128)(2,1)}, u32[]{:S(2)}, u32[]{:S(2)}) collective-permute-start(bf16[224,1024]{1,0:T(8,128)(2,1)S(1)} %collective-permute-done.2), channel_id=1, source_target_pairs={{0,2},{2,4},{4,6},{6,8},{8,10},{10,12},{12,14},{14,16},{16,18},{18... | collective-permute-start | bytes 1376264 | tf_op jit(solution)/shard_map/ppermute | solution.py:17
  251.3 68.8 %copy-start.30 = (bf16[224,1024]{1,0:T(8,128)(2,1)}, bf16[224,1024]{1,0:T(8,128)(2,1)S(1)}, u32[]{:S(2)}) copy-start(bf16[224,1024]{1,0:T(8,128)(2,1)S(1)} %collective-permute-done.24) | copy-start | bytes 1376260
  251.3 68.8 %collective-permute-start.25 = (bf16[224,1024]{1,0:T(8,128)(2,1)S(1)}, bf16[224,1024]{1,0:T(8,128)(2,1)}, u32[]{:S(2)}, u32[]{:S(2)}) collective-permute-start(bf16[224,1024]{1,0:T(8,128)(2,1)S(1)} %collective-permute-done.24), channel_id=1, source_target_pairs={{0,2},{2,4},{4,6},{6,8},{8,10},{10,12},{12,14},{14,16},{16,18},{18... | collective-permute-start | bytes 1376264 | tf_op jit(solution)/shard_map/ppermute | solution.py:17
  310.3 19.8 %collective-permute-start.4 = (bf16[224,1024]{1,0:T(8,128)(2,1)}, bf16[224,1024]{1,0:T(8,128)(2,1)}, u32[]{:S(2)}, u32[]{:S(2)}) collective-permute-start(bf16[224,1024]{1,0:T(8,128)(2,1)} %collective-permute-done.3), channel_id=1, source_target_pairs={{0,2},{2,4},{4,6},{6,8},{8,10},{10,12},{12,14},{14,16},{16,18},{18... | collective-permute-start | bytes 1376264 | tf_op jit(solution)/shard_map/ppermute | solution.py:17
  320.1 19.8 %collective-permute-start.26 = (bf16[224,1024]{1,0:T(8,128)(2,1)}, bf16[224,1024]{1,0:T(8,128)(2,1)}, u32[]{:S(2)}, u32[]{:S(2)}) collective-permute-start(bf16[224,1024]{1,0:T(8,128)(2,1)} %collective-permute-done.25), channel_id=1, source_target_pairs={{0,2},{2,4},{4,6},{6,8},{8,10},{10,12},{12,14},{14,16},{16,18},{18... | collective-permute-start | bytes 1376264 | tf_op jit(solution)/shard_map/ppermute | solution.py:17
  330.0 23.2 %collective-permute-start.5 = (bf16[224,1024]{1,0:T(8,128)(2,1)}, bf16[224,1024]{1,0:T(8,128)(2,1)}, u32[]{:S(2)}, u32[]{:S(2)}) collective-permute-start(bf16[224,1024]{1,0:T(8,128)(2,1)} %collective-permute-done.4), channel_id=1, source_target_pairs={{0,2},{2,4},{4,6},{6,8},{8,10},{10,12},{12,14},{14,16},{16,18},{18... | collective-permute-start | bytes 1376264 | tf_op jit(solution)/shard_map/ppermute | solution.py:17
  339.9 19.7 %collective-permute-start.27 = (bf16[224,1024]{1,0:T(8,128)(2,1)}, bf16[224,1024]{1,0:T(8,128)(2,1)}, u32[]{:S(2)}, u32[]{:S(2)}) collective-permute-start(bf16[224,1024]{1,0:T(8,128)(2,1)} %collective-permute-done.26), channel_id=1, source_target_pairs={{0,2},{2,4},{4,6},{6,8},{8,10},{10,12},{12,14},{14,16},{16,18},{18... | collective-permute-start | bytes 1376264 | tf_op jit(solution)/shard_map/ppermute | solution.py:17
  344.7 39.4 %collective-permute-start.11 = (bf16[224,2560]{1,0:T(8,128)(2,1)}, bf16[224,2560]{1,0:T(8,128)(2,1)}, u32[]{:S(2)}, u32[]{:S(2)}) collective-permute-start(bf16[224,2560]{1,0:T(8,128)(2,1)} %collective-permute-done.10), channel_id=1, source_target_pairs={{0,2},{2,4},{4,6},{6,8},{8,10},{10,12},{12,14},{14,16},{16,18},{18... | collective-permute-start | bytes 3440648 | tf_op jit(solution)/shard_map/ppermute | solution.py:17
  348.2 60.5 %collective-permute-start.33 = (bf16[224,2560]{1,0:T(8,128)(2,1)}, bf16[224,2560]{1,0:T(8,128)(2,1)}, u32[]{:S(2)}, u32[]{:S(2)}) collective-permute-start(bf16[224,2560]{1,0:T(8,128)(2,1)} %collective-permute-done.32), channel_id=1, source_target_pairs={{0,2},{2,4},{4,6},{6,8},{8,10},{10,12},{12,14},{14,16},{16,18},{18... | collective-permute-start | bytes 3440648 | tf_op jit(solution)/shard_map/ppermute | solution.py:17
  353.2 65.3 %collective-permute-start.6 = (bf16[224,1024]{1,0:T(8,128)(2,1)}, bf16[224,1024]{1,0:T(8,128)(2,1)S(1)}, u32[]{:S(2)}, u32[]{:S(2)}) collective-permute-start(bf16[224,1024]{1,0:T(8,128)(2,1)} %collective-permute-done.5), channel_id=1, source_target_pairs={{0,2},{2,4},{4,6},{6,8},{8,10},{10,12},{12,14},{14,16},{16,18},{18... | collective-permute-start | bytes 1376264 | tf_op jit(solution)/shard_map/ppermute | solution.py:17
  384.1 59.0 %collective-permute-start.12 = (bf16[224,2560]{1,0:T(8,128)(2,1)}, bf16[224,2560]{1,0:T(8,128)(2,1)}, u32[]{:S(2)}, u32[]{:S(2)}) collective-permute-start(bf16[224,2560]{1,0:T(8,128)(2,1)} %collective-permute-done.11), channel_id=1, source_target_pairs={{0,2},{2,4},{4,6},{6,8},{8,10},{10,12},{12,14},{14,16},{16,18},{18... | collective-permute-start | bytes 3440648 | tf_op jit(solution)/shard_map/ppermute | solution.py:17
  408.7 59.0 %collective-permute-start.34 = (bf16[224,2560]{1,0:T(8,128)(2,1)}, bf16[224,2560]{1,0:T(8,128)(2,1)S(1)}, u32[]{:S(2)}, u32[]{:S(2)}) collective-permute-start(bf16[224,2560]{1,0:T(8,128)(2,1)} %collective-permute-done.33), channel_id=1, source_target_pairs={{0,2},{2,4},{4,6},{6,8},{8,10},{10,12},{12,14},{14,16},{16,18},{18... | collective-permute-start | bytes 3440648 | tf_op jit(solution)/shard_map/ppermute | solution.py:17
  424.8 51.0 %copy-start.27 = (bf16[224,2560]{1,0:T(8,128)(2,1)S(1)}, bf16[224,2560]{1,0:T(8,128)(2,1)}, u32[]{:S(2)}) copy-start(bf16[224,2560]{1,0:T(8,128)(2,1)} %copy-done.26) | copy-start | bytes 3440644
  427.2 49.7 %copy-start.25 = (bf16[224,2560]{1,0:T(8,128)(2,1)S(1)}, bf16[224,2560]{1,0:T(8,128)(2,1)}, u32[]{:S(2)}) copy-start(bf16[224,2560]{1,0:T(8,128)(2,1)} %copy-done.24) | copy-start | bytes 3440644
  428.1 49.9 %copy-start.23 = (bf16[224,2560]{1,0:T(8,128)(2,1)S(1)}, bf16[224,2560]{1,0:T(8,128)(2,1)}, u32[]{:S(2)}) copy-start(bf16[224,2560]{1,0:T(8,128)(2,1)} %copy-done.22) | copy-start | bytes 3440644
  443.1 307.2 %collective-permute-start.13 = (bf16[224,2560]{1,0:T(8,128)(2,1)}, bf16[224,2560]{1,0:T(8,128)(2,1)}, u32[]{:S(2)}, u32[]{:S(2)}) collective-permute-start(bf16[224,2560]{1,0:T(8,128)(2,1)} %collective-permute-done.12), channel_id=1, source_target_pairs={{0,2},{2,4},{4,6},{6,8},{8,10},{10,12},{12,14},{14,16},{16,18},{18... | collective-permute-start | bytes 3440648 | tf_op jit(solution)/shard_map/ppermute | solution.py:17
  748.9 284.6 %collective-permute-start.35 = (f32[224,1024]{1,0:T(8,128)}, f32[224,1024]{1,0:T(8,128)}, u32[]{:S(2)}, u32[]{:S(2)}) collective-permute-start(f32[224,1024]{1,0:T(8,128)} %slice.56), channel_id=1, source_target_pairs={{2,0},{4,2},{6,4},{8,6},{10,8},{12,10},{14,12},{16,14},{18,16},{20... | collective-permute-start | bytes 2752520 | tf_op jit(solution)/shard_map/ppermute | solution.py:17
  1030.5 44.1 %copy-start.6 = (f32[1792,1024]{1,0:T(8,128)S(1)}, f32[1792,1024]{1,0:T(8,128)}, u32[]{:S(2)}) copy-start(f32[1792,1024]{1,0:T(8,128)} %get-tuple-element.408) | copy-start | bytes 22020100
  1032.0 101.6 %copy-start.7 = (f32[1792,1024]{1,0:T(8,128)S(1)}, f32[1792,1024]{1,0:T(8,128)}, u32[]{:S(2)}) copy-start(f32[1792,1024]{1,0:T(8,128)} %get-tuple-element.406) | copy-start | bytes 22020100
  1032.0 23.0 %collective-permute-start.14 = (f32[224,1024]{1,0:T(8,128)S(1)}, f32[224,1024]{1,0:T(8,128)S(1)}, u32[]{:S(2)}, u32[]{:S(2)}) collective-permute-start(f32[224,1024]{1,0:T(8,128)S(1)} %slice.48), channel_id=1, source_target_pairs={{2,0},{4,2},{6,4},{8,6},{10,8},{12,10},{14,12},{16,14},{18,16},{20... | collective-permute-start | bytes 2752520 | tf_op jit(solution)/shard_map/ppermute | solution.py:17
  1035.9 38.8 %collective-permute-start.36 = (f32[224,1024]{1,0:T(8,128)S(1)}, f32[224,1024]{1,0:T(8,128)S(1)}, u32[]{:S(2)}, u32[]{:S(2)}) collective-permute-start(f32[224,1024]{1,0:T(8,128)S(1)} %slice_add_fusion.5), channel_id=1, source_target_pairs={{2,0},{4,2},{6,4},{8,6},{10,8},{12,10},{14,12},{16,14},{18,16},{20... | collective-permute-start | bytes 2752520 | tf_op jit(solution)/shard_map/ppermute | solution.py:17
  1056.2 38.0 %collective-permute-start.15 = (f32[224,1024]{1,0:T(8,128)S(1)}, f32[224,1024]{1,0:T(8,128)S(1)}, u32[]{:S(2)}, u32[]{:S(2)}) collective-permute-start(f32[224,1024]{1,0:T(8,128)S(1)} %slice_add_fusion.11), channel_id=1, source_target_pairs={{2,0},{4,2},{6,4},{8,6},{10,8},{12,10},{14,12},{16,14},{18,16},{20... | collective-permute-start | bytes 2752520 | tf_op jit(solution)/shard_map/ppermute | solution.py:17
  1074.7 39.2 %collective-permute-start.37 = (f32[224,1024]{1,0:T(8,128)S(1)}, f32[224,1024]{1,0:T(8,128)S(1)}, u32[]{:S(2)}, u32[]{:S(2)}) collective-permute-start(f32[224,1024]{1,0:T(8,128)S(1)} %slice_add_fusion.4), channel_id=1, source_target_pairs={{2,0},{4,2},{6,4},{8,6},{10,8},{12,10},{14,12},{16,14},{18,16},{20... | collective-permute-start | bytes 2752520 | tf_op jit(solution)/shard_map/ppermute | solution.py:17
  1095.6 38.0 %collective-permute-start.16 = (f32[224,1024]{1,0:T(8,128)S(1)}, f32[224,1024]{1,0:T(8,128)S(1)}, u32[]{:S(2)}, u32[]{:S(2)}) collective-permute-start(f32[224,1024]{1,0:T(8,128)S(1)} %slice_add_fusion.10), channel_id=1, source_target_pairs={{2,0},{4,2},{6,4},{8,6},{10,8},{12,10},{14,12},{16,14},{18,16},{20... | collective-permute-start | bytes 2752520 | tf_op jit(solution)/shard_map/ppermute | solution.py:17
  1114.1 39.2 %collective-permute-start.38 = (f32[224,1024]{1,0:T(8,128)S(1)}, f32[224,1024]{1,0:T(8,128)S(1)}, u32[]{:S(2)}, u32[]{:S(2)}) collective-permute-start(f32[224,1024]{1,0:T(8,128)S(1)} %slice_add_fusion.3), channel_id=1, source_target_pairs={{2,0},{4,2},{6,4},{8,6},{10,8},{12,10},{14,12},{16,14},{18,16},{20... | collective-permute-start | bytes 2752520 | tf_op jit(solution)/shard_map/ppermute | solution.py:17
  1133.7 39.2 %collective-permute-start.17 = (f32[224,1024]{1,0:T(8,128)S(1)}, f32[224,1024]{1,0:T(8,128)S(1)}, u32[]{:S(2)}, u32[]{:S(2)}) collective-permute-start(f32[224,1024]{1,0:T(8,128)S(1)} %slice_add_fusion.9), channel_id=1, source_target_pairs={{2,0},{4,2},{6,4},{8,6},{10,8},{12,10},{14,12},{16,14},{18,16},{20... | collective-permute-start | bytes 2752520 | tf_op jit(solution)/shard_map/ppermute | solution.py:17
  1153.4 117.9 %copy-start.10 = (bf16[2048,1024]{1,0:T(8,128)(2,1)S(1)}, bf16[2048,1024]{1,0:T(8,128)(2,1)}, u32[]{:S(2)}) copy-start(bf16[2048,1024]{1,0:T(8,128)(2,1)} %param.15) | copy-start | bytes 12582916
  1153.4 117.8 %copy-start.13 = (f32[224,1024]{1,0:T(8,128)S(1)}, f32[224,1024]{1,0:T(8,128)}, u32[]{:S(2)}) copy-start(f32[224,1024]{1,0:T(8,128)} %get-tuple-element.407) | copy-start | bytes 2752516
  1153.4 39.2 %collective-permute-start.39 = (f32[224,1024]{1,0:T(8,128)S(1)}, f32[224,1024]{1,0:T(8,128)S(1)}, u32[]{:S(2)}, u32[]{:S(2)}) collective-permute-start(f32[224,1024]{1,0:T(8,128)S(1)} %slice_add_fusion.2), channel_id=1, source_target_pairs={{2,0},{4,2},{6,4},{8,6},{10,8},{12,10},{14,12},{16,14},{18,16},{20... | collective-permute-start | bytes 2752520 | tf_op jit(solution)/shard_map/ppermute | solution.py:17
  1173.0 39.2 %collective-permute-start.18 = (f32[224,1024]{1,0:T(8,128)S(1)}, f32[224,1024]{1,0:T(8,128)S(1)}, u32[]{:S(2)}, u32[]{:S(2)}) collective-permute-start(f32[224,1024]{1,0:T(8,128)S(1)} %slice_add_fusion.8), channel_id=1, source_target_pairs={{2,0},{4,2},{6,4},{8,6},{10,8},{12,10},{14,12},{16,14},{18,16},{20... | collective-permute-start | bytes 2752520 | tf_op jit(solution)/shard_map/ppermute | solution.py:17
  1192.7 39.2 %collective-permute-start.40 = (f32[224,1024]{1,0:T(8,128)S(1)}, f32[224,1024]{1,0:T(8,128)S(1)}, u32[]{:S(2)}, u32[]{:S(2)}) collective-permute-start(f32[224,1024]{1,0:T(8,128)S(1)} %slice_add_fusion.1), channel_id=1, source_target_pairs={{2,0},{4,2},{6,4},{8,6},{10,8},{12,10},{14,12},{16,14},{18,16},{20... | collective-permute-start | bytes 2752520 | tf_op jit(solution)/shard_map/ppermute | solution.py:17
  1212.4 39.2 %collective-permute-start.19 = (f32[224,1024]{1,0:T(8,128)S(1)}, f32[224,1024]{1,0:T(8,128)S(1)}, u32[]{:S(2)}, u32[]{:S(2)}) collective-permute-start(f32[224,1024]{1,0:T(8,128)S(1)} %slice_add_fusion.7), channel_id=1, source_target_pairs={{2,0},{4,2},{6,4},{8,6},{10,8},{12,10},{14,12},{16,14},{18,16},{20... | collective-permute-start | bytes 2752520 | tf_op jit(solution)/shard_map/ppermute | solution.py:17
  1232.0 58.9 %copy-start.12 = (bf16[2048,1024]{1,0:T(8,128)(2,1)S(1)}, bf16[2048,1024]{1,0:T(8,128)(2,1)}, u32[]{:S(2)}) copy-start(bf16[2048,1024]{1,0:T(8,128)(2,1)} %param.14) | copy-start | bytes 12582916
  1232.0 58.9 %copy-start.14 = (f32[224,1024]{1,0:T(8,128)S(1)}, f32[224,1024]{1,0:T(8,128)}, u32[]{:S(2)}) copy-start(f32[224,1024]{1,0:T(8,128)} %get-tuple-element.405) | copy-start | bytes 2752516
  1232.1 39.2 %collective-permute-start.41 = (f32[224,1024]{1,0:T(8,128)S(1)}, f32[224,1024]{1,0:T(8,128)S(1)}, u32[]{:S(2)}, u32[]{:S(2)}) collective-permute-start(f32[224,1024]{1,0:T(8,128)S(1)} %slice_add_fusion), channel_id=1, source_target_pairs={{2,0},{4,2},{6,4},{8,6},{10,8},{12,10},{14,12},{16,14},{18,16},{20... | collective-permute-start | bytes 2752520 | tf_op jit(solution)/shard_map/ppermute | solution.py:17
  1251.7 39.2 %collective-permute-start.20 = (f32[224,1024]{1,0:T(8,128)S(1)}, f32[224,1024]{1,0:T(8,128)S(1)}, u32[]{:S(2)}, u32[]{:S(2)}) collective-permute-start(f32[224,1024]{1,0:T(8,128)S(1)} %slice_add_fusion.6), channel_id=1, source_target_pairs={{2,0},{4,2},{6,4},{8,6},{10,8},{12,10},{14,12},{16,14},{18,16},{20... | collective-permute-start | bytes 2752520 | tf_op jit(solution)/shard_map/ppermute | solution.py:17
  1290.9 26.6 %copy-start.1 = (bf16[224,2048]{1,0:T(8,128)(2,1)S(1)}, bf16[224,2048]{1,0:T(8,128)(2,1)}, u32[]{:S(2)}) copy-start(bf16[224,2048]{1,0:T(8,128)(2,1)} %param.13) | copy-start | bytes 2752516
  (62 other events, 452.2 us)
Sparse Core Ops, SparseCore 0:
  1293.7 21.6 reduce-scatter.1
where the time goes:
time: 1330 us; the launch traced here: 1320 us
  waiting for transfers between devices  571 us (43%)
  matrix products  397 us (30%)
  local copies, waits for them, and re-layouts  192 us (14%)
  starting transfers between devices  133 us (10%)
  other arithmetic  14.7 us (1%)
  between operations  14.1 us (1%)
    ppermute x42, waiting for transfers between devices, from_behind(): return lax.ppermute(block, axis, route)  549 us
    div x16, matrix products, relation_probs(): return weights / jnp.sum(weights, axis=-1, keepdims=True)  232 us
    ppermute x42, starting transfers between devices, from_behind(): return lax.ppermute(block, axis, route)  133 us
    sub x8, matrix products, relation_probs(): weights = jnp.exp(masked - highest)  84.9 us
    dynamic_slice x64, local copies, waits for them, and re-layouts, columns(): lax.dynamic_slice_in_dim(values, group_index * group * width, group * wid...  75 us
    unnamed x82, local copies, waits for them, and re-layouts  44.8 us
    dot_general x8, matrix products, one_group(): jnp.einsum('hqk,khd->qhd', coupling, student_b, preferred_element_type=jn...  38.3 us
    dynamic_update_slice x16, local copies, waits for them, and re-layouts, one_group(): lax.dynamic_update_slice_in_dim(key_total, key_part, group_index * group...  37.1 us
  transfers between devices with their start and end apart: 43, of which 32 were waited for; matrix products, arithmetic and copies ran while one was open for 45% of the time, Pallas kernels for 0%

commit v1 on v0

v1 whole, which is shorter than its diff:
```python
import functools
import math

import jax
import jax.numpy as jnp
from jax import lax
from jax.experimental import pallas as pl
from jax.experimental.pallas import tpu as pltpu
from jax.sharding import PartitionSpec as P

DT = 5120
DS = 2048
HEADS = 64
REACH = 8
WT = DT // HEADS
WS = DS // HEADS
SEG0 = WT + WS
ONE0 = SEG0 + 4
MASK0 = ONE0 + 3
SLAB = 128
PACK = 8
LAG = 14
UNROLL = 4
SLOTS = 8
LIST = 640
HIDDEN = 1e30
LOG2E = math.log2(math.e)
SCALE_T = LOG2E / math.sqrt(WT)
SCALE_S = LOG2E / math.sqrt(WS)
SAFE = 90.0


def pack_kernel(hidden, wq, wk, tq, tk, extra, out, pick, place):
    @pl.when(pl.program_id(0) == 0)
    def _():
        row = lax.broadcasted_iota(jnp.int32, (256, 2 * SLAB), 0)
        lane = lax.broadcasted_iota(jnp.int32, (256, 2 * SLAB), 1)
        second = jnp.where(lane >= SLAB, 1, 0)
        column = lane - second * SLAB
        for pair in range(PACK // 2):
            source = column + second * WT + pair * 2 * WT % 128
            pick[pair] = jnp.where((row == source) & (column < WT), 1.0, 0.0).astype(jnp.bfloat16)
        for half in range(2):
            source = column - WT + second * WS + half * 2 * WS
            inside = (row == source) & (column >= WT) & (column < SEG0)
            place[half] = jnp.where(inside, 1.0, 0.0)[:128].astype(jnp.bfloat16)

    for rel, (weight, teacher) in enumerate(((wq, tq), (wk, tk))):
        student = jnp.dot(hidden[...], weight[...], preferred_element_type=jnp.float32).astype(
            jnp.bfloat16
        )
        for pair in range(PACK // 2):
            low = pair * 2 * WT // 128 * 128
            slab = jnp.dot(
                teacher[:, low : low + 256], pick[pair], preferred_element_type=jnp.float32
            )
            low = pair * 2 * WS // 128 * 128
            slab += jnp.dot(
                student[:, low : low + 128], place[pair % 2], preferred_element_type=jnp.float32
            )
            for second in range(2):
                part = slab[:, second * SLAB : (second + 1) * SLAB] + extra[...]
                out[rel, 2 * pair + second] = part.astype(jnp.bfloat16)


def pack(hidden, wq, wk, tq, tk, extra):
    rows = hidden.shape[0]
    heads = wq.shape[1] // WS
    return pl.pallas_call(
        pack_kernel,
        grid=(heads // PACK,),
        out_shape=jax.ShapeDtypeStruct((2, heads, rows, SLAB), jnp.bfloat16),
        in_specs=[
            pl.BlockSpec((rows, DS), lambda i: (0, 0)),
            pl.BlockSpec((DS, PACK * WS), lambda i: (0, i)),
            pl.BlockSpec((DS, PACK * WS), lambda i: (0, i)),
            pl.BlockSpec((rows, PACK * WT), lambda i: (0, i)),
            pl.BlockSpec((rows, PACK * WT), lambda i: (0, i)),
            pl.BlockSpec((rows, SLAB), lambda i: (0, 0)),
        ],
        out_specs=pl.BlockSpec((2, PACK, rows, SLAB), lambda i: (0, i, 0, 0)),
        scratch_shapes=[
            pltpu.VMEM((PACK // 2, 256, 2 * SLAB), jnp.bfloat16),
            pltpu.VMEM((2, 128, 2 * SLAB), jnp.bfloat16),
        ],
        compiler_params=pltpu.CompilerParams(vmem_limit_bytes=56 * 1024 * 1024),
        cost_estimate=pl.CostEstimate(
            flops=8 * rows * DS * heads * WS, bytes_accessed=16_000_000, transcendentals=0
        ),
        name="project_and_pack",
    )(hidden, wq, wk, tq, tk, extra)


def relation_kernel(
    blocks, ends, x, out, xt, wt, ws, t_rings, s_rings, causal, sums, grad, seen, opened, pairs, sem
):
    rows = x.shape[1]
    wide = xt.shape[2]
    f32 = jnp.float32

    def entry(place):
        code = pairs[place]
        query = code & 255
        key = (code >> 8) & 255
        return query, key, code >> 16

    def readable(block):
        return jnp.minimum(block, blocks - 1)

    key_at = lax.broadcasted_iota(jnp.int32, (rows, wide), 0)
    query_at = lax.broadcasted_iota(jnp.int32, (rows, wide), 1)
    causal[0] = jnp.zeros((rows, wide), f32)
    causal[1] = jnp.where(key_at <= query_at, 0.0, -HIDDEN)

    feature = lax.broadcasted_iota(jnp.int32, (SLAB, wide), 0)
    lane = lax.broadcasted_iota(jnp.int32, (SLAB, wide), 1)

    def look(block, carry):
        seen[pl.ds(block, 1)] = x[block, :16].astype(f32)[:1].astype(jnp.int32)
        return carry

    lax.fori_loop(0, blocks, look, 0)
    fetch = pltpu.make_async_copy(seen, opened, sem)
    fetch.start()
    fetch.wait()

    def list_pairs(block, total):
        for back in range(REACH):
            key = jnp.maximum(block - back, 0)
            code = block | (key << 8)
            if back == 0:
                pairs[total + LAG] = code | (1 << 16)
                total = total + 1
            else:
                pairs[total + LAG] = code
                is_open = (block >= back) & (opened[block, MASK0 + back - 1] == 1)
                is_open = is_open & (ends[0, block] == ends[1, key])
                total = total + is_open.astype(jnp.int32)
        return total

    def prepare(block, carry):
        peak_t, peak_s, total = carry
        total = list_pairs(block, total)
        tall = jnp.concatenate([x[block], jnp.zeros((wide - rows, SLAB), jnp.bfloat16)], axis=0)
        turned = tall.T
        xt[block] = turned
        values = turned.astype(f32)
        is_seg = (feature >= SEG0) & (feature < ONE0) & (lane < rows)
        bias = jnp.where(is_seg, (values - 1.0) * HIDDEN, 0.0)
        teacher = jnp.where(feature < WT, values, 0.0)
        student = jnp.where((feature >= WT) & (feature < SEG0), values, 0.0)
        wt[block] = (teacher + bias).astype(jnp.bfloat16)
        ws[block] = (student + bias).astype(jnp.bfloat16)
        grad[block] = jnp.zeros((WS, wide), f32)
        return (
            jnp.maximum(peak_t, jnp.sum(teacher * teacher, axis=0, keepdims=True)),
            jnp.maximum(peak_s, jnp.sum(student * student, axis=0, keepdims=True)),
            total,
        )

    none = jnp.zeros((1, wide), f32)
    peak_t, peak_s, count = lax.fori_loop(0, blocks, prepare, (none, none, 0))
    for place in range(LAG):
        pairs[place] = blocks | (blocks << 8)
    for place in range(LAG + UNROLL):
        pairs[count + LAG + place] = blocks | (blocks << 8)
    bound = jnp.maximum(jnp.max(peak_t) * SCALE_T, jnp.max(peak_s) * SCALE_S)

    @pl.when(jnp.logical_not(bound <= SAFE))
    def _():
        def raise_maxima(place, carry):
            query, key, diagonal = entry(place + LAG)
            for member, weights in enumerate((wt, ws)):
                scores = jnp.dot(x[key], weights[query], preferred_element_type=f32)
                scores = scores + causal[diagonal]
                top = jnp.max(scores.reshape(rows // 8, 8, wide), axis=0)
                sums[query, member] = jnp.where(
                    diagonal == 1, top, jnp.maximum(top, sums[query, member])
                )
            return carry

        lax.fori_loop(0, count, raise_maxima, 0)
        slab_row = lax.broadcasted_iota(jnp.int32, (SLAB - SEG0, wide), 0) + SEG0

        def set_maxima(block, carry):
            for member, weights in enumerate((wt, ws)):
                top = jnp.max(sums[block, member], axis=0, keepdims=True)
                slab = weights[block, SEG0:].astype(f32)
                rest = top
                for part in range(3):
                    piece = rest.astype(jnp.bfloat16).astype(f32)
                    rest = rest - piece
                    slab = jnp.where(slab_row == ONE0 + part, -piece, slab)
                weights[block, SEG0:] = slab.astype(jnp.bfloat16)
            return carry

        lax.fori_loop(0, blocks, set_maxima, 0)

    def inverse(place):
        query, _, _ = entry(place)
        total_t = jnp.sum(sums[query, 0], axis=0, keepdims=True)
        total_s = jnp.sum(sums[query, 1], axis=0, keepdims=True)
        return 1.0 / (total_t * math.sqrt(WS)), 1.0 / (total_s * math.sqrt(WS))

    def weigh(place, slot, t_ring, s_ring):
        query, key, diagonal = entry(place + LAG)
        keys = x[readable(key)]
        hide = causal[diagonal]
        for member, (weights, ring, scale) in enumerate(((wt, t_ring, SCALE_T), (ws, s_ring, SCALE_S))):
            scores = jnp.dot(keys, weights[readable(query)], preferred_element_type=f32)
            made = jnp.exp2(scores * scale + hide)
            ring[slot] = made
            part = jnp.sum(made.reshape(rows // 8, 8, wide), axis=0)
            sums[query, member] = jnp.where(diagonal == 1, part, part + sums[query, member])

    def couple(place, slot, t_ring, s_ring, scales):
        query, key, _ = entry(place)
        coupling = (s_ring[slot] * scales[1] - t_ring[slot] * scales[0]).astype(jnp.bfloat16)
        query_side = xt[readable(query), WT:SEG0]
        key_side = xt[readable(key), WT:SEG0, :rows]
        to_keys = lax.dot_general(
            query_side, coupling, (((1,), (1,)), ((), ())), preferred_element_type=f32
        )
        to_queries = jnp.dot(key_side, coupling, preferred_element_type=f32)
        grad[key, :, :rows] += to_keys
        grad[query] += to_queries

    def steps(turn, carry):
        place = UNROLL * turn
        scales = [inverse(place + step) for step in range(UNROLL)]
        for step in range(UNROLL):
            ring = (step - LAG) % UNROLL
            slot = (turn + (step - LAG) // UNROLL) & (SLOTS - 1)
            couple(place + step, slot, t_rings[ring], s_rings[ring], scales[step])
            weigh(place + step, turn & (SLOTS - 1), t_rings[step], s_rings[step])
        return carry

    lax.fori_loop(0, (count + LAG + UNROLL - 1) // UNROLL, steps, 0)

    def finish(block, carry):
        out[block] = grad[block, :, :rows].astype(jnp.bfloat16)
        return carry

    lax.fori_loop(0, blocks, finish, 0)


def relation(x, ends):
    blocks, rows, _ = x.shape
    wide = (rows + 127) // 128 * 128
    ring = pltpu.VMEM((SLOTS, rows, wide), jnp.float32)
    turned = pltpu.VMEM((blocks, SLAB, wide), jnp.bfloat16)
    return pl.pallas_call(
        functools.partial(relation_kernel, blocks),
        out_shape=jax.ShapeDtypeStruct((blocks, WS, rows), jnp.bfloat16),
        in_specs=[
            pl.BlockSpec(memory_space=pltpu.SMEM),
            pl.BlockSpec(memory_space=pltpu.VMEM),
        ],
        out_specs=pl.BlockSpec(memory_space=pltpu.VMEM),
        scratch_shapes=[
            turned,
            turned,
            turned,
            [ring] * UNROLL,
            [ring] * UNROLL,
            pltpu.VMEM((2, rows, wide), jnp.float32),
            pltpu.VMEM((blocks + 1, 2, 8, wide), jnp.float32),
            pltpu.VMEM((blocks + 1, WS, wide), jnp.float32),
            pltpu.VMEM((blocks, SLAB), jnp.int32),
            pltpu.SMEM((blocks, SLAB), jnp.int32),
            pltpu.SMEM((LIST,), jnp.int32),
            pltpu.SemaphoreType.DMA,
        ],
        compiler_params=pltpu.CompilerParams(vmem_limit_bytes=48 * 1024 * 1024),
        cost_estimate=pl.CostEstimate(
            flops=20_000_000_000, bytes_accessed=5_000_000, transcendentals=40_000_000
        ),
        name="relation_gradient",
    )(ends, x)


def shards(teacher_query, teacher_key, student_hidden, w_query, w_key, segment_ids, block_mask):
    rows = student_hidden.shape[0]
    block = lax.axis_index("ctx")
    ends = jnp.stack([segment_ids[::rows], segment_ids[rows - 1 :: rows]])

    own_seg = lax.dynamic_slice_in_dim(segment_ids, block * rows, rows)
    column = jnp.arange(SLAB, dtype=jnp.int32)[None, :]
    extra = (column == own_seg[:, None] + SEG0) | ((column >= ONE0) & (column < MASK0))
    extra = extra.astype(jnp.float32)
    extra += jnp.pad(block_mask.astype(jnp.float32), ((0, 0), (MASK0, SLAB - MASK0 - REACH + 1)))
    slabs = pack(
        student_hidden, w_query, w_key, teacher_query, teacher_key, extra
    )
    units = slabs.reshape(-1, rows, SLAB)
    row = lax.all_to_all(units, "ctx", 0, 0, tiled=True)
    turned = relation(row, ends)
    back = lax.all_to_all(turned, "ctx", 0, 0, tiled=True)
    half = back.shape[0] // 2
    grads = [back[:half].reshape(-1, rows), back[half:].reshape(-1, rows)]

    side = lax.axis_index("head")
    width = w_query.shape[0] // 2

    def project(part):
        return sum(
            lax.dot_general(
                grad,
                lax.dynamic_slice_in_dim(weight, part * width, width, 0),
                (((0,), (1,)), ((), ())),
                preferred_element_type=jnp.float32,
            )
            for grad, weight in zip(grads, (w_query, w_key))
        )

    away = lax.ppermute(project(1 - side), "head", [(0, 1), (1, 0)])
    return (project(side) + away).astype(jnp.bfloat16)


def solution(mesh):
    placed = (
        P("ctx", "head"),
        P("ctx", "head"),
        P("ctx", None),
        P(None, "head"),
        P(None, "head"),
        P(),
        P("ctx", None),
    )
    return jax.shard_map(
        shards, mesh=mesh, in_specs=placed, out_specs=P("ctx", "head"), check_vma=False
    )
```

time: 1330 us -> 246 us (0.18)
  waiting for transfers between devices: 571 us -> 59.7 us
  matrix products: 397 us -> 9.05 us
  local copies, waits for them, and re-layouts: 192 us -> 2.24 us
  Pallas kernels: 0 us -> 149 us
  starting transfers between devices: 133 us -> 23.4 us
  between operations: 14.1 us -> 0.07 us
    ppermute x42 -> x1, waiting for transfers between devices: 549 us -> 0.01 us  [shards(): away = lax.ppermute(project(1 - side), 'head', [(0, 1), (1, 0)])]
    div x16 -> x0, matrix products: 232 us -> none  [relation_probs(): return weights / jnp.sum(weights, axis=-1, keepdims=True)]
    pallas_call x0 -> x2, Pallas kernels: none -> 149 us  [the longest x1 137 us: relation(): pl.pallas_call(functools.partial(relation_kernel, blocks), out_shape=jax....]
    ppermute x42 -> x1, starting transfers between devices: 133 us -> 3.5 us  [shards(): away = lax.ppermute(project(1 - side), 'head', [(0, 1), (1, 0)])]
    sub x8 -> x0, matrix products: 84.9 us -> none  [relation_probs(): weights = jnp.exp(masked - highest)]
    dynamic_slice x64 -> x0, local copies, waits for them, and re-layouts: 75 us -> none  [columns(): lax.dynamic_slice_in_dim(values, group_index * group * width, group * wid...]
    dot_general x20 -> x4, matrix products: 80.1 us -> 9.05 us  [project(): lax.dot_general(grad, lax.dynamic_slice_in_dim(weight, part * width, widt...]
    all_to_all x0 -> x2, waiting for transfers between devices: none -> 59.7 us  [the longest x1 43.4 us: shards(): row = lax.all_to_all(units, 'ctx', 0, 0, tiled=True)]
  transfers between devices with their start and end apart: 43 -> 3, of which waited for: 32 -> 2; matrix products, arithmetic and copies ran while one was open for 45% -> 2% of each run, Pallas kernels for 0% -> 0%
where the time goes in v1:
time: 246 us
  Pallas kernels  149 us (61%)
  waiting for transfers between devices  59.7 us (24%)
  starting transfers between devices  23.4 us (10%)
  matrix products  9.05 us (4%)
    pallas_call x1, Pallas kernels, relation(): pl.pallas_call(functools.partial(relation_kernel, blocks), out_shape=jax....  137 us
    all_to_all x1, waiting for transfers between devices, shards(): row = lax.all_to_all(units, 'ctx', 0, 0, tiled=True)  43.4 us
    all_to_all x1, waiting for transfers between devices, shards(): back = lax.all_to_all(turned, 'ctx', 0, 0, tiled=True)  16.2 us
    all_to_all x1, starting transfers between devices, shards(): row = lax.all_to_all(units, 'ctx', 0, 0, tiled=True)  12.2 us
    pallas_call x1, Pallas kernels, pack(): pl.pallas_call(pack_kernel, grid=(heads // PACK,), out_shape=jax.ShapeDty...  12.2 us
    dot_general x4, matrix products, project(): lax.dot_general(grad, lax.dynamic_slice_in_dim(weight, part * width, widt...  9.05 us
    all_to_all x1, starting transfers between devices, shards(): back = lax.all_to_all(turned, 'ctx', 0, 0, tiled=True)  7.72 us
  transfers between devices with their start and end apart: 3, of which 2 were waited for; matrix products, arithmetic and copies ran while one was open for 2% of the time, Pallas kernels for 0%

profile of v1, /device:TPU:1, one launch (start us, length us, event | category | flops | bytes accessed | tf_op | source)
XLA Modules:
  0.0 246.0 jit_solution(8217704584099527827)
XLA Ops:
  0.0 0.7 convert_element_type.12
  0.7 0.1 pad_bitcast_fusion
  0.7 0.8 dynamic-slice_add_fusion
  1.5 0.7 convert_add_fusion.extra
  2.3 12.2 %project_and_pack.1 = bf16[2,32,224,128]{3,2,1,0:T(8,128)(2,1)} custom-call(bf16[224,2048]{1,0:T(8,128)(2,1)} %hidden.1, bf16[2048,1024]{1,0:T(8,128)(2,1)} %wq.1, bf16[2048,1024]{1,0:T(8,128)(2,1)} %wk.1, bf16[224,2560]{1,0:T(8,128)(2,1)} %tq.1, bf16[224,2560]{1,0:T(8,128)(2,1)} %tk.1, f32[224,128]{1,0:T(8,128)} %convert_add_fusion.extra), custom_call_target="tpu_custom_call" | custom-call | flops 3758096384 | bytes 16000000 | tf_op jit(solution)/shard_map/project_and_pack/pallas_call | solution.py:69
  14.5 12.2 %all-to-all-start = ((bf16[64,224,128]{2,1,0:T(8,128)(2,1)}), bf16[64,224,128]{2,1,0:T(8,128)(2,1)}, u32[]{:S(2)}, u32[]{:S(2)}) async-start(bf16[64,224,128]{2,1,0:T(8,128)(2,1)} %bitcast.11), calls=%async_computation | async-start | bytes 7340032 | tf_op jit(solution)/shard_map/all_to_all | solution.py:296
  26.7 1.0 slice.12
  27.6 1.0 slice.13
  28.6 43.4 %all-to-all-done.x = bf16[64,224,128]{2,1,0:T(8,128)(2,1)} async-done(((bf16[64,224,128]{2,1,0:T(8,128)(2,1)}), bf16[64,224,128]{2,1,0:T(8,128)(2,1)}, u32[]{:S(2)}, u32[]{:S(2)}) %all-to-all-start) | async-done | bytes 3670048 | tf_op jit(solution)/shard_map/all_to_all | solution.py:296
  72.0 137.2 %relation_gradient.1 = bf16[64,32,224]{2,1,0:T(8,128)(2,1)} custom-call(s32[2,64]{1,0:T(2,128)S(1)} %pad_add_fusion.ends, bf16[64,224,128]{2,1,0:T(8,128)(2,1)} %all-to-all-done.x), custom_call_target="tpu_custom_call" | custom-call | flops 20000000000 | bytes 5000000 | tf_op jit(solution)/shard_map/relation_gradient/pallas_call | solution.py:252
  209.2 7.7 %all-to-all-start.1 = ((bf16[64,32,224]{2,1,0:T(8,128)(2,1)}), bf16[64,32,224]{2,1,0:T(8,128)(2,1)S(1)}, u32[]{:S(2)}, u32[]{:S(2)}) async-start(bf16[64,32,224]{2,1,0:T(8,128)(2,1)} %relation_gradient.1), calls=%async_computation.1 | async-start | bytes 2097152 | tf_op jit(solution)/shard_map/all_to_all | solution.py:298
  216.9 16.2 %all-to-all-done.1 = bf16[64,32,224]{2,1,0:T(8,128)(2,1)S(1)} async-done(((bf16[64,32,224]{2,1,0:T(8,128)(2,1)}), bf16[64,32,224]{2,1,0:T(8,128)(2,1)S(1)}, u32[]{:S(2)}, u32[]{:S(2)}) %all-to-all-start.1) | async-done | bytes 917536 | tf_op jit(solution)/shard_map/all_to_all | solution.py:298
  233.2 0.0 copy-start
  233.2 0.1 fusion.25
  233.3 2.6 %fusion = f32[224,1024]{1,0:T(8,128)S(1)} fusion(bf16[1024,224]{1,0:T(8,128)(2,1)S(1)} %bitcast.14, bf16[2048,1024]{1,0:T(8,128)(2,1)} %wk.1, s32[]{:T(128)S(6)} %select_n.13), kind=kOutput, calls=%fused_computation | convolution fusion | flops 469762048 | bytes 3473412 | tf_op jit(solution)/shard_map/dot_general | solution.py:307
  235.8 0.2 copy-done
  236.0 0.8 fusion.14
  236.9 3.5 %collective-permute-start = (f32[224,1024]{1,0:T(8,128)S(1)}, f32[224,1024]{1,0:T(8,128)S(1)}, u32[]{:S(2)}, u32[]{:S(2)}) collective-permute-start(f32[224,1024]{1,0:T(8,128)S(1)} %fusion.14), channel_id=1, source_target_pairs={{0,1},{1,0},{2,3},{3,2},{4,5},{5,4},{6,7},{7,6},{8,9},{9,8},{10,11... | collective-permute-start | bytes 2752520 | tf_op jit(solution)/shard_map/ppermute | solution.py:316
  240.4 2.4 fusion.4
  242.8 0.0 collective-permute-done
  242.8 3.2 %fusion.17 = bf16[224,1024]{1,0:T(8,128)(2,1)} fusion(f32[224,1024]{1,0:T(8,128)S(1)} %collective-permute-done, f32[224,1024]{1,0:T(8,128)S(1)} %fusion.4, bf16[1024,224]{1,0:T(8,128)(2,1)S(1)} %bitcast.13, bf16[2048,1024]{1,0:T(8,128)(2,1)} %wq.1, s32[]{:T(128)S(6)} %select_n.12), kind=kOutput, calls=%fused_computation.11 | convolution fusion | flops 470450176 | bytes 4849668 | tf_op jit(solution)/shard_map/dot_general | solution.py:307
  (2 shorter events, 0.0 us)
Async XLA Ops:
  14.5 57.6 %all-to-all-start = ((bf16[64,224,128]{2,1,0:T(8,128)(2,1)}), bf16[64,224,128]{2,1,0:T(8,128)(2,1)}, u32[]{:S(2)}, u32[]{:S(2)}) async-start(bf16[64,224,128]{2,1,0:T(8,128)(2,1)} %bitcast.11), calls=%async_computation | async-start | bytes 7340032 | tf_op jit(solution)/shard_map/all_to_all | solution.py:296
  209.2 24.0 %all-to-all-start.1 = ((bf16[64,32,224]{2,1,0:T(8,128)(2,1)}), bf16[64,32,224]{2,1,0:T(8,128)(2,1)S(1)}, u32[]{:S(2)}, u32[]{:S(2)}) async-start(bf16[64,32,224]{2,1,0:T(8,128)(2,1)} %relation_gradient.1), calls=%async_computation.1 | async-start | bytes 2097152 | tf_op jit(solution)/shard_map/all_to_all | solution.py:298
  233.2 2.8 %copy-start = (bf16[2048,1024]{1,0:T(8,128)(2,1)S(1)}, bf16[2048,1024]{1,0:T(8,128)(2,1)}, u32[]{:S(2)}) copy-start(bf16[2048,1024]{1,0:T(8,128)(2,1)} %wq.1) | copy-start | bytes 12582916
  236.9 5.9 %collective-permute-start = (f32[224,1024]{1,0:T(8,128)S(1)}, f32[224,1024]{1,0:T(8,128)S(1)}, u32[]{:S(2)}, u32[]{:S(2)}) collective-permute-start(f32[224,1024]{1,0:T(8,128)S(1)} %fusion.14), channel_id=1, source_target_pairs={{0,1},{1,0},{2,3},{3,2},{4,5},{5,4},{6,7},{7,6},{8,9},{9,8},{10,11... | collective-permute-start | bytes 2752520 | tf_op jit(solution)/shard_map/ppermute | solution.py:316

commit v2 on v0

v2 whole, which is shorter than its diff:
```python
import functools
import math

import jax
import jax.numpy as jnp
from jax import lax
from jax.experimental import pallas as pl
from jax.experimental.pallas import tpu as pltpu
from jax.sharding import PartitionSpec as P

DT = 5120
DS = 2048
HEADS = 64
REACH = 8
WT = DT // HEADS
WS = DS // HEADS
DEPTH = 128
EXTRA = 16
DOCS = 4
PACK = 8
LISTED = 8
UNROLL = 4
LAG = 3 * UNROLL
SLOTS = 4
AHEAD = 2
LIST = 640
HIDDEN = 1e30
LOG2E = math.log2(math.e)
SCALE_T = LOG2E / math.sqrt(WT)
SCALE_S = LOG2E / math.sqrt(WS)
SAFE = 90.0
MIB = 1024 * 1024
f32 = jnp.float32
bf16 = jnp.bfloat16


def round_up(value, unit):
    return (value + unit - 1) // unit * unit


def project_kernel(hidden, wq, wk, extra, out):
    for rel, weight in enumerate((wq, wk)):
        student = jnp.dot(hidden[...], weight[...], preferred_element_type=f32).astype(bf16)
        turned = jnp.concatenate([student, extra[...]], axis=0).T
        out[rel] = turned.reshape(out.shape[1:])


def project(hidden, wq, wk, mask):
    rows = hidden.shape[0]
    wide = round_up(rows, 128)
    heads = wq.shape[1] // WS
    extra = jnp.pad(mask.astype(bf16).T, ((0, wide - rows - REACH + 1), (0, 0)))
    extra = jnp.broadcast_to(extra, (wide - rows, PACK * WS))
    return pl.pallas_call(
        project_kernel,
        grid=(heads // PACK,),
        out_shape=jax.ShapeDtypeStruct((2, heads, WS, wide), bf16),
        in_specs=[
            pl.BlockSpec((rows, DS), lambda i: (0, 0)),
            pl.BlockSpec((DS, PACK * WS), lambda i: (0, i)),
            pl.BlockSpec((DS, PACK * WS), lambda i: (0, i)),
            pl.BlockSpec((wide - rows, PACK * WS), lambda i: (0, 0)),
        ],
        out_specs=pl.BlockSpec((2, PACK, WS, wide), lambda i: (0, i, 0, 0)),
        compiler_params=pltpu.CompilerParams(vmem_limit_bytes=56 * MIB),
        cost_estimate=pl.CostEstimate(
            flops=4 * rows * DS * heads * WS, bytes_accessed=10_000_000, transcendentals=0
        ),
        name="project_student",
    )(hidden, wq, wk, extra)


def turn_kernel(tq, tk, out):
    rows = tq.shape[0]
    wide = out.shape[-1]
    for rel, teacher in enumerate((tq, tk)):
        zeros = jnp.zeros((wide - rows, teacher.shape[1]), bf16)
        turned = jnp.concatenate([teacher[...], zeros], axis=0).T
        out[rel] = turned.reshape(out.shape[1:])


def turn(tq, tk):
    rows, columns = tq.shape
    wide = round_up(rows, 128)
    heads = columns // WT
    return pl.pallas_call(
        turn_kernel,
        grid=(heads // PACK,),
        out_shape=jax.ShapeDtypeStruct((2, heads, WT, wide), bf16),
        in_specs=[pl.BlockSpec((rows, PACK * WT), lambda i: (0, i))] * 2,
        out_specs=pl.BlockSpec((2, PACK, WT, wide), lambda i: (0, i, 0, 0)),
        compiler_params=pltpu.CompilerParams(vmem_limit_bytes=56 * MIB),
        cost_estimate=pl.CostEstimate(flops=0, bytes_accessed=5_000_000, transcendentals=0),
        name="turn_teacher",
    )(tq, tk)


def read_pair(pairs, place):
    code = pairs[place]
    return code & 255, code >> 8


def fill(block, slab, segments, keys, weights):
    width, wide = slab.shape
    rows = keys.shape[1]
    row = lax.broadcasted_iota(jnp.int32, (EXTRA, wide), 0)
    lane = lax.broadcasted_iota(jnp.int32, (EXTRA, wide), 1)
    hot = jnp.where(row == segments[pl.ds(block, 1)], 1.0, 0.0)
    key_extra = jnp.where((row >= DOCS) & (row < DOCS + 3), 1.0, hot)
    query_extra = jnp.where((row < DOCS) & (lane < rows), (hot - 1.0) * HIDDEN, 0.0)
    zeros = jnp.zeros((DEPTH - EXTRA - width, wide), bf16)
    weights[block] = jnp.concatenate([slab, query_extra.astype(bf16), zeros], axis=0)
    keys[block] = jnp.concatenate([slab, key_extra.astype(bf16), zeros], axis=0).T[:rows]
    values = slab.astype(f32)
    return jnp.sum(values * values, axis=0, keepdims=True)


def subtract_maxima(width, blocks, count, pairs, keys, weights, causal, sums):
    rows, wide = causal.shape

    def highest(query, key):
        return jnp.dot(keys[key], weights[query], preferred_element_type=f32)

    def fold(scores):
        return jnp.max(scores.reshape(rows // 8, 8, wide), axis=0)

    def own_maxima(block, carry):
        sums[block] = fold(highest(block, block) + causal[...])
        return carry

    def raise_maxima(place, carry):
        query, key = read_pair(pairs, place + LAG)
        sums[query] = jnp.maximum(fold(highest(query, key)), sums[query])
        return carry

    lax.fori_loop(0, blocks, own_maxima, 0)
    lax.fori_loop(0, count, raise_maxima, 0)
    row = lax.broadcasted_iota(jnp.int32, (EXTRA, wide), 0)

    def set_maxima(block, carry):
        rest = jnp.max(sums[block], axis=0, keepdims=True)
        extra = weights[block, width : width + EXTRA].astype(f32)
        for part in range(3):
            piece = rest.astype(bf16).astype(f32)
            rest = rest - piece
            extra = jnp.where(row == DOCS + part, -piece, extra)
        weights[block, width : width + EXTRA] = extra.astype(bf16)
        return carry

    lax.fori_loop(0, blocks, set_maxima, 0)


def fill_causal(causal):
    key_at = lax.broadcasted_iota(jnp.int32, causal.shape, 0)
    query_at = lax.broadcasted_iota(jnp.int32, causal.shape, 1)
    causal[...] = jnp.where(key_at <= query_at, 0.0, -HIDDEN)


def weigh(query, key, keys, weights, scale, hide=None):
    last = keys.shape[0] - 1
    scores = jnp.dot(
        keys[jnp.minimum(key, last)],
        weights[jnp.minimum(query, last)],
        preferred_element_type=f32,
    )
    scores = scores * scale
    made = jnp.exp2(scores if hide is None else scores + hide)
    rows, wide = made.shape
    return made, jnp.sum(made.reshape(rows // 8, 8, wide), axis=0)


def student_kernel(
    blocks, ends, segments, slabs, made, scales, features, pairs, count_out, keys, weights, ring, causal, sums, seen, opened, sem, sems
):
    rows, wide = causal.shape
    fill_causal(causal)

    def look(block, carry):
        seen[pl.ds(block, 1)] = slabs[block, :16, wide - 128 :].astype(f32)[:1].astype(jnp.int32)
        return carry

    lax.fori_loop(0, blocks, look, 0)
    fetch = pltpu.make_async_copy(seen, opened, sem)
    fetch.start()
    fetch.wait()
    mask_lane = rows % 128

    def list_pairs(block, total):
        for back in range(1, REACH):
            key = jnp.maximum(block - back, 0)
            pairs[total + LAG] = block | (key << 8)
            is_open = (block >= back) & (opened[block, mask_lane + back - 1] == 1)
            is_open = is_open & (ends[0, block] == ends[1, key])
            total = total + is_open.astype(jnp.int32)
        return total

    lane = lax.broadcasted_iota(jnp.int32, (WS, wide), 1)

    def prepare(block, carry):
        peak, total = carry
        total = list_pairs(block, total)
        slab = jnp.where(lane < rows, slabs[block].astype(f32), 0.0).astype(bf16)
        features[block] = slab
        return jnp.maximum(peak, fill(block, slab, segments, keys, weights)), total

    peak, count = lax.fori_loop(0, blocks, prepare, (jnp.zeros((1, wide), f32), 0))
    count_out[0] = count
    for place in range(LAG):
        pairs[place] = blocks | (blocks << 8)
    for place in range(LAG + LISTED):
        pairs[count + LAG + place] = blocks | (blocks << 8)

    @pl.when(jnp.logical_not(jnp.max(peak) * SCALE_S <= SAFE))
    def _():
        subtract_maxima(WS, blocks, count, pairs, keys, weights, causal, sums)

    def send(turn):
        slot = turn & (SLOTS - 1)
        group = made.at[pl.ds(turn * LISTED, LISTED)]
        return pltpu.make_async_copy(ring.at[slot], group, sems.at[slot])

    def free(turn):
        @pl.when(turn >= SLOTS)
        def _():
            send(turn - SLOTS).wait()

    own_turns = blocks // LISTED

    def own(turn, carry):
        free(turn)
        for step in range(LISTED):
            block = turn * LISTED + step
            ring[turn & (SLOTS - 1), step], sums[block] = weigh(
                block, block, keys, weights, SCALE_S, causal[...]
            )
        send(turn).start()
        return carry

    def others(turn, carry):
        free(turn)
        for step in range(LISTED):
            query, key = read_pair(pairs, (turn - own_turns) * LISTED + step + LAG)
            ring[turn & (SLOTS - 1), step], part = weigh(query, key, keys, weights, SCALE_S)
            sums[query] += part
        send(turn).start()
        return carry

    def drain(turn, carry):
        send(turn).wait()
        return carry

    turns = own_turns + (count + LISTED - 1) // LISTED
    lax.fori_loop(0, own_turns, own, 0)
    lax.fori_loop(own_turns, turns, others, 0)
    lax.fori_loop(turns - SLOTS, turns, drain, 0)

    def finish(block, carry):
        total = jnp.sum(sums[block], axis=0, keepdims=True) * math.sqrt(WS)
        scales[block] = jnp.broadcast_to(1.0 / total, (8, wide))
        return carry

    lax.fori_loop(0, blocks, finish, 0)


def student_weights(slabs, ends, segments, rows):
    blocks, _, wide = slabs.shape
    vmem = pl.BlockSpec(memory_space=pltpu.VMEM)
    smem = pl.BlockSpec(memory_space=pltpu.SMEM)
    return pl.pallas_call(
        functools.partial(student_kernel, blocks),
        out_shape=(
            jax.ShapeDtypeStruct((blocks * REACH, rows, wide), f32),
            jax.ShapeDtypeStruct((blocks, 8, wide), f32),
            jax.ShapeDtypeStruct((blocks, WS, wide), bf16),
            jax.ShapeDtypeStruct((LIST,), jnp.int32),
            jax.ShapeDtypeStruct((1,), jnp.int32),
        ),
        in_specs=[smem, vmem, vmem],
        out_specs=(pl.BlockSpec(memory_space=pl.ANY), vmem, vmem, smem, smem),
        scratch_shapes=[
            pltpu.VMEM((blocks, rows, DEPTH), bf16),
            pltpu.VMEM((blocks, DEPTH, wide), bf16),
            pltpu.VMEM((SLOTS, LISTED, rows, wide), f32),
            pltpu.VMEM((rows, wide), f32),
            pltpu.VMEM((blocks + 1, 8, wide), f32),
            pltpu.VMEM((blocks, 128), jnp.int32),
            pltpu.SMEM((blocks, 128), jnp.int32),
            pltpu.SemaphoreType.DMA,
            pltpu.SemaphoreType.DMA((SLOTS,)),
        ],
        compiler_params=pltpu.CompilerParams(vmem_limit_bytes=48 * MIB),
        cost_estimate=pl.CostEstimate(
            flops=10_000_000_000, bytes_accessed=80_000_000, transcendentals=20_000_000
        ),
        name="student_weights",
    )(ends, segments, slabs)


def gradient_kernel(
    blocks, count_in, pairs, segments, slabs, made, scales, features, out, keys, weights, rings, own_ring, fetched, causal, sums, grad, sems
):
    rows, wide = causal.shape
    count = count_in[0]
    fill_causal(causal)
    turns = (count + LAG + UNROLL - 1) // UNROLL

    def fetch(turn):
        group = jnp.clip(turn - LAG // UNROLL, 0, (made.shape[0] - blocks) // UNROLL - 1)
        first = jnp.where(turn < turns, blocks + group * UNROLL, (turn - turns) * UNROLL)
        slot = turn & (SLOTS - 1)
        group = made.at[pl.ds(first, UNROLL)]
        return pltpu.make_async_copy(group, fetched.at[slot], sems.at[slot])

    for turn in range(AHEAD):
        fetch(turn).start()

    def prepare(block, peak):
        grad[block] = jnp.zeros((WS, wide), f32)
        return jnp.maximum(peak, fill(block, slabs[block], segments, keys, weights))

    peak = lax.fori_loop(0, blocks, prepare, jnp.zeros((1, wide), f32))

    @pl.when(jnp.logical_not(jnp.max(peak) * SCALE_T <= SAFE))
    def _():
        subtract_maxima(WT, blocks, count, pairs, keys, weights, causal, sums)

    def readable(block):
        return jnp.minimum(block, blocks - 1)

    def inverses(query):
        total = jnp.sum(sums[query], axis=0, keepdims=True) * math.sqrt(WS)
        return 1.0 / total, scales[readable(query), :1]

    def couple(query, key, teacher, student, scale):
        coupling = (student * scale[1] - teacher * scale[0]).astype(bf16)
        query_side = features[readable(query)]
        key_side = features[readable(key), :, :rows]
        grad[key, :, :rows] += lax.dot_general(
            query_side, coupling, (((1,), (1,)), ((), ())), preferred_element_type=f32
        )
        grad[query] += jnp.dot(key_side, coupling, preferred_element_type=f32)

    def own_weights(turn, carry):
        for step in range(UNROLL):
            block = turn * UNROLL + step
            own_ring[block], sums[block] = weigh(
                block, block, keys, weights, SCALE_T, causal[...]
            )
        return carry

    def half(turn, parity):
        slot = turn & (SLOTS - 1)
        fetch(turn).wait()
        fetch(turn + AHEAD).start()
        place = UNROLL * turn
        old = [read_pair(pairs, place + step) for step in range(UNROLL)]
        new = [read_pair(pairs, place + step + LAG) for step in range(UNROLL)]
        scale = [inverses(query) for query, _ in old]
        now = turn >> 1 & 1
        before = (turn - LAG // UNROLL) >> 1 & 1
        for step in range(UNROLL):
            teacher = rings[1 - parity][before, step]
            couple(*old[step], teacher, fetched[slot, step], scale[step])
            rings[parity][now, step], part = weigh(*new[step], keys, weights, SCALE_T)
            sums[new[step][0]] += part

    def others(turn, carry):
        for parity in range(2):
            pl.when(turn & 1 == parity)(functools.partial(half, turn, parity))
        return carry

    own_turns = blocks // UNROLL

    def own_terms(turn, carry):
        slot = turn & (SLOTS - 1)
        fetch(turn).wait()

        @pl.when(turn + AHEAD < turns + own_turns)
        def _():
            fetch(turn + AHEAD).start()

        scale = [inverses((turn - turns) * UNROLL + step) for step in range(UNROLL)]
        for step in range(UNROLL):
            block = (turn - turns) * UNROLL + step
            couple(block, block, own_ring[block], fetched[slot, step], scale[step])
        return carry

    lax.fori_loop(0, own_turns, own_weights, 0)
    lax.fori_loop(0, turns, others, 0)
    lax.fori_loop(turns, turns + own_turns, own_terms, 0)

    def finish(block, carry):
        out[block] = grad[block, :, :rows].astype(bf16)
        return carry

    lax.fori_loop(0, blocks, finish, 0)


def relation_gradient(slabs, segments, made, scales, features, pairs, count):
    blocks, _, wide = slabs.shape
    rows = made.shape[1]
    vmem = pl.BlockSpec(memory_space=pltpu.VMEM)
    smem = pl.BlockSpec(memory_space=pltpu.SMEM)
    return pl.pallas_call(
        functools.partial(gradient_kernel, blocks),
        out_shape=jax.ShapeDtypeStruct((blocks, WS, rows), bf16),
        in_specs=[smem, smem, vmem, vmem, pl.BlockSpec(memory_space=pl.ANY), vmem, vmem],
        out_specs=vmem,
        scratch_shapes=[
            pltpu.VMEM((blocks, rows, DEPTH), bf16),
            pltpu.VMEM((blocks, DEPTH, wide), bf16),
            [pltpu.VMEM((2, UNROLL, rows, wide), f32)] * 2,
            pltpu.VMEM((blocks, rows, wide), f32),
            pltpu.VMEM((SLOTS, UNROLL, rows, wide), f32),
            pltpu.VMEM((rows, wide), f32),
            pltpu.VMEM((blocks + 1, 8, wide), f32),
            pltpu.VMEM((blocks + 1, WS, wide), f32),
            pltpu.SemaphoreType.DMA((SLOTS,)),
        ],
        compiler_params=pltpu.CompilerParams(vmem_limit_bytes=56 * MIB),
        cost_estimate=pl.CostEstimate(
            flops=20_000_000_000, bytes_accessed=80_000_000, transcendentals=20_000_000
        ),
        name="relation_gradient",
    )(count, pairs, segments, slabs, made, scales, features)


def head_gradient(student, teacher, segment_ids, rows):
    blocks, _, wide = student.shape
    ends = jnp.stack([segment_ids[::rows], segment_ids[rows - 1 :: rows]])
    segments = jnp.pad(
        segment_ids.reshape(blocks, rows), ((0, 0), (0, wide - rows)), constant_values=-1
    )
    made, scales, features, pairs, count = student_weights(student, ends, segments, rows)
    return relation_gradient(teacher, segments, made, scales, features, pairs, count)


def shards(teacher_query, teacher_key, student_hidden, w_query, w_key, segment_ids, block_mask):
    rows = student_hidden.shape[0]
    student = project(student_hidden, w_query, w_key, block_mask)
    teacher = turn(teacher_query, teacher_key)
    student = lax.all_to_all(student.reshape(-1, *student.shape[2:]), "ctx", 0, 0, tiled=True)
    teacher = lax.all_to_all(teacher.reshape(-1, *teacher.shape[2:]), "ctx", 0, 0, tiled=True)
    turned = head_gradient(student, teacher, segment_ids, rows)
    back = lax.all_to_all(turned, "ctx", 0, 0, tiled=True)
    half = back.shape[0] // 2
    grads = [back[:half].reshape(-1, rows), back[half:].reshape(-1, rows)]

    side = lax.axis_index("head")
    width = w_query.shape[0] // 2

    def unproject(part):
        return sum(
            lax.dot_general(
                grad,
                lax.dynamic_slice_in_dim(weight, part * width, width, 0),
                (((0,), (1,)), ((), ())),
                preferred_element_type=f32,
            )
            for grad, weight in zip(grads, (w_query, w_key))
        )

    away = lax.ppermute(unproject(1 - side), "head", [(0, 1), (1, 0)])
    return (unproject(side) + away).astype(bf16)


def solution(mesh):
    placed = (
        P("ctx", "head"),
        P("ctx", "head"),
        P("ctx", None),
        P(None, "head"),
        P(None, "head"),
        P(),
        P("ctx", None),
    )
    return jax.shard_map(
        shards, mesh=mesh, in_specs=placed, out_specs=P("ctx", "head"), check_vma=False
    )
```

time: 1330 us -> 291 us (0.22)
  waiting for transfers between devices: 571 us -> 28.4 us
  matrix products: 397 us -> 9.06 us
  Pallas kernels: 0 us -> 218 us
  local copies, waits for them, and re-layouts: 192 us -> 3.74 us
  starting transfers between devices: 133 us -> 31.6 us
  other arithmetic: 14.7 us -> 0.67 us
  between operations: 14.1 us -> 0.15 us
    ppermute x42 -> x1, waiting for transfers between devices: 549 us -> 0.01 us  [shards(): away = lax.ppermute(unproject(1 - side), 'head', [(0, 1), (1, 0)])]
    div x16 -> x0, matrix products: 232 us -> none  [relation_probs(): return weights / jnp.sum(weights, axis=-1, keepdims=True)]
    pallas_call x0 -> x4, Pallas kernels: none -> 218 us  [the longest x1 120 us: relation_gradient(): pl.pallas_call(functools.partial(gradient_kernel, blocks), out_shape=jax....]
    ppermute x42 -> x1, starting transfers between devices: 133 us -> 4.22 us  [shards(): away = lax.ppermute(unproject(1 - side), 'head', [(0, 1), (1, 0)])]
    sub x8 -> x0, matrix products: 84.9 us -> none  [relation_probs(): weights = jnp.exp(masked - highest)]
    dynamic_slice x64 -> x0, local copies, waits for them, and re-layouts: 75 us -> none  [columns(): lax.dynamic_slice_in_dim(values, group_index * group * width, group * wid...]
    dot_general x20 -> x4, matrix products: 80.1 us -> 9.06 us  [unproject(): lax.dot_general(grad, lax.dynamic_slice_in_dim(weight, part * width, widt...]
    dynamic_update_slice x32 -> x0, local copies, waits for them, and re-layouts: 44.2 us -> none  [the longest x16 37.1 us: one_group(): lax.dynamic_update_slice_in_dim(key_total, key_part, group_index * group...]
  transfers between devices with their start and end apart: 43 -> 4, of which waited for: 32 -> 2; matrix products, arithmetic and copies ran while one was open for 45% -> 1% of each run, Pallas kernels for 0% -> 31%
where the time goes in v2:
time: 291 us; the launch traced here: 292 us
  Pallas kernels  218 us (75%)
  starting transfers between devices  31.6 us (11%)
  waiting for transfers between devices  28.4 us (10%)
  matrix products  9.06 us (3%)
  local copies, waits for them, and re-layouts  3.74 us (1%)
    pallas_call x1, Pallas kernels, relation_gradient(): pl.pallas_call(functools.partial(gradient_kernel, blocks), out_shape=jax....  120 us
    pallas_call x1, Pallas kernels, student_weights(): pl.pallas_call(functools.partial(student_kernel, blocks), out_shape=(jax....  87.2 us
    all_to_all x1, waiting for transfers between devices, shards(): back = lax.all_to_all(turned, 'ctx', 0, 0, tiled=True)  15.5 us
    all_to_all x1, waiting for transfers between devices, shards(): lax.all_to_all(student.reshape(-1, *student.shape[2:]), 'ctx', 0, 0, tile...  12.8 us
    all_to_all x1, starting transfers between devices, shards(): lax.all_to_all(student.reshape(-1, *student.shape[2:]), 'ctx', 0, 0, tile...  12 us
    all_to_all x1, starting transfers between devices, shards(): back = lax.all_to_all(turned, 'ctx', 0, 0, tiled=True)  9.72 us
    dot_general x4, matrix products, unproject(): lax.dot_general(grad, lax.dynamic_slice_in_dim(weight, part * width, widt...  9.06 us
    pallas_call x1, Pallas kernels, project(): pl.pallas_call(project_kernel, grid=(heads // PACK,), out_shape=jax.Shape...  6.66 us
  transfers between devices with their start and end apart: 4, of which 2 were waited for; matrix products, arithmetic and copies ran while one was open for 1% of the time, Pallas kernels for 31%

profile of v2, /device:TPU:1, one launch (start us, length us, event | category | flops | bytes accessed | tf_op | source)
XLA Modules:
  0.0 291.8 jit_solution(1248610254566100092)
XLA Ops:
  0.0 0.7 convert_bitcast_fusion
  0.7 0.7 broadcast_in_dim.8.extra
  1.3 6.7 %project_student.1 = bf16[2,32,32,256]{3,2,1,0:T(8,128)(2,1)} custom-call(bf16[224,2048]{1,0:T(8,128)(2,1)} %hidden.1, bf16[2048,1024]{1,0:T(8,128)(2,1)} %wq.1, bf16[2048,1024]{1,0:T(8,128)(2,1)} %wk.1, bf16[32,256]{1,0:T(8,128)(2,1)} %broadcast_in_dim.8.extra), custom_call_target="tpu_custom_call" | custom-call | flops 1879048192 | bytes 10000000 | tf_op jit(solution)/shard_map/project_student/pallas_call | solution.py:54
  8.0 12.0 %all-to-all-start = ((bf16[64,32,256]{2,1,0:T(8,128)(2,1)}), bf16[64,32,256]{2,1,0:T(8,128)(2,1)S(1)}, u32[]{:S(2)}, u32[]{:S(2)}) async-start(bf16[64,32,256]{2,1,0:T(8,128)(2,1)} %bitcast.19), calls=%async_computation | async-start | bytes 2097152 | tf_op jit(solution)/shard_map/all_to_all | solution.py:442
  20.0 4.3 %turn_teacher.1 = bf16[2,32,80,256]{3,2,1,0:T(8,128)(2,1)} custom-call(bf16[224,2560]{1,0:T(8,128)(2,1)} %tq.1, bf16[224,2560]{1,0:T(8,128)(2,1)} %tk.1), custom_call_target="tpu_custom_call" | custom-call | bytes 5000000 | tf_op jit(solution)/shard_map/turn_teacher/pallas_call | solution.py:86
  24.3 12.8 %all-to-all-done.slabs = bf16[64,32,256]{2,1,0:T(8,128)(2,1)S(1)} async-done(((bf16[64,32,256]{2,1,0:T(8,128)(2,1)}), bf16[64,32,256]{2,1,0:T(8,128)(2,1)S(1)}, u32[]{:S(2)}, u32[]{:S(2)}) %all-to-all-start) | async-done | bytes 1048608 | tf_op jit(solution)/shard_map/all_to_all | solution.py:442
  37.1 0.0 copy-start.5
  37.1 5.7 %all-to-all-start.1 = ((bf16[64,80,256]{2,1,0:T(8,128)(2,1)}), bf16[64,80,256]{2,1,0:T(8,128)(2,1)}, u32[]{:S(2)}, u32[]{:S(2)}) async-start(bf16[64,80,256]{2,1,0:T(8,128)(2,1)} %bitcast.14), calls=%async_computation.1 | async-start | bytes 5242880 | tf_op jit(solution)/shard_map/all_to_all | solution.py:443
  42.9 0.0 copy-done.5
  42.9 0.1 slice.12
  43.0 0.2 slice.13
  43.2 0.1 reshape.15
  43.3 0.0 copy-start.2
  43.3 87.2 %student_weights.1 = (f32[512,224,256]{2,1,0:T(8,128)}, f32[64,8,256]{2,1,0:T(8,128)S(1)}, bf16[64,32,256]{2,1,0:T(8,128)(2,1)S(1)}, s32[640]{0:T(1024)S(1)}, s32[1]{0:T(128)}) custom-call(s32[2,64]{1,0:T(2,128)S(1)} %pad_add_fusion.ends, s32[64,256]{1,0:T(8,128)S(1)} %pad.8.segments, bf16[64,32,256]{2,1,0:T(8,128)(2,1)S(1)} %all-to-all-done.slabs), custom_call_target="tpu_custom_call" | custom-call | flops 10000000000 | bytes 80000000 | tf_op jit(solution)/shard_map/student_weights/pallas_call | solution.py:269
  130.5 0.0 copy-done.2
  130.5 0.0 copy-start
  130.5 1.0 copy-done
  131.5 0.0 copy-start.1
  131.5 0.8 copy-done.1
  132.4 0.0 copy-start.3
  132.4 0.6 copy-done.3
  132.9 0.0 all-to-all-done.1.slabs
  132.9 120.1 %relation_gradient.1 = bf16[64,32,224]{2,1,0:T(8,128)(2,1)} custom-call(s32[1]{0:T(128)} %get-tuple-element.10.count_in, s32[640]{0:T(1024)} %copy-done.3, s32[64,256]{1,0:T(8,128)} %copy-done.2, bf16[64,80,256]{2,1,0:T(8,128)(2,1)} %all-to-all-done.1.slabs, f32[512,224,256]{2,1,0:T(8,128)} %get-tuple-element.12.made, f32[64,8,256]{2,1,0:T(8,128)} %copy-done.1, ...), custom_call_target="tpu_custom_call" | custom-call | flops 20000000000 | bytes 80000000 | tf_op jit(solution)/shard_map/relation_gradient/pallas_call | solution.py:404
  253.0 9.7 %all-to-all-start.2 = ((bf16[64,32,224]{2,1,0:T(8,128)(2,1)}), bf16[64,32,224]{2,1,0:T(8,128)(2,1)S(1)}, u32[]{:S(2)}, u32[]{:S(2)}) async-start(bf16[64,32,224]{2,1,0:T(8,128)(2,1)} %relation_gradient.1), calls=%async_computation.2 | async-start | bytes 2097152 | tf_op jit(solution)/shard_map/all_to_all | solution.py:445
  262.7 15.5 %all-to-all-done.2 = bf16[64,32,224]{2,1,0:T(8,128)(2,1)S(1)} async-done(((bf16[64,32,224]{2,1,0:T(8,128)(2,1)}), bf16[64,32,224]{2,1,0:T(8,128)(2,1)S(1)}, u32[]{:S(2)}, u32[]{:S(2)}) %all-to-all-start.2) | async-done | bytes 917536 | tf_op jit(solution)/shard_map/all_to_all | solution.py:445
  278.3 0.0 copy-start.4
  278.3 0.1 fusion.24
  278.3 2.6 fusion
  280.9 0.2 copy-done.4
  281.1 0.8 fusion.14
  281.9 4.2 %collective-permute-start = (f32[224,1024]{1,0:T(8,128)S(1)}, f32[224,1024]{1,0:T(8,128)S(1)}, u32[]{:S(2)}, u32[]{:S(2)}) collective-permute-start(f32[224,1024]{1,0:T(8,128)S(1)} %fusion.14), channel_id=1, source_target_pairs={{0,1},{1,0},{2,3},{3,2},{4,5},{5,4},{6,7},{7,6},{8,9},{9,8},{10,11... | collective-permute-start | bytes 2752520 | tf_op jit(solution)/shard_map/ppermute | solution.py:463
  286.2 2.4 fusion.4
  288.6 0.0 collective-permute-done
  288.6 3.2 %fusion.17 = bf16[224,1024]{1,0:T(8,128)(2,1)} fusion(f32[224,1024]{1,0:T(8,128)S(1)} %collective-permute-done, f32[224,1024]{1,0:T(8,128)S(1)} %fusion.4, bf16[1024,224]{1,0:T(8,128)(2,1)S(1)} %bitcast.16, bf16[2048,1024]{1,0:T(8,128)(2,1)} %wq.1, s32[]{:T(128)S(6)} %select_n.8), kind=kOutput, calls=%fused_computation.11 | convolution fusion | flops 470450176 | bytes 4849668 | tf_op jit(solution)/shard_map/dot_general | solution.py:454
  (3 shorter events, 0.0 us)
Async XLA Ops:
  8.0 29.1 %all-to-all-start = ((bf16[64,32,256]{2,1,0:T(8,128)(2,1)}), bf16[64,32,256]{2,1,0:T(8,128)(2,1)S(1)}, u32[]{:S(2)}, u32[]{:S(2)}) async-start(bf16[64,32,256]{2,1,0:T(8,128)(2,1)} %bitcast.19), calls=%async_computation | async-start | bytes 2097152 | tf_op jit(solution)/shard_map/all_to_all | solution.py:442
  37.1 5.7 %copy-start.5 = (s32[14336]{0:T(1024)S(1)}, s32[14336]{0:T(1024)}, u32[]{:S(2)}) copy-start(s32[14336]{0:T(1024)} %param.12) | copy-start | bytes 172036
  37.1 95.8 %all-to-all-start.1 = ((bf16[64,80,256]{2,1,0:T(8,128)(2,1)}), bf16[64,80,256]{2,1,0:T(8,128)(2,1)}, u32[]{:S(2)}, u32[]{:S(2)}) async-start(bf16[64,80,256]{2,1,0:T(8,128)(2,1)} %bitcast.14), calls=%async_computation.1 | async-start | bytes 5242880 | tf_op jit(solution)/shard_map/all_to_all | solution.py:443
  43.3 87.2 %copy-start.2 = (s32[64,256]{1,0:T(8,128)}, s32[64,256]{1,0:T(8,128)S(1)}, u32[]{:S(2)}) copy-start(s32[64,256]{1,0:T(8,128)S(1)} %pad.8.segments) | copy-start | bytes 196612
  130.5 1.0 copy-start
  131.5 0.8 copy-start.1
  132.4 0.6 copy-start.3
  253.0 25.3 %all-to-all-start.2 = ((bf16[64,32,224]{2,1,0:T(8,128)(2,1)}), bf16[64,32,224]{2,1,0:T(8,128)(2,1)S(1)}, u32[]{:S(2)}, u32[]{:S(2)}) async-start(bf16[64,32,224]{2,1,0:T(8,128)(2,1)} %relation_gradient.1), calls=%async_computation.2 | async-start | bytes 2097152 | tf_op jit(solution)/shard_map/all_to_all | solution.py:445
  278.3 2.8 copy-start.4
  281.9 6.6 %collective-permute-start = (f32[224,1024]{1,0:T(8,128)S(1)}, f32[224,1024]{1,0:T(8,128)S(1)}, u32[]{:S(2)}, u32[]{:S(2)}) collective-permute-start(f32[224,1024]{1,0:T(8,128)S(1)} %fusion.14), channel_id=1, source_target_pairs={{0,1},{1,0},{2,3},{3,2},{4,5},{5,4},{6,7},{7,6},{8,9},{9,8},{10,11... | collective-permute-start | bytes 2752520 | tf_op jit(solution)/shard_map/ppermute | solution.py:463

commit v3 on v1

--- a/solution.py
+++ b/solution.py
@@ -92,7 +92,7 @@
 
 
 def relation_kernel(
-    blocks, ends, x, out, xt, wt, ws, t_rings, s_rings, causal, sums, grad, seen, opened, pairs, sem
+    blocks, ends, x, out, xt, both, t_rings, s_rings, causal, sums, grad, seen, opened, pairs, sem
 ):
     rows = x.shape[1]
     wide = xt.shape[2]
@@ -149,8 +149,8 @@
         bias = jnp.where(is_seg, (values - 1.0) * HIDDEN, 0.0)
         teacher = jnp.where(feature < WT, values, 0.0)
         student = jnp.where((feature >= WT) & (feature < SEG0), values, 0.0)
-        wt[block] = (teacher + bias).astype(jnp.bfloat16)
-        ws[block] = (student + bias).astype(jnp.bfloat16)
+        both[block, :, :wide] = (teacher + bias).astype(jnp.bfloat16)
+        both[block, :, wide:] = (student + bias).astype(jnp.bfloat16)
         grad[block] = jnp.zeros((WS, wide), f32)
         return (
             jnp.maximum(peak_t, jnp.sum(teacher * teacher, axis=0, keepdims=True)),
@@ -170,8 +170,9 @@
     def _():
         def raise_maxima(place, carry):
             query, key, diagonal = entry(place + LAG)
-            for member, weights in enumerate((wt, ws)):
-                scores = jnp.dot(x[key], weights[query], preferred_element_type=f32)
+            for member in range(2):
+                columns = slice(member * wide, (member + 1) * wide)
+                scores = jnp.dot(x[key], both[query, :, columns], preferred_element_type=f32)
                 scores = scores + causal[diagonal]
                 top = jnp.max(scores.reshape(rows // 8, 8, wide), axis=0)
                 sums[query, member] = jnp.where(
@@ -183,15 +184,16 @@
         slab_row = lax.broadcasted_iota(jnp.int32, (SLAB - SEG0, wide), 0) + SEG0
 
         def set_maxima(block, carry):
-            for member, weights in enumerate((wt, ws)):
+            for member in range(2):
+                columns = slice(member * wide, (member + 1) * wide)
                 top = jnp.max(sums[block, member], axis=0, keepdims=True)
-                slab = weights[block, SEG0:].astype(f32)
+                slab = both[block, SEG0:, columns].astype(f32)
                 rest = top
                 for part in range(3):
                     piece = rest.astype(jnp.bfloat16).astype(f32)
                     rest = rest - piece
                     slab = jnp.where(slab_row == ONE0 + part, -piece, slab)
-                weights[block, SEG0:] = slab.astype(jnp.bfloat16)
+                both[block, SEG0:, columns] = slab.astype(jnp.bfloat16)
             return carry
 
         lax.fori_loop(0, blocks, set_maxima, 0)
@@ -206,8 +208,9 @@
         query, key, diagonal = entry(place + LAG)
         keys = x[readable(key)]
         hide = causal[diagonal]
-        for member, (weights, ring, scale) in enumerate(((wt, t_ring, SCALE_T), (ws, s_ring, SCALE_S))):
-            scores = jnp.dot(keys, weights[readable(query)], preferred_element_type=f32)
+        products = jnp.dot(keys, both[readable(query)], preferred_element_type=f32)
+        for member, (ring, scale) in enumerate(((t_ring, SCALE_T), (s_ring, SCALE_S))):
+            scores = products[:, member * wide : (member + 1) * wide]
             made = jnp.exp2(scores * scale + hide)
             ring[slot] = made
             part = jnp.sum(made.reshape(rows // 8, 8, wide), axis=0)
@@ -259,8 +262,7 @@
         out_specs=pl.BlockSpec(memory_space=pltpu.VMEM),
         scratch_shapes=[
             turned,
-            turned,
-            turned,
+            pltpu.VMEM((blocks, SLAB, 2 * wide), jnp.bfloat16),
             [ring] * UNROLL,
             [ring] * UNROLL,
             pltpu.VMEM((2, rows, wide), jnp.float32),

time: 246 us -> 252 us (1.024)
  Pallas kernels: 149 us -> 154 us
    pallas_call x1, Pallas kernels: 137 us -> 142 us  [relation(): pl.pallas_call(functools.partial(relation_kernel, blocks), out_shape=jax....]
where the time goes in v3:
time: 252 us; the launch traced here: 251 us
  Pallas kernels  154 us (61%)
  waiting for transfers between devices  59.7 us (24%)
  starting transfers between devices  23.4 us (9%)
  matrix products  9.07 us (4%)
    pallas_call x1, Pallas kernels, relation(): pl.pallas_call(functools.partial(relation_kernel, blocks), out_shape=jax....  142 us
    all_to_all x1, waiting for transfers between devices, shards(): row = lax.all_to_all(units, 'ctx', 0, 0, tiled=True)  43.4 us
    all_to_all x1, waiting for transfers between devices, shards(): back = lax.all_to_all(turned, 'ctx', 0, 0, tiled=True)  16.2 us
    all_to_all x1, starting transfers between devices, shards(): row = lax.all_to_all(units, 'ctx', 0, 0, tiled=True)  12.2 us
    pallas_call x1, Pallas kernels, pack(): pl.pallas_call(pack_kernel, grid=(heads // PACK,), out_shape=jax.ShapeDty...  12.2 us
    dot_general x4, matrix products, project(): lax.dot_general(grad, lax.dynamic_slice_in_dim(weight, part * width, widt...  9.07 us
    all_to_all x1, starting transfers between devices, shards(): back = lax.all_to_all(turned, 'ctx', 0, 0, tiled=True)  7.73 us
  transfers between devices with their start and end apart: 3, of which 2 were waited for; matrix products, arithmetic and copies ran while one was open for 2% of the time, Pallas kernels for 0%

profile of v3, /device:TPU:1, one launch (start us, length us, event | category | flops | bytes accessed | tf_op | source)
XLA Modules:
  0.0 250.9 jit_solution(7865052946670836845)
XLA Ops:
  0.0 0.7 convert_element_type.12
  0.7 0.1 pad_bitcast_fusion
  0.7 0.8 dynamic-slice_add_fusion
  1.5 0.7 convert_add_fusion.extra
  2.3 12.2 %project_and_pack.1 = bf16[2,32,224,128]{3,2,1,0:T(8,128)(2,1)} custom-call(bf16[224,2048]{1,0:T(8,128)(2,1)} %hidden.1, bf16[2048,1024]{1,0:T(8,128)(2,1)} %wq.1, bf16[2048,1024]{1,0:T(8,128)(2,1)} %wk.1, bf16[224,2560]{1,0:T(8,128)(2,1)} %tq.1, bf16[224,2560]{1,0:T(8,128)(2,1)} %tk.1, f32[224,128]{1,0:T(8,128)} %convert_add_fusion.extra), custom_call_target="tpu_custom_call" | custom-call | flops 3758096384 | bytes 16000000 | tf_op jit(solution)/shard_map/project_and_pack/pallas_call | solution.py:69
  14.5 12.2 %all-to-all-start = ((bf16[64,224,128]{2,1,0:T(8,128)(2,1)}), bf16[64,224,128]{2,1,0:T(8,128)(2,1)}, u32[]{:S(2)}, u32[]{:S(2)}) async-start(bf16[64,224,128]{2,1,0:T(8,128)(2,1)} %bitcast.11), calls=%async_computation | async-start | bytes 7340032 | tf_op jit(solution)/shard_map/all_to_all | solution.py:298
  26.7 1.0 slice.12
  27.6 1.0 slice.13
  28.6 43.4 %all-to-all-done.x = bf16[64,224,128]{2,1,0:T(8,128)(2,1)} async-done(((bf16[64,224,128]{2,1,0:T(8,128)(2,1)}), bf16[64,224,128]{2,1,0:T(8,128)(2,1)}, u32[]{:S(2)}, u32[]{:S(2)}) %all-to-all-start) | async-done | bytes 3670048 | tf_op jit(solution)/shard_map/all_to_all | solution.py:298
  72.0 142.1 %relation_gradient.1 = bf16[64,32,224]{2,1,0:T(8,128)(2,1)} custom-call(s32[2,64]{1,0:T(2,128)S(1)} %pad_add_fusion.ends, bf16[64,224,128]{2,1,0:T(8,128)(2,1)} %all-to-all-done.x), custom_call_target="tpu_custom_call" | custom-call | flops 20000000000 | bytes 5000000 | tf_op jit(solution)/shard_map/relation_gradient/pallas_call | solution.py:255
  214.1 7.7 %all-to-all-start.1 = ((bf16[64,32,224]{2,1,0:T(8,128)(2,1)}), bf16[64,32,224]{2,1,0:T(8,128)(2,1)S(1)}, u32[]{:S(2)}, u32[]{:S(2)}) async-start(bf16[64,32,224]{2,1,0:T(8,128)(2,1)} %relation_gradient.1), calls=%async_computation.1 | async-start | bytes 2097152 | tf_op jit(solution)/shard_map/all_to_all | solution.py:300
  221.9 16.2 %all-to-all-done.1 = bf16[64,32,224]{2,1,0:T(8,128)(2,1)S(1)} async-done(((bf16[64,32,224]{2,1,0:T(8,128)(2,1)}), bf16[64,32,224]{2,1,0:T(8,128)(2,1)S(1)}, u32[]{:S(2)}, u32[]{:S(2)}) %all-to-all-start.1) | async-done | bytes 917536 | tf_op jit(solution)/shard_map/all_to_all | solution.py:300
  238.1 0.0 copy-start
  238.1 0.1 fusion.25
  238.2 2.6 %fusion = f32[224,1024]{1,0:T(8,128)S(1)} fusion(bf16[1024,224]{1,0:T(8,128)(2,1)S(1)} %bitcast.14, bf16[2048,1024]{1,0:T(8,128)(2,1)} %wk.1, s32[]{:T(128)S(6)} %select_n.13), kind=kOutput, calls=%fused_computation | convolution fusion | flops 469762048 | bytes 3473412 | tf_op jit(solution)/shard_map/dot_general | solution.py:309
  240.7 0.2 copy-done
  240.9 0.8 fusion.14
  241.8 3.5 %collective-permute-start = (f32[224,1024]{1,0:T(8,128)S(1)}, f32[224,1024]{1,0:T(8,128)S(1)}, u32[]{:S(2)}, u32[]{:S(2)}) collective-permute-start(f32[224,1024]{1,0:T(8,128)S(1)} %fusion.14), channel_id=1, source_target_pairs={{0,1},{1,0},{2,3},{3,2},{4,5},{5,4},{6,7},{7,6},{8,9},{9,8},{10,11... | collective-permute-start | bytes 2752520 | tf_op jit(solution)/shard_map/ppermute | solution.py:318
  245.3 2.4 fusion.4
  247.7 0.0 collective-permute-done
  247.7 3.2 %fusion.17 = bf16[224,1024]{1,0:T(8,128)(2,1)} fusion(f32[224,1024]{1,0:T(8,128)S(1)} %collective-permute-done, f32[224,1024]{1,0:T(8,128)S(1)} %fusion.4, bf16[1024,224]{1,0:T(8,128)(2,1)S(1)} %bitcast.13, bf16[2048,1024]{1,0:T(8,128)(2,1)} %wq.1, s32[]{:T(128)S(6)} %select_n.12), kind=kOutput, calls=%fused_computation.11 | convolution fusion | flops 470450176 | bytes 4849668 | tf_op jit(solution)/shard_map/dot_general | solution.py:309
  (2 shorter events, 0.0 us)
Async XLA Ops:
  14.5 57.6 %all-to-all-start = ((bf16[64,224,128]{2,1,0:T(8,128)(2,1)}), bf16[64,224,128]{2,1,0:T(8,128)(2,1)}, u32[]{:S(2)}, u32[]{:S(2)}) async-start(bf16[64,224,128]{2,1,0:T(8,128)(2,1)} %bitcast.11), calls=%async_computation | async-start | bytes 7340032 | tf_op jit(solution)/shard_map/all_to_all | solution.py:298
  214.1 24.0 %all-to-all-start.1 = ((bf16[64,32,224]{2,1,0:T(8,128)(2,1)}), bf16[64,32,224]{2,1,0:T(8,128)(2,1)S(1)}, u32[]{:S(2)}, u32[]{:S(2)}) async-start(bf16[64,32,224]{2,1,0:T(8,128)(2,1)} %relation_gradient.1), calls=%async_computation.1 | async-start | bytes 2097152 | tf_op jit(solution)/shard_map/all_to_all | solution.py:300
  238.1 2.8 %copy-start = (bf16[2048,1024]{1,0:T(8,128)(2,1)S(1)}, bf16[2048,1024]{1,0:T(8,128)(2,1)}, u32[]{:S(2)}) copy-start(bf16[2048,1024]{1,0:T(8,128)(2,1)} %wq.1) | copy-start | bytes 12582916
  241.8 5.9 %collective-permute-start = (f32[224,1024]{1,0:T(8,128)S(1)}, f32[224,1024]{1,0:T(8,128)S(1)}, u32[]{:S(2)}, u32[]{:S(2)}) collective-permute-start(f32[224,1024]{1,0:T(8,128)S(1)} %fusion.14), channel_id=1, source_target_pairs={{0,1},{1,0},{2,3},{3,2},{4,5},{5,4},{6,7},{7,6},{8,9},{9,8},{10,11... | collective-permute-start | bytes 2752520 | tf_op jit(solution)/shard_map/ppermute | solution.py:318

commit v4 on v2

v4 whole, which is shorter than its diff:
```python
import functools
import math

import jax
import jax.numpy as jnp
from jax import lax
from jax.experimental import pallas as pl
from jax.experimental.pallas import tpu as pltpu
from jax.sharding import PartitionSpec as P

DT = 5120
DS = 2048
HEADS = 64
REACH = 8
WT = DT // HEADS
WS = DS // HEADS
DEPTH = 128
EXTRA = 16
DOCS = 4
PACK = 8
LISTED = 8
UNROLL = 4
LAG = 3 * UNROLL
SLOTS = 4
AHEAD = 2
LIST = 640
HIDDEN = 1e30
LOG2E = math.log2(math.e)
SCALE_T = LOG2E / math.sqrt(WT)
SCALE_S = LOG2E / math.sqrt(WS)
SAFE = 90.0
MIB = 1024 * 1024
f32 = jnp.float32
bf16 = jnp.bfloat16


def round_up(value, unit):
    return (value + unit - 1) // unit * unit


def project_kernel(mask, hidden, wq, wk, out):
    rows, wide = hidden.shape[0], out.shape[-1]
    row = lax.broadcasted_iota(jnp.int32, (wide - rows, PACK * WS), 0)
    extra = jnp.zeros(row.shape, f32)
    for back in range(REACH - 1):
        extra = jnp.where(row == back, mask[0, back].astype(f32), extra)
    extra = extra.astype(bf16)
    for rel, weight in enumerate((wq, wk)):
        student = jnp.dot(hidden[...], weight[...], preferred_element_type=f32).astype(bf16)
        turned = jnp.concatenate([student, extra], axis=0).T
        out[rel] = turned.reshape(out.shape[1:])


def project(hidden, wq, wk, mask):
    rows = hidden.shape[0]
    wide = round_up(rows, 128)
    heads = wq.shape[1] // WS
    return pl.pallas_call(
        project_kernel,
        grid=(heads // PACK,),
        out_shape=jax.ShapeDtypeStruct((2, heads, WS, wide), bf16),
        in_specs=[
            pl.BlockSpec(memory_space=pltpu.SMEM),
            pl.BlockSpec((rows, DS), lambda i: (0, 0)),
            pl.BlockSpec((DS, PACK * WS), lambda i: (0, i)),
            pl.BlockSpec((DS, PACK * WS), lambda i: (0, i)),
        ],
        out_specs=pl.BlockSpec((2, PACK, WS, wide), lambda i: (0, i, 0, 0)),
        compiler_params=pltpu.CompilerParams(vmem_limit_bytes=56 * MIB),
        cost_estimate=pl.CostEstimate(
            flops=4 * rows * DS * heads * WS, bytes_accessed=10_000_000, transcendentals=0
        ),
        name="project_student",
    )(mask, hidden, wq, wk)


def turn_kernel(tq, tk, out):
    rows = tq.shape[0]
    wide = out.shape[-1]
    for rel, teacher in enumerate((tq, tk)):
        zeros = jnp.zeros((wide - rows, teacher.shape[1]), bf16)
        turned = jnp.concatenate([teacher[...], zeros], axis=0).T
        out[rel] = turned.reshape(out.shape[1:])


def turn(tq, tk):
    rows, columns = tq.shape
    wide = round_up(rows, 128)
    heads = columns // WT
    return pl.pallas_call(
        turn_kernel,
        grid=(heads // PACK,),
        out_shape=jax.ShapeDtypeStruct((2, heads, WT, wide), bf16),
        in_specs=[pl.BlockSpec((rows, PACK * WT), lambda i: (0, i))] * 2,
        out_specs=pl.BlockSpec((2, PACK, WT, wide), lambda i: (0, i, 0, 0)),
        compiler_params=pltpu.CompilerParams(vmem_limit_bytes=56 * MIB),
        cost_estimate=pl.CostEstimate(flops=0, bytes_accessed=5_000_000, transcendentals=0),
        name="turn_teacher",
    )(tq, tk)


def read_pair(pairs, place):
    code = pairs[place]
    return code & 255, (code >> 8) & 255, code >> 16


def fill(block, slab, segments, keys, weights):
    width, wide = slab.shape
    rows = keys.shape[1]
    row = lax.broadcasted_iota(jnp.int32, (EXTRA, wide), 0)
    lane = lax.broadcasted_iota(jnp.int32, (EXTRA, wide), 1)
    hot = jnp.where(row == segments[pl.ds(block, 1)], 1.0, 0.0)
    key_extra = jnp.where((row >= DOCS) & (row < DOCS + 3), 1.0, hot)
    query_extra = jnp.where((row < DOCS) & (lane < rows), (hot - 1.0) * HIDDEN, 0.0)
    zeros = jnp.zeros((DEPTH - EXTRA - width, wide), bf16)
    weights[block] = jnp.concatenate([slab, query_extra.astype(bf16), zeros], axis=0)
    keys[block] = jnp.concatenate([slab, key_extra.astype(bf16), zeros], axis=0).T[:rows]
    values = slab.astype(f32)
    return jnp.sum(values * values, axis=0, keepdims=True)


def subtract_maxima(width, blocks, count, pairs, keys, weights, causal, sums):
    rows, wide = causal.shape[1:]

    def raise_maxima(place, carry):
        query, key, diagonal = read_pair(pairs, place + LAG)
        scores = jnp.dot(keys[key], weights[query], preferred_element_type=f32)
        scores = scores + causal[diagonal]
        top = jnp.max(scores.reshape(rows // 8, 8, wide), axis=0)
        sums[query] = jnp.where(diagonal == 1, top, jnp.maximum(top, sums[query]))
        return carry

    lax.fori_loop(0, count, raise_maxima, 0)
    row = lax.broadcasted_iota(jnp.int32, (EXTRA, wide), 0)

    def set_maxima(block, carry):
        rest = jnp.max(sums[block], axis=0, keepdims=True)
        extra = weights[block, width : width + EXTRA].astype(f32)
        for part in range(3):
            piece = rest.astype(bf16).astype(f32)
            rest = rest - piece
            extra = jnp.where(row == DOCS + part, -piece, extra)
        weights[block, width : width + EXTRA] = extra.astype(bf16)
        return carry

    lax.fori_loop(0, blocks, set_maxima, 0)


def fill_causal(causal):
    shape = causal.shape[1:]
    key_at = lax.broadcasted_iota(jnp.int32, shape, 0)
    query_at = lax.broadcasted_iota(jnp.int32, shape, 1)
    causal[0] = jnp.zeros(shape, f32)
    causal[1] = jnp.where(key_at <= query_at, 0.0, -HIDDEN)


def weigh(place, blocks, pairs, keys, weights, scale, causal, ring, slot, sums):
    query, key, diagonal = read_pair(pairs, place + LAG)
    rows, wide = causal.shape[1:]
    scores = jnp.dot(
        keys[jnp.minimum(key, blocks - 1)],
        weights[jnp.minimum(query, blocks - 1)],
        preferred_element_type=f32,
    )
    made = jnp.exp2(scores * scale + causal[diagonal])
    ring[slot] = made
    part = jnp.sum(made.reshape(rows // 8, 8, wide), axis=0)
    sums[query] = jnp.where(diagonal == 1, part, part + sums[query])


def student_kernel(
    blocks, ends, segments, slabs, made, scales, features, pairs, count_out, keys, weights, rings, causal, sums, seen, opened, sem, sems
):
    rows, wide = causal.shape[1:]
    fill_causal(causal)

    def look(block, carry):
        seen[pl.ds(block, 1)] = slabs[block, :16, wide - 128 :].astype(f32)[:1].astype(jnp.int32)
        return carry

    lax.fori_loop(0, blocks, look, 0, unroll=8)
    fetch = pltpu.make_async_copy(seen, opened, sem)
    fetch.start()
    fetch.wait()
    mask_lane = rows % 128

    def list_pairs(block, total):
        for back in range(REACH):
            key = jnp.maximum(block - back, 0)
            code = block | (key << 8)
            if back == 0:
                pairs[total + LAG] = code | (1 << 16)
                total = total + 1
            else:
                pairs[total + LAG] = code
                is_open = (block >= back) & (opened[block, mask_lane + back - 1] == 1)
                is_open = is_open & (ends[0, block] == ends[1, key])
                total = total + is_open.astype(jnp.int32)
        return total

    lane = lax.broadcasted_iota(jnp.int32, (WS, wide), 1)

    def prepare(block, carry):
        peak, total = carry
        total = list_pairs(block, total)
        slab = jnp.where(lane < rows, slabs[block].astype(f32), 0.0).astype(bf16)
        features[block] = slab
        return jnp.maximum(peak, fill(block, slab, segments, keys, weights)), total

    peak, count = lax.fori_loop(0, blocks, prepare, (jnp.zeros((1, wide), f32), 0), unroll=4)
    count_out[0] = count
    for place in range(LAG):
        pairs[place] = blocks | (blocks << 8)
    for place in range(LAG + LISTED):
        pairs[count + LAG + place] = blocks | (blocks << 8)

    @pl.when(jnp.logical_not(jnp.max(peak) * SCALE_S <= SAFE))
    def _():
        subtract_maxima(WS, blocks, count, pairs, keys, weights, causal, sums)

    def send(place, step, slot):
        return pltpu.make_async_copy(rings[step].at[slot], made.at[place], sems.at[step, slot])

    def steps(turn, carry):
        slot = turn & (SLOTS - 1)

        @pl.when(turn >= SLOTS)
        def _():
            for step in range(LISTED):
                send(LISTED * turn + step, step, slot).wait()

        for step in range(LISTED):
            place = LISTED * turn + step
            weigh(place, blocks, pairs, keys, weights, SCALE_S, causal, rings[step], slot, sums)
        for step in range(LISTED):
            send(LISTED * turn + step, step, slot).start()
        return carry

    turns = (count + LISTED - 1) // LISTED
    lax.fori_loop(0, turns, steps, 0)

    def drain(turn, carry):
        for step in range(LISTED):
            send(LISTED * turn + step, step, turn & (SLOTS - 1)).wait()
        return carry

    lax.fori_loop(jnp.maximum(turns - SLOTS, 0), turns, drain, 0)

    def finish(block, carry):
        total = jnp.sum(sums[block], axis=0, keepdims=True) * math.sqrt(WS)
        scales[block] = jnp.broadcast_to(1.0 / total, (8, wide))
        return carry

    lax.fori_loop(0, blocks, finish, 0, unroll=8)


def student_weights(slabs, ends, segments, rows):
    blocks, _, wide = slabs.shape
    vmem = pl.BlockSpec(memory_space=pltpu.VMEM)
    smem = pl.BlockSpec(memory_space=pltpu.SMEM)
    ring = pltpu.VMEM((SLOTS, rows, wide), f32)
    return pl.pallas_call(
        functools.partial(student_kernel, blocks),
        out_shape=(
            jax.ShapeDtypeStruct((blocks * REACH, rows, wide), f32),
            jax.ShapeDtypeStruct((blocks, 8, wide), f32),
            jax.ShapeDtypeStruct((blocks, WS, wide), bf16),
            jax.ShapeDtypeStruct((LIST,), jnp.int32),
            jax.ShapeDtypeStruct((1,), jnp.int32),
        ),
        in_specs=[smem, vmem, vmem],
        out_specs=(pl.BlockSpec(memory_space=pl.ANY), vmem, vmem, smem, smem),
        scratch_shapes=[
            pltpu.VMEM((blocks, rows, DEPTH), bf16),
            pltpu.VMEM((blocks, DEPTH, wide), bf16),
            [ring] * LISTED,
            pltpu.VMEM((2, rows, wide), f32),
            pltpu.VMEM((blocks + 1, 8, wide), f32),
            pltpu.VMEM((blocks, 128), jnp.int32),
            pltpu.SMEM((blocks, 128), jnp.int32),
            pltpu.SemaphoreType.DMA,
            pltpu.SemaphoreType.DMA((LISTED, SLOTS)),
        ],
        compiler_params=pltpu.CompilerParams(vmem_limit_bytes=48 * MIB),
        cost_estimate=pl.CostEstimate(
            flops=10_000_000_000, bytes_accessed=80_000_000, transcendentals=20_000_000
        ),
        name="student_weights",
    )(ends, segments, slabs)


def gradient_kernel(
    blocks, count_in, pairs, segments, slabs, made, scales, features, out, keys, weights, rings, fetched, causal, sums, grad, sems
):
    rows, wide = causal.shape[1:]
    count = count_in[0]
    fill_causal(causal)

    def fetch(turn, step):
        pair = jnp.clip(UNROLL * turn + step - LAG, 0, made.shape[0] - 1)
        slot = turn & (SLOTS - 1)
        return pltpu.make_async_copy(made.at[pair], fetched[step].at[slot], sems.at[step, slot])

    for turn in range(AHEAD):
        for step in range(UNROLL):
            fetch(turn, step).start()

    def prepare(block, peak):
        grad[block] = jnp.zeros((WS, wide), f32)
        return jnp.maximum(peak, fill(block, slabs[block], segments, keys, weights))

    peak = lax.fori_loop(0, blocks, prepare, jnp.zeros((1, wide), f32), unroll=4)

    @pl.when(jnp.logical_not(jnp.max(peak) * SCALE_T <= SAFE))
    def _():
        subtract_maxima(WT, blocks, count, pairs, keys, weights, causal, sums)

    def readable(block):
        return jnp.minimum(block, blocks - 1)

    def inverses(place):
        query, _, _ = read_pair(pairs, place)
        total = jnp.sum(sums[query], axis=0, keepdims=True) * math.sqrt(WS)
        return 1.0 / total, scales[readable(query), :1]

    def couple(place, teacher, student, scale):
        query, key, _ = read_pair(pairs, place)
        coupling = (student * scale[1] - teacher * scale[0]).astype(bf16)
        query_side = features[readable(query)]
        key_side = features[readable(key), :, :rows]
        grad[key, :, :rows] += lax.dot_general(
            query_side, coupling, (((1,), (1,)), ((), ())), preferred_element_type=f32
        )
        grad[query] += jnp.dot(key_side, coupling, preferred_element_type=f32)

    def half(turn, parity):
        slot = turn & (SLOTS - 1)
        for step in range(UNROLL):
            fetch(turn, step).wait()
        for step in range(UNROLL):
            fetch(turn + AHEAD, step).start()
        scale = [inverses(UNROLL * turn + step) for step in range(UNROLL)]
        now = turn // 2 & 1
        before = (turn - LAG // UNROLL) // 2 & 1
        for step in range(UNROLL):
            place = UNROLL * turn + step
            old = rings[1 - parity][step][before]
            couple(place, old, fetched[step][slot], scale[step])
            ring = rings[parity][step]
            weigh(place, blocks, pairs, keys, weights, SCALE_T, causal, ring, now, sums)

    def steps(turn, carry):
        for parity in range(2):
            pl.when(turn & 1 == parity)(functools.partial(half, turn, parity))
        return carry

    turns = (count + LAG + UNROLL - 1) // UNROLL
    lax.fori_loop(0, turns, steps, 0)
    for turn in range(AHEAD):
        for step in range(UNROLL):
            fetch(turns + turn, step).wait()

    def finish(block, carry):
        out[block] = grad[block, :, :rows].astype(bf16)
        return carry

    lax.fori_loop(0, blocks, finish, 0, unroll=8)


def relation_gradient(slabs, segments, made, scales, features, pairs, count):
    blocks, _, wide = slabs.shape
    rows = made.shape[1]
    vmem = pl.BlockSpec(memory_space=pltpu.VMEM)
    smem = pl.BlockSpec(memory_space=pltpu.SMEM)
    ring = pltpu.VMEM((SLOTS, rows, wide), f32)
    return pl.pallas_call(
        functools.partial(gradient_kernel, blocks),
        out_shape=jax.ShapeDtypeStruct((blocks, WS, rows), bf16),
        in_specs=[smem, smem, vmem, vmem, pl.BlockSpec(memory_space=pl.ANY), vmem, vmem],
        out_specs=vmem,
        scratch_shapes=[
            pltpu.VMEM((blocks, rows, DEPTH), bf16),
            pltpu.VMEM((blocks, DEPTH, wide), bf16),
            [[pltpu.VMEM((2, rows, wide), f32)] * UNROLL] * 2,
            [ring] * UNROLL,
            pltpu.VMEM((2, rows, wide), f32),
            pltpu.VMEM((blocks + 1, 8, wide), f32),
            pltpu.VMEM((blocks + 1, WS, wide), f32),
            pltpu.SemaphoreType.DMA((UNROLL, SLOTS)),
        ],
        compiler_params=pltpu.CompilerParams(vmem_limit_bytes=48 * MIB),
        cost_estimate=pl.CostEstimate(
            flops=20_000_000_000, bytes_accessed=80_000_000, transcendentals=20_000_000
        ),
        name="relation_gradient",
    )(count, pairs, segments, slabs, made, scales, features)


def head_gradient(student, teacher, segment_ids, rows):
    blocks, _, wide = student.shape
    ends = jnp.stack([segment_ids[::rows], segment_ids[rows - 1 :: rows]])
    segments = jnp.pad(
        segment_ids.reshape(blocks, rows), ((0, 0), (0, wide - rows)), constant_values=-1
    )
    made, scales, features, pairs, count = student_weights(student, ends, segments, rows)
    return relation_gradient(teacher, segments, made, scales, features, pairs, count)


def unproject_kernel(part, grads, wq, wk, out):
    half = grads.shape[0] // 2
    rows, wide = grads.shape[2], round_up(grads.shape[2], 128)
    total = jnp.zeros((wq.shape[0], wide), f32)
    for rel, weight in enumerate((wq, wk)):
        turned = grads[rel * half : (rel + 1) * half].reshape(half * WS, rows)
        turned = jnp.concatenate([turned, jnp.zeros((half * WS, wide - rows), bf16)], axis=1)
        total += jnp.dot(weight[...], turned, preferred_element_type=f32)
    out[...] = total.T[:rows].astype(out.dtype)


def unproject(part, grads, wq, wk, dtype):
    rows = grads.shape[2]
    width = wq.shape[0] // 2
    tile = 256
    steps = width // tile

    def weight_block(i, part):
        return part[0] * steps + i, 0

    weight = pl.BlockSpec((tile, wq.shape[1]), weight_block)
    return pl.pallas_call(
        unproject_kernel,
        grid_spec=pltpu.PrefetchScalarGridSpec(
            num_scalar_prefetch=1,
            grid=(steps,),
            in_specs=[pl.BlockSpec(grads.shape, lambda i, part: (0, 0, 0)), weight, weight],
            out_specs=pl.BlockSpec((rows, tile), lambda i, part: (0, i)),
        ),
        out_shape=jax.ShapeDtypeStruct((rows, width), dtype),
        compiler_params=pltpu.CompilerParams(vmem_limit_bytes=56 * MIB),
        cost_estimate=pl.CostEstimate(
            flops=4 * rows * width * wq.shape[1], bytes_accessed=6_000_000, transcendentals=0
        ),
        name="unproject",
    )(part[None], grads, wq, wk)


def shards(teacher_query, teacher_key, student_hidden, w_query, w_key, segment_ids, block_mask):
    rows = student_hidden.shape[0]
    student = project(student_hidden, w_query, w_key, block_mask)
    teacher = turn(teacher_query, teacher_key)
    student = lax.all_to_all(student.reshape(-1, *student.shape[2:]), "ctx", 0, 0, tiled=True)
    teacher = lax.all_to_all(teacher.reshape(-1, *teacher.shape[2:]), "ctx", 0, 0, tiled=True)
    turned = head_gradient(student, teacher, segment_ids, rows)
    back = lax.all_to_all(turned, "ctx", 0, 0, tiled=True)
    side = lax.axis_index("head")
    away = unproject(1 - side, back, w_query, w_key, bf16)
    away = lax.ppermute(away, "head", [(0, 1), (1, 0)])
    own = unproject(side, back, w_query, w_key, f32)
    return (own + away).astype(bf16)


def solution(mesh):
    placed = (
        P("ctx", "head"),
        P("ctx", "head"),
        P("ctx", None),
        P(None, "head"),
        P(None, "head"),
        P(),
        P("ctx", None),
    )
    return jax.shard_map(
        shards, mesh=mesh, in_specs=placed, out_specs=P("ctx", "head"), check_vma=False
    )
```

time: 291 us -> 295 us (1.014)
  matrix products: 9.06 us -> 0 us
  Pallas kernels: 218 us -> 227 us
  local copies, waits for them, and re-layouts: 3.74 us -> 6.74 us
    pallas_call x0 -> x2, Pallas kernels: none -> 10.4 us  [unproject(): pl.pallas_call(unproject_kernel, grid_spec=pltpu.PrefetchScalarGridSpec(n...]
    dot_general x4 -> x0, matrix products: 9.06 us -> none  [unproject(): lax.dot_general(grad, lax.dynamic_slice_in_dim(weight, part * width, widt...]
    pallas_call x1, Pallas kernels: 120 us -> 115 us  [relation_gradient(): pl.pallas_call(functools.partial(gradient_kernel, blocks), out_shape=jax....]
    unnamed x12 -> x14, local copies, waits for them, and re-layouts: 2.58 us -> 6.35 us
  transfers between devices with their start and end apart: 4 -> 4, of which waited for: 2 -> 2; matrix products, arithmetic and copies ran while one was open for 1% -> 0% of each run, Pallas kernels for 31% -> 34%
where the time goes in v4:
time: 295 us
  Pallas kernels  227 us (77%)
  starting transfers between devices  30.8 us (10%)
  waiting for transfers between devices  28.6 us (10%)
  local copies, waits for them, and re-layouts  6.74 us (2%)
    pallas_call x1, Pallas kernels, relation_gradient(): pl.pallas_call(functools.partial(gradient_kernel, blocks), out_shape=jax....  115 us
    pallas_call x1, Pallas kernels, student_weights(): pl.pallas_call(functools.partial(student_kernel, blocks), out_shape=(jax....  90 us
    all_to_all x1, waiting for transfers between devices, shards(): back = lax.all_to_all(turned, 'ctx', 0, 0, tiled=True)  15.7 us
    all_to_all x1, waiting for transfers between devices, shards(): lax.all_to_all(student.reshape(-1, *student.shape[2:]), 'ctx', 0, 0, tile...  12.8 us
    all_to_all x1, starting transfers between devices, shards(): lax.all_to_all(student.reshape(-1, *student.shape[2:]), 'ctx', 0, 0, tile...  12 us
    pallas_call x2, Pallas kernels, unproject(): pl.pallas_call(unproject_kernel, grid_spec=pltpu.PrefetchScalarGridSpec(n...  10.4 us
    all_to_all x1, starting transfers between devices, shards(): back = lax.all_to_all(turned, 'ctx', 0, 0, tiled=True)  9.78 us
    pallas_call x1, Pallas kernels, project(): pl.pallas_call(project_kernel, grid=(heads // PACK,), out_shape=jax.Shape...  6.66 us
  transfers between devices with their start and end apart: 4, of which 2 were waited for; matrix products, arithmetic and copies ran while one was open for 0% of the time, Pallas kernels for 34%

profile of v4, /device:TPU:1, one launch (start us, length us, event | category | flops | bytes accessed | tf_op | source)
XLA Modules:
  0.0 294.9 jit_solution(14436635083971818128)
XLA Ops:
  0.0 6.7 %project_student.1 = bf16[2,32,32,256]{3,2,1,0:T(8,128)(2,1)} custom-call(s32[1,7]{1,0:T(1,128)} %mask.1, bf16[224,2048]{1,0:T(8,128)(2,1)} %hidden.1, bf16[2048,1024]{1,0:T(8,128)(2,1)} %wq.5, bf16[2048,1024]{1,0:T(8,128)(2,1)} %wk.5), custom_call_target="tpu_custom_call" | custom-call | flops 1879048192 | bytes 10000000 | tf_op jit(solution)/shard_map/project_student/pallas_call | solution.py:58
  6.7 12.0 %all-to-all-start = ((bf16[64,32,256]{2,1,0:T(8,128)(2,1)}), bf16[64,32,256]{2,1,0:T(8,128)(2,1)S(1)}, u32[]{:S(2)}, u32[]{:S(2)}) async-start(bf16[64,32,256]{2,1,0:T(8,128)(2,1)} %bitcast.7), calls=%async_computation | async-start | bytes 2097152 | tf_op jit(solution)/shard_map/all_to_all | solution.py:451
  18.6 4.3 %turn_teacher.1 = bf16[2,32,80,256]{3,2,1,0:T(8,128)(2,1)} custom-call(bf16[224,2560]{1,0:T(8,128)(2,1)} %tq.1, bf16[224,2560]{1,0:T(8,128)(2,1)} %tk.1), custom_call_target="tpu_custom_call" | custom-call | bytes 5000000 | tf_op jit(solution)/shard_map/turn_teacher/pallas_call | solution.py:90
  23.0 12.8 %all-to-all-done.slabs = bf16[64,32,256]{2,1,0:T(8,128)(2,1)S(1)} async-done(((bf16[64,32,256]{2,1,0:T(8,128)(2,1)}), bf16[64,32,256]{2,1,0:T(8,128)(2,1)S(1)}, u32[]{:S(2)}, u32[]{:S(2)}) %all-to-all-start) | async-done | bytes 1048608 | tf_op jit(solution)/shard_map/all_to_all | solution.py:451
  35.8 0.0 copy-start.3
  35.8 1.0 copy-done.3
  36.8 0.0 copy-start.6
  36.8 5.2 %all-to-all-start.1 = ((bf16[64,80,256]{2,1,0:T(8,128)(2,1)}), bf16[64,80,256]{2,1,0:T(8,128)(2,1)S(1)}, u32[]{:S(2)}, u32[]{:S(2)}) async-start(bf16[64,80,256]{2,1,0:T(8,128)(2,1)} %bitcast.6), calls=%async_computation.1 | async-start | bytes 5242880 | tf_op jit(solution)/shard_map/all_to_all | solution.py:452
  42.0 0.0 copy-done.6
  42.0 0.1 slice.6
  42.1 0.2 slice.7
  42.3 0.1 reshape.9
  42.4 0.0 copy-start.4
  42.4 1.2 copy-done.4
  43.6 90.0 %student_weights.1 = (f32[512,224,256]{2,1,0:T(8,128)}, f32[64,8,256]{2,1,0:T(8,128)S(1)}, bf16[64,32,256]{2,1,0:T(8,128)(2,1)S(1)}, s32[640]{0:T(1024)S(1)}, s32[1]{0:T(128)}) custom-call(s32[2,64]{1,0:T(2,128)S(1)} %pad_add_fusion.ends, s32[64,256]{1,0:T(8,128)S(1)} %pad.4.segments, bf16[64,32,256]{2,1,0:T(8,128)(2,1)S(1)} %copy-done.4), custom_call_target="tpu_custom_call" | custom-call | flops 10000000000 | bytes 80000000 | tf_op jit(solution)/shard_map/student_weights/pallas_call | solution.py:262
  133.6 0.0 copy-start.1
  133.6 1.0 copy-done.1
  134.6 0.0 all-to-all-done.1.slabs
  134.6 0.0 copy-start.2
  134.6 1.2 copy-done.2
  135.8 115.2 %relation_gradient.1 = bf16[64,32,224]{2,1,0:T(8,128)(2,1)S(1)} custom-call(s32[1]{0:T(128)} %get-tuple-element.10.count_in, s32[640]{0:T(1024)S(1)} %get-tuple-element.11.pairs, s32[64,256]{1,0:T(8,128)S(1)} %pad.4.segments, bf16[64,80,256]{2,1,0:T(8,128)(2,1)S(1)} %all-to-all-done.1.slabs, f32[512,224,256]{2,1,0:T(8,128)} %get-tuple-element.12.made, ...), custom_call_target="tpu_custom_call" | custom-call | flops 20000000000 | bytes 80000000 | tf_op jit(solution)/shard_map/relation_gradient/pallas_call | solution.py:376
  251.1 0.0 copy-start
  251.1 1.0 copy-done
  252.0 9.8 %all-to-all-start.2 = ((bf16[64,32,224]{2,1,0:T(8,128)(2,1)}), bf16[64,32,224]{2,1,0:T(8,128)(2,1)S(1)}, u32[]{:S(2)}, u32[]{:S(2)}) async-start(bf16[64,32,224]{2,1,0:T(8,128)(2,1)} %copy-done), calls=%async_computation.2 | async-start | bytes 2097152 | tf_op jit(solution)/shard_map/all_to_all | solution.py:454
  261.8 15.7 %all-to-all-done.2.grads = bf16[64,32,224]{2,1,0:T(8,128)(2,1)S(1)} async-done(((bf16[64,32,224]{2,1,0:T(8,128)(2,1)}), bf16[64,32,224]{2,1,0:T(8,128)(2,1)S(1)}, u32[]{:S(2)}, u32[]{:S(2)}) %all-to-all-start.2) | async-done | bytes 917536 | tf_op jit(solution)/shard_map/all_to_all | solution.py:454
  277.6 0.0 copy-start.5
  277.6 1.0 copy-done.5
  278.6 5.1 %unproject.3 = bf16[224,1024]{1,0:T(8,128)(2,1)} custom-call(s32[1]{0:T(128)} %bitcast.5.part, bf16[64,32,224]{2,1,0:T(8,128)(2,1)} %copy-done.5, bf16[2048,1024]{1,0:T(8,128)(2,1)} %wq.5, bf16[2048,1024]{1,0:T(8,128)(2,1)} %wk.5), custom_call_target="tpu_custom_call" | custom-call | flops 939524096 | bytes 6000000 | tf_op jit(solution)/shard_map/unproject/pallas_call | solution.py:430
  283.7 3.9 %collective-permute-start = (bf16[224,1024]{1,0:T(8,128)(2,1)}, bf16[224,1024]{1,0:T(8,128)(2,1)S(1)}, u32[]{:S(2)}, u32[]{:S(2)}) collective-permute-start(bf16[224,1024]{1,0:T(8,128)(2,1)} %unproject.3), channel_id=1, source_target_pairs={{0,1},{1,0},{2,3},{3,2},{4,5},{5,4},{6,7},{7,6},{8,9},{9,8},{10,11... | collective-permute-start | bytes 1376264 | tf_op jit(solution)/shard_map/ppermute | solution.py:457
  287.6 5.3 %unproject.2 = f32[224,1024]{1,0:T(8,128)} custom-call(s32[1]{0:T(128)} %bitcast.part, bf16[64,32,224]{2,1,0:T(8,128)(2,1)} %copy-done.5, bf16[2048,1024]{1,0:T(8,128)(2,1)} %wq.5, bf16[2048,1024]{1,0:T(8,128)(2,1)} %wk.5), custom_call_target="tpu_custom_call" | custom-call | flops 939524096 | bytes 6000000 | tf_op jit(solution)/shard_map/unproject/pallas_call | solution.py:430
  292.9 0.0 collective-permute-done
  292.9 2.1 add_convert_fusion
  (2 shorter events, 0.0 us)
Async XLA Ops:
  6.7 29.1 %all-to-all-start = ((bf16[64,32,256]{2,1,0:T(8,128)(2,1)}), bf16[64,32,256]{2,1,0:T(8,128)(2,1)S(1)}, u32[]{:S(2)}, u32[]{:S(2)}) async-start(bf16[64,32,256]{2,1,0:T(8,128)(2,1)} %bitcast.7), calls=%async_computation | async-start | bytes 2097152 | tf_op jit(solution)/shard_map/all_to_all | solution.py:451
  35.8 1.0 copy-start.3
  36.8 5.2 %copy-start.6 = (s32[14336]{0:T(1024)S(1)}, s32[14336]{0:T(1024)}, u32[]{:S(2)}) copy-start(s32[14336]{0:T(1024)} %param.12) | copy-start | bytes 172036
  36.8 97.8 %all-to-all-start.1 = ((bf16[64,80,256]{2,1,0:T(8,128)(2,1)}), bf16[64,80,256]{2,1,0:T(8,128)(2,1)S(1)}, u32[]{:S(2)}, u32[]{:S(2)}) async-start(bf16[64,80,256]{2,1,0:T(8,128)(2,1)} %bitcast.6), calls=%async_computation.1 | async-start | bytes 5242880 | tf_op jit(solution)/shard_map/all_to_all | solution.py:452
  42.4 1.2 copy-start.4
  133.6 1.0 copy-start.1
  134.6 1.2 copy-start.2
  251.1 1.0 copy-start
  252.0 25.5 %all-to-all-start.2 = ((bf16[64,32,224]{2,1,0:T(8,128)(2,1)}), bf16[64,32,224]{2,1,0:T(8,128)(2,1)S(1)}, u32[]{:S(2)}, u32[]{:S(2)}) async-start(bf16[64,32,224]{2,1,0:T(8,128)(2,1)} %copy-done), calls=%async_computation.2 | async-start | bytes 2097152 | tf_op jit(solution)/shard_map/all_to_all | solution.py:454
  277.6 1.0 copy-start.5
  283.7 9.2 %collective-permute-start = (bf16[224,1024]{1,0:T(8,128)(2,1)}, bf16[224,1024]{1,0:T(8,128)(2,1)S(1)}, u32[]{:S(2)}, u32[]{:S(2)}) collective-permute-start(bf16[224,1024]{1,0:T(8,128)(2,1)} %unproject.3), channel_id=1, source_target_pairs={{0,1},{1,0},{2,3},{3,2},{4,5},{5,4},{6,7},{7,6},{8,9},{9,8},{10,11... | collective-permute-start | bytes 1376264 | tf_op jit(solution)/shard_map/ppermute | solution.py:457

commit v5 on v4

--- a/solution.py
+++ b/solution.py
@@ -154,18 +154,22 @@
     causal[1] = jnp.where(key_at <= query_at, 0.0, -HIDDEN)
 
 
+def halves(rows):
+    return (0, 128), (128, rows)
+
+
 def weigh(place, blocks, pairs, keys, weights, scale, causal, ring, slot, sums):
     query, key, diagonal = read_pair(pairs, place + LAG)
     rows, wide = causal.shape[1:]
-    scores = jnp.dot(
-        keys[jnp.minimum(key, blocks - 1)],
-        weights[jnp.minimum(query, blocks - 1)],
-        preferred_element_type=f32,
-    )
-    made = jnp.exp2(scores * scale + causal[diagonal])
-    ring[slot] = made
-    part = jnp.sum(made.reshape(rows // 8, 8, wide), axis=0)
-    sums[query] = jnp.where(diagonal == 1, part, part + sums[query])
+    key_block = jnp.minimum(key, blocks - 1)
+    operand = weights[jnp.minimum(query, blocks - 1)]
+    part = jnp.where(diagonal == 1, 0.0, sums[query])
+    for low, high in halves(rows):
+        scores = jnp.dot(keys[key_block, low:high], operand, preferred_element_type=f32)
+        made = jnp.exp2(scores * scale + causal[diagonal, low:high])
+        ring[slot, low:high] = made
+        part += jnp.sum(made.reshape((high - low) // 8, 8, wide), axis=0)
+    sums[query] = part
 
 
 def student_kernel(
@@ -325,13 +329,17 @@
 
     def couple(place, teacher, student, scale):
         query, key, _ = read_pair(pairs, place)
-        coupling = (student * scale[1] - teacher * scale[0]).astype(bf16)
         query_side = features[readable(query)]
-        key_side = features[readable(key), :, :rows]
-        grad[key, :, :rows] += lax.dot_general(
-            query_side, coupling, (((1,), (1,)), ((), ())), preferred_element_type=f32
-        )
-        grad[query] += jnp.dot(key_side, coupling, preferred_element_type=f32)
+        to_queries = jnp.zeros((WS, wide), f32)
+        for low, high in halves(rows):
+            coupling = student[low:high] * scale[1] - teacher[low:high] * scale[0]
+            coupling = coupling.astype(bf16)
+            key_side = features[readable(key), :, low:high]
+            grad[key, :, low:high] += lax.dot_general(
+                query_side, coupling, (((1,), (1,)), ((), ())), preferred_element_type=f32
+            )
+            to_queries += jnp.dot(key_side, coupling, preferred_element_type=f32)
+        grad[query] += to_queries
 
     def half(turn, parity):
         slot = turn & (SLOTS - 1)
@@ -344,8 +352,8 @@
         before = (turn - LAG // UNROLL) // 2 & 1
         for step in range(UNROLL):
             place = UNROLL * turn + step
-            old = rings[1 - parity][step][before]
-            couple(place, old, fetched[step][slot], scale[step])
+            old = rings[1 - parity][step].at[before]
+            couple(place, old, fetched[step].at[slot], scale[step])
             ring = rings[parity][step]
             weigh(place, blocks, pairs, keys, weights, SCALE_T, causal, ring, now, sums)
 
@@ -361,7 +369,7 @@
             fetch(turns + turn, step).wait()
 
     def finish(block, carry):
-        out[block] = grad[block, :, :rows].astype(bf16)
+        out[block] = grad[block].astype(bf16)
         return carry
 
     lax.fori_loop(0, blocks, finish, 0, unroll=8)
@@ -375,7 +383,7 @@
     ring = pltpu.VMEM((SLOTS, rows, wide), f32)
     return pl.pallas_call(
         functools.partial(gradient_kernel, blocks),
-        out_shape=jax.ShapeDtypeStruct((blocks, WS, rows), bf16),
+        out_shape=jax.ShapeDtypeStruct((blocks, WS, wide), bf16),
         in_specs=[smem, smem, vmem, vmem, pl.BlockSpec(memory_space=pl.ANY), vmem, vmem],
         out_specs=vmem,
         scratch_shapes=[
@@ -406,35 +414,43 @@
     return relation_gradient(teacher, segments, made, scales, features, pairs, count)
 
 
-def unproject_kernel(part, grads, wq, wk, out):
+def unproject_kernel(part, grads, wq, wk, out, held, sems):
     half = grads.shape[0] // 2
-    rows, wide = grads.shape[2], round_up(grads.shape[2], 128)
-    total = jnp.zeros((wq.shape[0], wide), f32)
+    rows, width = out.shape
+    pieces = held.shape[1]
+    size = width // pieces
+    copies = []
     for rel, weight in enumerate((wq, wk)):
-        turned = grads[rel * half : (rel + 1) * half].reshape(half * WS, rows)
-        turned = jnp.concatenate([turned, jnp.zeros((half * WS, wide - rows), bf16)], axis=1)
-        total += jnp.dot(weight[...], turned, preferred_element_type=f32)
+        for piece in range(pieces):
+            first = pl.multiple_of(part[0] * width + piece * size, size)
+            copies.append(
+                pltpu.make_async_copy(
+                    weight.at[pl.ds(first, size)], held.at[rel, piece], sems.at[rel, piece]
+                )
+            )
+            copies[-1].start()
+    total = jnp.zeros((width, grads.shape[2]), f32)
+    for rel in range(2):
+        turned = grads[rel * half : (rel + 1) * half].reshape(half * WS, grads.shape[2])
+        for piece in range(pieces):
+            copies[rel * pieces + piece].wait()
+        weight = held[rel].reshape(width, half * WS)
+        total += jnp.dot(weight, turned, preferred_element_type=f32)
     out[...] = total.T[:rows].astype(out.dtype)
 
 
-def unproject(part, grads, wq, wk, dtype):
-    rows = grads.shape[2]
+def unproject(part, grads, wq, wk, rows, dtype):
     width = wq.shape[0] // 2
-    tile = 256
-    steps = width // tile
-
-    def weight_block(i, part):
-        return part[0] * steps + i, 0
-
-    weight = pl.BlockSpec((tile, wq.shape[1]), weight_block)
+    vmem = pl.BlockSpec(memory_space=pltpu.VMEM)
+    hbm = pl.BlockSpec(memory_space=pl.ANY)
     return pl.pallas_call(
         unproject_kernel,
-        grid_spec=pltpu.PrefetchScalarGridSpec(
-            num_scalar_prefetch=1,
-            grid=(steps,),
-            in_specs=[pl.BlockSpec(grads.shape, lambda i, part: (0, 0, 0)), weight, weight],
-            out_specs=pl.BlockSpec((rows, tile), lambda i, part: (0, i)),
-        ),
+        in_specs=[pl.BlockSpec(memory_space=pltpu.SMEM), vmem, hbm, hbm],
+        out_specs=vmem,
+        scratch_shapes=[
+            pltpu.VMEM((2, 4, width // 4, wq.shape[1]), bf16),
+            pltpu.SemaphoreType.DMA((2, 4)),
+        ],
         out_shape=jax.ShapeDtypeStruct((rows, width), dtype),
         compiler_params=pltpu.CompilerParams(vmem_limit_bytes=56 * MIB),
         cost_estimate=pl.CostEstimate(
@@ -453,9 +469,9 @@
     turned = head_gradient(student, teacher, segment_ids, rows)
     back = lax.all_to_all(turned, "ctx", 0, 0, tiled=True)
     side = lax.axis_index("head")
-    away = unproject(1 - side, back, w_query, w_key, bf16)
+    away = unproject(1 - side, back, w_query, w_key, rows, bf16)
     away = lax.ppermute(away, "head", [(0, 1), (1, 0)])
-    own = unproject(side, back, w_query, w_key, f32)
+    own = unproject(side, back, w_query, w_key, rows, f32)
     return (own + away).astype(bf16)
 
 

time: 295 us -> 293 us (level)
  no operation moved by 1% of the time
where the time goes in v5:
time: 293 us; the launch traced here: 294 us
  Pallas kernels  226 us (77%)
  starting transfers between devices  31 us (11%)
  waiting for transfers between devices  28.6 us (10%)
  local copies, waits for them, and re-layouts  6.74 us (2%)
    pallas_call x1, Pallas kernels, relation_gradient(): pl.pallas_call(functools.partial(gradient_kernel, blocks), out_shape=jax....  114 us
    pallas_call x1, Pallas kernels, student_weights(): pl.pallas_call(functools.partial(student_kernel, blocks), out_shape=(jax....  89.3 us
    all_to_all x1, waiting for transfers between devices, shards(): back = lax.all_to_all(turned, 'ctx', 0, 0, tiled=True)  15.7 us
    all_to_all x1, waiting for transfers between devices, shards(): lax.all_to_all(student.reshape(-1, *student.shape[2:]), 'ctx', 0, 0, tile...  12.8 us
    all_to_all x1, starting transfers between devices, shards(): lax.all_to_all(student.reshape(-1, *student.shape[2:]), 'ctx', 0, 0, tile...  12 us
    pallas_call x2, Pallas kernels, unproject(): pl.pallas_call(unproject_kernel, in_specs=[pl.BlockSpec(memory_space=pltp...  11.3 us
    all_to_all x1, starting transfers between devices, shards(): back = lax.all_to_all(turned, 'ctx', 0, 0, tiled=True)  9.78 us
    pallas_call x1, Pallas kernels, project(): pl.pallas_call(project_kernel, grid=(heads // PACK,), out_shape=jax.Shape...  6.66 us
  transfers between devices with their start and end apart: 4, of which 2 were waited for; matrix products, arithmetic and copies ran while one was open for 0% of the time, Pallas kernels for 34%

profile of v5, /device:TPU:1, one launch (start us, length us, event | category | flops | bytes accessed | tf_op | source)
XLA Modules:
  0.0 294.5 jit_solution(14315324140443736674)
XLA Ops:
  0.0 6.7 %project_student.1 = bf16[2,32,32,256]{3,2,1,0:T(8,128)(2,1)} custom-call(s32[1,7]{1,0:T(1,128)} %mask.1, bf16[224,2048]{1,0:T(8,128)(2,1)} %hidden.1, bf16[2048,1024]{1,0:T(8,128)(2,1)} %wq.5, bf16[2048,1024]{1,0:T(8,128)(2,1)} %wk.5), custom_call_target="tpu_custom_call" | custom-call | flops 1879048192 | bytes 10000000 | tf_op jit(solution)/shard_map/project_student/pallas_call | solution.py:58
  6.7 12.0 %all-to-all-start = ((bf16[64,32,256]{2,1,0:T(8,128)(2,1)}), bf16[64,32,256]{2,1,0:T(8,128)(2,1)S(1)}, u32[]{:S(2)}, u32[]{:S(2)}) async-start(bf16[64,32,256]{2,1,0:T(8,128)(2,1)} %bitcast.7), calls=%async_computation | async-start | bytes 2097152 | tf_op jit(solution)/shard_map/all_to_all | solution.py:467
  18.6 4.3 %turn_teacher.1 = bf16[2,32,80,256]{3,2,1,0:T(8,128)(2,1)} custom-call(bf16[224,2560]{1,0:T(8,128)(2,1)} %tq.1, bf16[224,2560]{1,0:T(8,128)(2,1)} %tk.1), custom_call_target="tpu_custom_call" | custom-call | bytes 5000000 | tf_op jit(solution)/shard_map/turn_teacher/pallas_call | solution.py:90
  23.0 12.8 %all-to-all-done.slabs = bf16[64,32,256]{2,1,0:T(8,128)(2,1)S(1)} async-done(((bf16[64,32,256]{2,1,0:T(8,128)(2,1)}), bf16[64,32,256]{2,1,0:T(8,128)(2,1)S(1)}, u32[]{:S(2)}, u32[]{:S(2)}) %all-to-all-start) | async-done | bytes 1048608 | tf_op jit(solution)/shard_map/all_to_all | solution.py:467
  35.8 0.0 copy-start.3
  35.8 1.0 copy-done.3
  36.8 0.0 copy-start.6
  36.8 5.2 %all-to-all-start.1 = ((bf16[64,80,256]{2,1,0:T(8,128)(2,1)}), bf16[64,80,256]{2,1,0:T(8,128)(2,1)S(1)}, u32[]{:S(2)}, u32[]{:S(2)}) async-start(bf16[64,80,256]{2,1,0:T(8,128)(2,1)} %bitcast.6), calls=%async_computation.1 | async-start | bytes 5242880 | tf_op jit(solution)/shard_map/all_to_all | solution.py:468
  42.0 0.0 copy-done.6
  42.0 0.1 slice.6
  42.1 0.2 slice.7
  42.3 0.1 reshape.9
  42.4 0.0 copy-start.4
  42.4 1.2 copy-done.4
  43.6 89.3 %student_weights.1 = (f32[512,224,256]{2,1,0:T(8,128)}, f32[64,8,256]{2,1,0:T(8,128)S(1)}, bf16[64,32,256]{2,1,0:T(8,128)(2,1)S(1)}, s32[640]{0:T(1024)S(1)}, s32[1]{0:T(128)}) custom-call(s32[2,64]{1,0:T(2,128)S(1)} %pad_add_fusion.ends, s32[64,256]{1,0:T(8,128)S(1)} %pad.4.segments, bf16[64,32,256]{2,1,0:T(8,128)(2,1)S(1)} %copy-done.4), custom_call_target="tpu_custom_call" | custom-call | flops 10000000000 | bytes 80000000 | tf_op jit(solution)/shard_map/student_weights/pallas_call | solution.py:266
  132.9 0.0 copy-start.1
  132.9 1.0 copy-done.1
  133.9 0.0 all-to-all-done.1.slabs
  133.9 0.0 copy-start.2
  133.9 1.2 copy-done.2
  135.1 114.4 %relation_gradient.1 = bf16[64,32,256]{2,1,0:T(8,128)(2,1)S(1)} custom-call(s32[1]{0:T(128)} %get-tuple-element.10.count_in, s32[640]{0:T(1024)S(1)} %get-tuple-element.11.pairs, s32[64,256]{1,0:T(8,128)S(1)} %pad.4.segments, bf16[64,80,256]{2,1,0:T(8,128)(2,1)S(1)} %all-to-all-done.1.slabs, f32[512,224,256]{2,1,0:T(8,128)} %get-tuple-element.12.made, ...), custom_call_target="tpu_custom_call" | custom-call | flops 20000000000 | bytes 80000000 | tf_op jit(solution)/shard_map/relation_gradient/pallas_call | solution.py:384
  249.5 0.0 copy-start
  249.5 1.0 copy-done
  250.4 9.8 %all-to-all-start.2 = ((bf16[64,32,256]{2,1,0:T(8,128)(2,1)}), bf16[64,32,256]{2,1,0:T(8,128)(2,1)S(1)}, u32[]{:S(2)}, u32[]{:S(2)}) async-start(bf16[64,32,256]{2,1,0:T(8,128)(2,1)} %copy-done), calls=%async_computation.2 | async-start | bytes 2097152 | tf_op jit(solution)/shard_map/all_to_all | solution.py:470
  260.2 15.7 %all-to-all-done.2.grads = bf16[64,32,256]{2,1,0:T(8,128)(2,1)S(1)} async-done(((bf16[64,32,256]{2,1,0:T(8,128)(2,1)}), bf16[64,32,256]{2,1,0:T(8,128)(2,1)S(1)}, u32[]{:S(2)}, u32[]{:S(2)}) %all-to-all-start.2) | async-done | bytes 1048608 | tf_op jit(solution)/shard_map/all_to_all | solution.py:470
  276.0 0.0 copy-start.5
  276.0 1.0 copy-done.5
  277.0 5.5 %unproject.3 = bf16[224,1024]{1,0:T(8,128)(2,1)} custom-call(s32[1]{0:T(128)} %bitcast.5.part, bf16[64,32,256]{2,1,0:T(8,128)(2,1)} %copy-done.5, bf16[2048,1024]{1,0:T(8,128)(2,1)} %wq.5, bf16[2048,1024]{1,0:T(8,128)(2,1)} %wk.5), custom_call_target="tpu_custom_call" | custom-call | flops 939524096 | bytes 6000000 | tf_op jit(solution)/shard_map/unproject/pallas_call | solution.py:446
  282.5 4.1 %collective-permute-start = (bf16[224,1024]{1,0:T(8,128)(2,1)}, bf16[224,1024]{1,0:T(8,128)(2,1)S(1)}, u32[]{:S(2)}, u32[]{:S(2)}) collective-permute-start(bf16[224,1024]{1,0:T(8,128)(2,1)} %unproject.3), channel_id=1, source_target_pairs={{0,1},{1,0},{2,3},{3,2},{4,5},{5,4},{6,7},{7,6},{8,9},{9,8},{10,11... | collective-permute-start | bytes 1376264 | tf_op jit(solution)/shard_map/ppermute | solution.py:473
  286.6 5.8 %unproject.2 = f32[224,1024]{1,0:T(8,128)} custom-call(s32[1]{0:T(128)} %bitcast.part, bf16[64,32,256]{2,1,0:T(8,128)(2,1)} %copy-done.5, bf16[2048,1024]{1,0:T(8,128)(2,1)} %wq.5, bf16[2048,1024]{1,0:T(8,128)(2,1)} %wk.5), custom_call_target="tpu_custom_call" | custom-call | flops 939524096 | bytes 6000000 | tf_op jit(solution)/shard_map/unproject/pallas_call | solution.py:446
  292.4 0.0 collective-permute-done
  292.4 2.1 add_convert_fusion
  (2 shorter events, 0.0 us)
Async XLA Ops:
  6.7 29.1 %all-to-all-start = ((bf16[64,32,256]{2,1,0:T(8,128)(2,1)}), bf16[64,32,256]{2,1,0:T(8,128)(2,1)S(1)}, u32[]{:S(2)}, u32[]{:S(2)}) async-start(bf16[64,32,256]{2,1,0:T(8,128)(2,1)} %bitcast.7), calls=%async_computation | async-start | bytes 2097152 | tf_op jit(solution)/shard_map/all_to_all | solution.py:467
  35.8 1.0 copy-start.3
  36.8 5.2 %copy-start.6 = (s32[14336]{0:T(1024)S(1)}, s32[14336]{0:T(1024)}, u32[]{:S(2)}) copy-start(s32[14336]{0:T(1024)} %param.12) | copy-start | bytes 172036
  36.8 97.1 %all-to-all-start.1 = ((bf16[64,80,256]{2,1,0:T(8,128)(2,1)}), bf16[64,80,256]{2,1,0:T(8,128)(2,1)S(1)}, u32[]{:S(2)}, u32[]{:S(2)}) async-start(bf16[64,80,256]{2,1,0:T(8,128)(2,1)} %bitcast.6), calls=%async_computation.1 | async-start | bytes 5242880 | tf_op jit(solution)/shard_map/all_to_all | solution.py:468
  42.4 1.2 copy-start.4
  132.9 1.0 copy-start.1
  133.9 1.2 copy-start.2
  249.5 1.0 copy-start
  250.4 25.5 %all-to-all-start.2 = ((bf16[64,32,256]{2,1,0:T(8,128)(2,1)}), bf16[64,32,256]{2,1,0:T(8,128)(2,1)S(1)}, u32[]{:S(2)}, u32[]{:S(2)}) async-start(bf16[64,32,256]{2,1,0:T(8,128)(2,1)} %copy-done), calls=%async_computation.2 | async-start | bytes 2097152 | tf_op jit(solution)/shard_map/all_to_all | solution.py:470
  276.0 1.0 copy-start.5
  282.5 9.9 %collective-permute-start = (bf16[224,1024]{1,0:T(8,128)(2,1)}, bf16[224,1024]{1,0:T(8,128)(2,1)S(1)}, u32[]{:S(2)}, u32[]{:S(2)}) collective-permute-start(bf16[224,1024]{1,0:T(8,128)(2,1)} %unproject.3), channel_id=1, source_target_pairs={{0,1},{1,0},{2,3},{3,2},{4,5},{5,4},{6,7},{7,6},{8,9},{9,8},{10,11... | collective-permute-start | bytes 1376264 | tf_op jit(solution)/shard_map/ppermute | solution.py:473

commit v6 on v5

--- a/solution.py
+++ b/solution.py
@@ -25,10 +25,9 @@
 AHEAD = 2
 LIST = 640
 HIDDEN = 1e30
-LOG2E = math.log2(math.e)
-SCALE_T = LOG2E / math.sqrt(WT)
-SCALE_S = LOG2E / math.sqrt(WS)
-SAFE = 90.0
+SCALE_T = 1.0 / math.sqrt(WT)
+SCALE_S = 1.0 / math.sqrt(WS)
+SAFE = 60.0
 MIB = 1024 * 1024
 f32 = jnp.float32
 bf16 = jnp.bfloat16
@@ -166,7 +165,7 @@
     part = jnp.where(diagonal == 1, 0.0, sums[query])
     for low, high in halves(rows):
         scores = jnp.dot(keys[key_block, low:high], operand, preferred_element_type=f32)
-        made = jnp.exp2(scores * scale + causal[diagonal, low:high])
+        made = jnp.exp(scores * scale + causal[diagonal, low:high])
         ring[slot, low:high] = made
         part += jnp.sum(made.reshape((high - low) // 8, 8, wide), axis=0)
     sums[query] = part
@@ -414,45 +413,26 @@
     return relation_gradient(teacher, segments, made, scales, features, pairs, count)
 
 
-def unproject_kernel(part, grads, wq, wk, out, held, sems):
+def unproject_kernel(part, grads, wq, wk, out):
     half = grads.shape[0] // 2
     rows, width = out.shape
-    pieces = held.shape[1]
-    size = width // pieces
-    copies = []
+    columns = pl.ds(pl.multiple_of(part[0] * width, 256), width)
+    total = jnp.zeros((width, grads.shape[2]), f32)
     for rel, weight in enumerate((wq, wk)):
-        for piece in range(pieces):
-            first = pl.multiple_of(part[0] * width + piece * size, size)
-            copies.append(
-                pltpu.make_async_copy(
-                    weight.at[pl.ds(first, size)], held.at[rel, piece], sems.at[rel, piece]
-                )
-            )
-            copies[-1].start()
-    total = jnp.zeros((width, grads.shape[2]), f32)
-    for rel in range(2):
         turned = grads[rel * half : (rel + 1) * half].reshape(half * WS, grads.shape[2])
-        for piece in range(pieces):
-            copies[rel * pieces + piece].wait()
-        weight = held[rel].reshape(width, half * WS)
-        total += jnp.dot(weight, turned, preferred_element_type=f32)
+        total += jnp.dot(weight[columns], turned, preferred_element_type=f32)
     out[...] = total.T[:rows].astype(out.dtype)
 
 
 def unproject(part, grads, wq, wk, rows, dtype):
     width = wq.shape[0] // 2
     vmem = pl.BlockSpec(memory_space=pltpu.VMEM)
-    hbm = pl.BlockSpec(memory_space=pl.ANY)
     return pl.pallas_call(
         unproject_kernel,
-        in_specs=[pl.BlockSpec(memory_space=pltpu.SMEM), vmem, hbm, hbm],
+        in_specs=[pl.BlockSpec(memory_space=pltpu.SMEM), vmem, vmem, vmem],
         out_specs=vmem,
-        scratch_shapes=[
-            pltpu.VMEM((2, 4, width // 4, wq.shape[1]), bf16),
-            pltpu.SemaphoreType.DMA((2, 4)),
-        ],
         out_shape=jax.ShapeDtypeStruct((rows, width), dtype),
-        compiler_params=pltpu.CompilerParams(vmem_limit_bytes=56 * MIB),
+        compiler_params=pltpu.CompilerParams(vmem_limit_bytes=32 * MIB),
         cost_estimate=pl.CostEstimate(
             flops=4 * rows * width * wq.shape[1], bytes_accessed=6_000_000, transcendentals=0
         ),

time: 293 us -> 279 us (0.952)
  Pallas kernels: 226 us -> 212 us
  local copies, waits for them, and re-layouts: 6.74 us -> 10.1 us
    pallas_call x2, Pallas kernels: 11.3 us -> 2.63 us  [unproject(): pl.pallas_call(unproject_kernel, in_specs=[pl.BlockSpec(memory_space=pltp...]
    unnamed x14 -> x16, local copies, waits for them, and re-layouts: 6.35 us -> 9.73 us
  transfers between devices with their start and end apart: 4 -> 4, of which waited for: 2 -> 3; matrix products, arithmetic and copies ran while one was open for 0% -> 0% of each run, Pallas kernels for 34% -> 33%
where the time goes in v6:
time: 279 us; the launch traced here: 283 us
  Pallas kernels  212 us (76%)
  starting transfers between devices  30.9 us (11%)
  waiting for transfers between devices  28.7 us (10%)
  local copies, waits for them, and re-layouts  10.1 us (4%)
    pallas_call x1, Pallas kernels, relation_gradient(): pl.pallas_call(functools.partial(gradient_kernel, blocks), out_shape=jax....  112 us
    pallas_call x1, Pallas kernels, student_weights(): pl.pallas_call(functools.partial(student_kernel, blocks), out_shape=(jax....  87.3 us
    all_to_all x1, waiting for transfers between devices, shards(): back = lax.all_to_all(turned, 'ctx', 0, 0, tiled=True)  15.7 us
    all_to_all x1, waiting for transfers between devices, shards(): lax.all_to_all(student.reshape(-1, *student.shape[2:]), 'ctx', 0, 0, tile...  12.8 us
    all_to_all x1, starting transfers between devices, shards(): lax.all_to_all(student.reshape(-1, *student.shape[2:]), 'ctx', 0, 0, tile...  12 us
    all_to_all x1, starting transfers between devices, shards(): back = lax.all_to_all(turned, 'ctx', 0, 0, tiled=True)  9.78 us
    unnamed x16, local copies, waits for them, and re-layouts  9.73 us
    pallas_call x1, Pallas kernels, project(): pl.pallas_call(project_kernel, grid=(heads // PACK,), out_shape=jax.Shape...  6.65 us
  transfers between devices with their start and end apart: 4, of which 3 were waited for; matrix products, arithmetic and copies ran while one was open for 0% of the time, Pallas kernels for 33%

profile of v6, /device:TPU:1, one launch (start us, length us, event | category | flops | bytes accessed | tf_op | source)
XLA Modules:
  0.0 283.2 jit_solution(11063546737475856149)
XLA Ops:
  0.0 6.7 %project_student.1 = bf16[2,32,32,256]{3,2,1,0:T(8,128)(2,1)} custom-call(s32[1,7]{1,0:T(1,128)} %mask.1, bf16[224,2048]{1,0:T(8,128)(2,1)} %hidden.1, bf16[2048,1024]{1,0:T(8,128)(2,1)} %wq.5, bf16[2048,1024]{1,0:T(8,128)(2,1)} %wk.5), custom_call_target="tpu_custom_call" | custom-call | flops 1879048192 | bytes 10000000 | tf_op jit(solution)/shard_map/project_student/pallas_call | solution.py:57
  6.7 12.0 %all-to-all-start = ((bf16[64,32,256]{2,1,0:T(8,128)(2,1)}), bf16[64,32,256]{2,1,0:T(8,128)(2,1)S(1)}, u32[]{:S(2)}, u32[]{:S(2)}) async-start(bf16[64,32,256]{2,1,0:T(8,128)(2,1)} %bitcast.7), calls=%async_computation | async-start | bytes 2097152 | tf_op jit(solution)/shard_map/all_to_all | solution.py:447
  18.6 4.3 %turn_teacher.1 = bf16[2,32,80,256]{3,2,1,0:T(8,128)(2,1)} custom-call(bf16[224,2560]{1,0:T(8,128)(2,1)} %tq.1, bf16[224,2560]{1,0:T(8,128)(2,1)} %tk.1), custom_call_target="tpu_custom_call" | custom-call | bytes 5000000 | tf_op jit(solution)/shard_map/turn_teacher/pallas_call | solution.py:89
  22.9 12.8 %all-to-all-done.slabs = bf16[64,32,256]{2,1,0:T(8,128)(2,1)S(1)} async-done(((bf16[64,32,256]{2,1,0:T(8,128)(2,1)}), bf16[64,32,256]{2,1,0:T(8,128)(2,1)S(1)}, u32[]{:S(2)}, u32[]{:S(2)}) %all-to-all-start) | async-done | bytes 1048608 | tf_op jit(solution)/shard_map/all_to_all | solution.py:447
  35.8 0.0 copy-start.5
  35.8 1.0 copy-done.5
  36.8 0.0 copy-start.7
  36.8 5.2 %all-to-all-start.1 = ((bf16[64,80,256]{2,1,0:T(8,128)(2,1)}), bf16[64,80,256]{2,1,0:T(8,128)(2,1)S(1)}, u32[]{:S(2)}, u32[]{:S(2)}) async-start(bf16[64,80,256]{2,1,0:T(8,128)(2,1)} %bitcast.6), calls=%async_computation.1 | async-start | bytes 5242880 | tf_op jit(solution)/shard_map/all_to_all | solution.py:448
  41.9 0.0 copy-done.7
  42.0 0.1 slice.6
  42.1 0.2 slice.7
  42.3 0.1 reshape.9
  42.4 0.0 copy-start.6
  42.4 1.2 copy-done.6
  43.6 87.3 %student_weights.1 = (f32[512,224,256]{2,1,0:T(8,128)}, f32[64,8,256]{2,1,0:T(8,128)S(1)}, bf16[64,32,256]{2,1,0:T(8,128)(2,1)S(1)}, s32[640]{0:T(1024)S(1)}, s32[1]{0:T(128)}) custom-call(s32[2,64]{1,0:T(2,128)S(1)} %pad_add_fusion.ends, s32[64,256]{1,0:T(8,128)S(1)} %pad.4.segments, bf16[64,32,256]{2,1,0:T(8,128)(2,1)S(1)} %copy-done.6), custom_call_target="tpu_custom_call" | custom-call | flops 10000000000 | bytes 80000000 | tf_op jit(solution)/shard_map/student_weights/pallas_call | solution.py:265
  130.9 0.0 copy-start.3
  130.9 1.0 copy-done.3
  131.9 0.0 all-to-all-done.1.slabs
  131.9 0.0 copy-start.4
  131.9 1.2 copy-done.4
  133.1 111.5 %relation_gradient.1 = bf16[64,32,256]{2,1,0:T(8,128)(2,1)S(1)} custom-call(s32[1]{0:T(128)} %get-tuple-element.10.count_in, s32[640]{0:T(1024)S(1)} %get-tuple-element.11.pairs, s32[64,256]{1,0:T(8,128)S(1)} %pad.4.segments, bf16[64,80,256]{2,1,0:T(8,128)(2,1)S(1)} %all-to-all-done.1.slabs, f32[512,224,256]{2,1,0:T(8,128)} %get-tuple-element.12.made, ...), custom_call_target="tpu_custom_call" | custom-call | flops 20000000000 | bytes 80000000 | tf_op jit(solution)/shard_map/relation_gradient/pallas_call | solution.py:383
  244.6 0.0 copy-start.2
  244.6 1.0 copy-done.2
  245.6 9.8 %all-to-all-start.2 = ((bf16[64,32,256]{2,1,0:T(8,128)(2,1)}), bf16[64,32,256]{2,1,0:T(8,128)(2,1)S(1)}, u32[]{:S(2)}, u32[]{:S(2)}) async-start(bf16[64,32,256]{2,1,0:T(8,128)(2,1)} %copy-done.2), calls=%async_computation.2 | async-start | bytes 2097152 | tf_op jit(solution)/shard_map/all_to_all | solution.py:450
  255.4 15.7 %all-to-all-done.2.grads = bf16[64,32,256]{2,1,0:T(8,128)(2,1)S(1)} async-done(((bf16[64,32,256]{2,1,0:T(8,128)(2,1)}), bf16[64,32,256]{2,1,0:T(8,128)(2,1)S(1)}, u32[]{:S(2)}, u32[]{:S(2)}) %all-to-all-start.2) | async-done | bytes 1048608 | tf_op jit(solution)/shard_map/all_to_all | solution.py:450
  271.2 0.0 copy-start
  271.2 2.2 copy-done
  273.3 0.0 copy-start.1
  273.3 2.2 copy-done.1
  275.5 1.3 unproject.3
  276.9 4.0 %collective-permute-start = (bf16[224,1024]{1,0:T(8,128)(2,1)S(1)}, bf16[224,1024]{1,0:T(8,128)(2,1)S(1)}, u32[]{:S(2)}, u32[]{:S(2)}) collective-permute-start(bf16[224,1024]{1,0:T(8,128)(2,1)S(1)} %unproject.3), channel_id=1, source_target_pairs={{0,1},{1,0},{2,3},{3,2},{4,5},{5,4},{6,7},{7,6},{8,9},{9,8},{10,11... | collective-permute-start | bytes 1376264 | tf_op jit(solution)/shard_map/ppermute | solution.py:453
  280.9 1.3 unproject.2
  282.2 0.1 collective-permute-done
  282.3 0.9 add_convert_fusion
  (2 shorter events, 0.0 us)
Async XLA Ops:
  6.7 29.1 %all-to-all-start = ((bf16[64,32,256]{2,1,0:T(8,128)(2,1)}), bf16[64,32,256]{2,1,0:T(8,128)(2,1)S(1)}, u32[]{:S(2)}, u32[]{:S(2)}) async-start(bf16[64,32,256]{2,1,0:T(8,128)(2,1)} %bitcast.7), calls=%async_computation | async-start | bytes 2097152 | tf_op jit(solution)/shard_map/all_to_all | solution.py:447
  35.8 1.0 copy-start.5
  36.8 5.2 %copy-start.7 = (s32[14336]{0:T(1024)S(1)}, s32[14336]{0:T(1024)}, u32[]{:S(2)}) copy-start(s32[14336]{0:T(1024)} %param.12) | copy-start | bytes 172036
  36.8 95.1 %all-to-all-start.1 = ((bf16[64,80,256]{2,1,0:T(8,128)(2,1)}), bf16[64,80,256]{2,1,0:T(8,128)(2,1)S(1)}, u32[]{:S(2)}, u32[]{:S(2)}) async-start(bf16[64,80,256]{2,1,0:T(8,128)(2,1)} %bitcast.6), calls=%async_computation.1 | async-start | bytes 5242880 | tf_op jit(solution)/shard_map/all_to_all | solution.py:448
  42.4 1.2 copy-start.6
  130.9 1.0 copy-start.3
  131.9 1.2 copy-start.4
  244.6 1.0 copy-start.2
  245.6 25.5 %all-to-all-start.2 = ((bf16[64,32,256]{2,1,0:T(8,128)(2,1)}), bf16[64,32,256]{2,1,0:T(8,128)(2,1)S(1)}, u32[]{:S(2)}, u32[]{:S(2)}) async-start(bf16[64,32,256]{2,1,0:T(8,128)(2,1)} %copy-done.2), calls=%async_computation.2 | async-start | bytes 2097152 | tf_op jit(solution)/shard_map/all_to_all | solution.py:450
  271.2 2.2 copy-start
  273.3 2.2 copy-start.1
  276.9 5.4 %collective-permute-start = (bf16[224,1024]{1,0:T(8,128)(2,1)S(1)}, bf16[224,1024]{1,0:T(8,128)(2,1)S(1)}, u32[]{:S(2)}, u32[]{:S(2)}) collective-permute-start(bf16[224,1024]{1,0:T(8,128)(2,1)S(1)} %unproject.3), channel_id=1, source_target_pairs={{0,1},{1,0},{2,3},{3,2},{4,5},{5,4},{6,7},{7,6},{8,9},{9,8},{10,11... | collective-permute-start | bytes 1376264 | tf_op jit(solution)/shard_map/ppermute | solution.py:453

commit v7 on v6

--- a/solution.py
+++ b/solution.py
@@ -157,7 +157,7 @@
     return (0, 128), (128, rows)
 
 
-def weigh(place, blocks, pairs, keys, weights, scale, causal, ring, slot, sums):
+def weigh(place, blocks, pairs, keys, weights, scale, causal, target, sums):
     query, key, diagonal = read_pair(pairs, place + LAG)
     rows, wide = causal.shape[1:]
     key_block = jnp.minimum(key, blocks - 1)
@@ -166,16 +166,19 @@
     for low, high in halves(rows):
         scores = jnp.dot(keys[key_block, low:high], operand, preferred_element_type=f32)
         made = jnp.exp(scores * scale + causal[diagonal, low:high])
-        ring[slot, low:high] = made
+        target[low:high] = made
         part += jnp.sum(made.reshape((high - low) // 8, 8, wide), axis=0)
     sums[query] = part
 
 
 def student_kernel(
-    blocks, ends, segments, slabs, made, scales, features, pairs, count_out, keys, weights, rings, causal, sums, seen, opened, sem, sems
+    blocks, ends, segments, slabs_in, made, scales, features_out, pairs, count_out, slabs, features, keys, weights, ring, causal, sums, seen, opened, sem, sems
 ):
     rows, wide = causal.shape[1:]
+    arrive = pltpu.make_async_copy(slabs_in, slabs, sem)
+    arrive.start()
     fill_causal(causal)
+    arrive.wait()
 
     def look(block, carry):
         seen[pl.ds(block, 1)] = slabs[block, :16, wide - 128 :].astype(f32)[:1].astype(jnp.int32)
@@ -221,33 +224,37 @@
     def _():
         subtract_maxima(WS, blocks, count, pairs, keys, weights, causal, sums)
 
-    def send(place, step, slot):
-        return pltpu.make_async_copy(rings[step].at[slot], made.at[place], sems.at[step, slot])
+    leave = pltpu.make_async_copy(features, features_out, sem)
+    leave.start()
+
+    def send(turn):
+        slot = turn & (SLOTS - 1)
+        group = made.at[pl.ds(turn * LISTED, LISTED)]
+        return pltpu.make_async_copy(ring.at[slot], group, sems.at[slot])
 
     def steps(turn, carry):
         slot = turn & (SLOTS - 1)
 
         @pl.when(turn >= SLOTS)
         def _():
-            for step in range(LISTED):
-                send(LISTED * turn + step, step, slot).wait()
+            send(turn - SLOTS).wait()
 
         for step in range(LISTED):
             place = LISTED * turn + step
-            weigh(place, blocks, pairs, keys, weights, SCALE_S, causal, rings[step], slot, sums)
-        for step in range(LISTED):
-            send(LISTED * turn + step, step, slot).start()
+            target = ring.at[slot, step]
+            weigh(place, blocks, pairs, keys, weights, SCALE_S, causal, target, sums)
+        send(turn).start()
         return carry
 
     turns = (count + LISTED - 1) // LISTED
     lax.fori_loop(0, turns, steps, 0)
 
     def drain(turn, carry):
-        for step in range(LISTED):
-            send(LISTED * turn + step, step, turn & (SLOTS - 1)).wait()
+        send(turn).wait()
         return carry
 
     lax.fori_loop(jnp.maximum(turns - SLOTS, 0), turns, drain, 0)
+    leave.wait()
 
     def finish(block, carry):
         total = jnp.sum(sums[block], axis=0, keepdims=True) * math.sqrt(WS)
@@ -261,7 +268,8 @@
     blocks, _, wide = slabs.shape
     vmem = pl.BlockSpec(memory_space=pltpu.VMEM)
     smem = pl.BlockSpec(memory_space=pltpu.SMEM)
-    ring = pltpu.VMEM((SLOTS, rows, wide), f32)
+    hbm = pl.BlockSpec(memory_space=pl.ANY)
+    slab = pltpu.VMEM((blocks, WS, wide), bf16)
     return pl.pallas_call(
         functools.partial(student_kernel, blocks),
         out_shape=(
@@ -271,18 +279,20 @@
             jax.ShapeDtypeStruct((LIST,), jnp.int32),
             jax.ShapeDtypeStruct((1,), jnp.int32),
         ),
-        in_specs=[smem, vmem, vmem],
-        out_specs=(pl.BlockSpec(memory_space=pl.ANY), vmem, vmem, smem, smem),
+        in_specs=[smem, vmem, hbm],
+        out_specs=(hbm, vmem, hbm, smem, smem),
         scratch_shapes=[
+            slab,
+            slab,
             pltpu.VMEM((blocks, rows, DEPTH), bf16),
             pltpu.VMEM((blocks, DEPTH, wide), bf16),
-            [ring] * LISTED,
+            pltpu.VMEM((SLOTS, LISTED, rows, wide), f32),
             pltpu.VMEM((2, rows, wide), f32),
             pltpu.VMEM((blocks + 1, 8, wide), f32),
             pltpu.VMEM((blocks, 128), jnp.int32),
             pltpu.SMEM((blocks, 128), jnp.int32),
             pltpu.SemaphoreType.DMA,
-            pltpu.SemaphoreType.DMA((LISTED, SLOTS)),
+            pltpu.SemaphoreType.DMA((SLOTS,)),
         ],
         compiler_params=pltpu.CompilerParams(vmem_limit_bytes=48 * MIB),
         cost_estimate=pl.CostEstimate(
@@ -293,20 +303,22 @@
 
 
 def gradient_kernel(
-    blocks, count_in, pairs, segments, slabs, made, scales, features, out, keys, weights, rings, fetched, causal, sums, grad, sems
+    blocks, count_in, pairs, segments, slabs, made, scales, features_in, out, features, result, keys, weights, rings, fetched, causal, sums, grad, sems, sem, out_sems
 ):
     rows, wide = causal.shape[1:]
     count = count_in[0]
+    arrive = pltpu.make_async_copy(features_in, features, sem)
+    arrive.start()
     fill_causal(causal)
 
-    def fetch(turn, step):
-        pair = jnp.clip(UNROLL * turn + step - LAG, 0, made.shape[0] - 1)
+    def fetch(turn):
+        group = jnp.clip(turn - LAG // UNROLL, 0, made.shape[0] // UNROLL - 1)
         slot = turn & (SLOTS - 1)
-        return pltpu.make_async_copy(made.at[pair], fetched[step].at[slot], sems.at[step, slot])
+        group = made.at[pl.ds(group * UNROLL, UNROLL)]
+        return pltpu.make_async_copy(group, fetched.at[slot], sems.at[slot])
 
     for turn in range(AHEAD):
-        for step in range(UNROLL):
-            fetch(turn, step).start()
+        fetch(turn).start()
 
     def prepare(block, peak):
         grad[block] = jnp.zeros((WS, wide), f32)
@@ -342,19 +354,17 @@
 
     def half(turn, parity):
         slot = turn & (SLOTS - 1)
-        for step in range(UNROLL):
-            fetch(turn, step).wait()
-        for step in range(UNROLL):
-            fetch(turn + AHEAD, step).start()
+        fetch(turn).wait()
+        fetch(turn + AHEAD).start()
         scale = [inverses(UNROLL * turn + step) for step in range(UNROLL)]
         now = turn // 2 & 1
         before = (turn - LAG // UNROLL) // 2 & 1
         for step in range(UNROLL):
             place = UNROLL * turn + step
-            old = rings[1 - parity][step].at[before]
-            couple(place, old, fetched[step].at[slot], scale[step])
-            ring = rings[parity][step]
-            weigh(place, blocks, pairs, keys, weights, SCALE_T, causal, ring, now, sums)
+            old = rings[1 - parity].at[before, step]
+            couple(place, old, fetched.at[slot, step], scale[step])
+            target = rings[parity].at[now, step]
+            weigh(place, blocks, pairs, keys, weights, SCALE_T, causal, target, sums)
 
     def steps(turn, carry):
         for parity in range(2):
@@ -362,16 +372,26 @@
         return carry
 
     turns = (count + LAG + UNROLL - 1) // UNROLL
+    arrive.wait()
     lax.fori_loop(0, turns, steps, 0)
     for turn in range(AHEAD):
-        for step in range(UNROLL):
-            fetch(turns + turn, step).wait()
+        fetch(turns + turn).wait()
+
+    pieces = out_sems.shape[0]
+    size = blocks // pieces
 
     def finish(block, carry):
-        out[block] = grad[block].astype(bf16)
-        return carry
-
-    lax.fori_loop(0, blocks, finish, 0, unroll=8)
+        result[block] = grad[block].astype(bf16)
+        return carry
+
+    copies = []
+    for piece in range(pieces):
+        lax.fori_loop(piece * size, (piece + 1) * size, finish, 0, unroll=8)
+        part = pl.ds(piece * size, size)
+        copies.append(pltpu.make_async_copy(result.at[part], out.at[part], out_sems.at[piece]))
+        copies[-1].start()
+    for copy in copies:
+        copy.wait()
 
 
 def relation_gradient(slabs, segments, made, scales, features, pairs, count):
@@ -379,21 +399,26 @@
     rows = made.shape[1]
     vmem = pl.BlockSpec(memory_space=pltpu.VMEM)
     smem = pl.BlockSpec(memory_space=pltpu.SMEM)
-    ring = pltpu.VMEM((SLOTS, rows, wide), f32)
+    hbm = pl.BlockSpec(memory_space=pl.ANY)
+    slab = pltpu.VMEM((blocks, WS, wide), bf16)
     return pl.pallas_call(
         functools.partial(gradient_kernel, blocks),
         out_shape=jax.ShapeDtypeStruct((blocks, WS, wide), bf16),
-        in_specs=[smem, smem, vmem, vmem, pl.BlockSpec(memory_space=pl.ANY), vmem, vmem],
-        out_specs=vmem,
+        in_specs=[smem, smem, vmem, vmem, hbm, vmem, hbm],
+        out_specs=hbm,
         scratch_shapes=[
+            slab,
+            slab,
             pltpu.VMEM((blocks, rows, DEPTH), bf16),
             pltpu.VMEM((blocks, DEPTH, wide), bf16),
-            [[pltpu.VMEM((2, rows, wide), f32)] * UNROLL] * 2,
-            [ring] * UNROLL,
+            [pltpu.VMEM((2, UNROLL, rows, wide), f32)] * 2,
+            pltpu.VMEM((SLOTS, UNROLL, rows, wide), f32),
             pltpu.VMEM((2, rows, wide), f32),
             pltpu.VMEM((blocks + 1, 8, wide), f32),
             pltpu.VMEM((blocks + 1, WS, wide), f32),
-            pltpu.SemaphoreType.DMA((UNROLL, SLOTS)),
+            pltpu.SemaphoreType.DMA((SLOTS,)),
+            pltpu.SemaphoreType.DMA,
+            pltpu.SemaphoreType.DMA((4,)),
         ],
         compiler_params=pltpu.CompilerParams(vmem_limit_bytes=48 * MIB),
         cost_estimate=pl.CostEstimate(

time: 279 us -> 281 us (level)
  Pallas kernels: 212 us -> 216 us
where the time goes in v7:
time: 281 us; the launch traced here: 286 us
  Pallas kernels  216 us (77%)
  starting transfers between devices  30.9 us (11%)
  waiting for transfers between devices  28.7 us (10%)
  local copies, waits for them, and re-layouts  10.1 us (4%)
    pallas_call x1, Pallas kernels, relation_gradient(): pl.pallas_call(functools.partial(gradient_kernel, blocks), out_shape=jax....  114 us
    pallas_call x1, Pallas kernels, student_weights(): pl.pallas_call(functools.partial(student_kernel, blocks), out_shape=(jax....  88.2 us
    all_to_all x1, waiting for transfers between devices, shards(): back = lax.all_to_all(turned, 'ctx', 0, 0, tiled=True)  15.7 us
    all_to_all x1, waiting for transfers between devices, shards(): lax.all_to_all(student.reshape(-1, *student.shape[2:]), 'ctx', 0, 0, tile...  12.8 us
    all_to_all x1, starting transfers between devices, shards(): lax.all_to_all(student.reshape(-1, *student.shape[2:]), 'ctx', 0, 0, tile...  12 us
    all_to_all x1, starting transfers between devices, shards(): back = lax.all_to_all(turned, 'ctx', 0, 0, tiled=True)  9.78 us
    unnamed x16, local copies, waits for them, and re-layouts  9.73 us
    pallas_call x1, Pallas kernels, project(): pl.pallas_call(project_kernel, grid=(heads // PACK,), out_shape=jax.Shape...  6.65 us
  transfers between devices with their start and end apart: 4, of which 3 were waited for; matrix products, arithmetic and copies ran while one was open for 0% of the time, Pallas kernels for 33%

profile of v7, /device:TPU:1, one launch (start us, length us, event | category | flops | bytes accessed | tf_op | source)
XLA Modules:
  0.0 286.4 jit_solution(15000767535418883958)
XLA Ops:
  0.0 6.7 %project_student.1 = bf16[2,32,32,256]{3,2,1,0:T(8,128)(2,1)} custom-call(s32[1,7]{1,0:T(1,128)} %mask.1, bf16[224,2048]{1,0:T(8,128)(2,1)} %hidden.1, bf16[2048,1024]{1,0:T(8,128)(2,1)} %wq.5, bf16[2048,1024]{1,0:T(8,128)(2,1)} %wk.5), custom_call_target="tpu_custom_call" | custom-call | flops 1879048192 | bytes 10000000 | tf_op jit(solution)/shard_map/project_student/pallas_call | solution.py:57
  6.7 12.0 %all-to-all-start = ((bf16[64,32,256]{2,1,0:T(8,128)(2,1)}), bf16[64,32,256]{2,1,0:T(8,128)(2,1)S(1)}, u32[]{:S(2)}, u32[]{:S(2)}) async-start(bf16[64,32,256]{2,1,0:T(8,128)(2,1)} %bitcast.7), calls=%async_computation | async-start | bytes 2097152 | tf_op jit(solution)/shard_map/all_to_all | solution.py:472
  18.6 4.3 %turn_teacher.1 = bf16[2,32,80,256]{3,2,1,0:T(8,128)(2,1)} custom-call(bf16[224,2560]{1,0:T(8,128)(2,1)} %tq.1, bf16[224,2560]{1,0:T(8,128)(2,1)} %tk.1), custom_call_target="tpu_custom_call" | custom-call | bytes 5000000 | tf_op jit(solution)/shard_map/turn_teacher/pallas_call | solution.py:89
  22.9 12.8 %all-to-all-done.slabs_in = bf16[64,32,256]{2,1,0:T(8,128)(2,1)S(1)} async-done(((bf16[64,32,256]{2,1,0:T(8,128)(2,1)}), bf16[64,32,256]{2,1,0:T(8,128)(2,1)S(1)}, u32[]{:S(2)}, u32[]{:S(2)}) %all-to-all-start) | async-done | bytes 1048608 | tf_op jit(solution)/shard_map/all_to_all | solution.py:472
  35.8 0.0 copy-start.5
  35.8 1.0 copy-done.5
  36.8 0.0 copy-start.7
  36.8 5.2 %all-to-all-start.1 = ((bf16[64,80,256]{2,1,0:T(8,128)(2,1)}), bf16[64,80,256]{2,1,0:T(8,128)(2,1)S(1)}, u32[]{:S(2)}, u32[]{:S(2)}) async-start(bf16[64,80,256]{2,1,0:T(8,128)(2,1)} %bitcast.6), calls=%async_computation.1 | async-start | bytes 5242880 | tf_op jit(solution)/shard_map/all_to_all | solution.py:473
  41.9 0.0 copy-done.7
  42.0 0.1 slice.6
  42.1 0.2 slice.7
  42.3 0.1 reshape.9
  42.4 0.0 copy-start.6
  42.4 1.2 copy-done.6
  43.6 88.2 %student_weights.1 = (f32[512,224,256]{2,1,0:T(8,128)}, f32[64,8,256]{2,1,0:T(8,128)S(1)}, bf16[64,32,256]{2,1,0:T(8,128)(2,1)S(1)}, s32[640]{0:T(1024)S(1)}, s32[1]{0:T(128)}) custom-call(s32[2,64]{1,0:T(2,128)S(1)} %pad_add_fusion.ends, s32[64,256]{1,0:T(8,128)S(1)} %pad.4.segments, bf16[64,32,256]{2,1,0:T(8,128)(2,1)S(1)} %copy-done.6), custom_call_target="tpu_custom_call" | custom-call | flops 10000000000 | bytes 80000000 | tf_op jit(solution)/shard_map/student_weights/pallas_call | solution.py:273
  131.8 0.0 copy-start.3
  131.8 1.0 copy-done.3
  132.8 0.0 all-to-all-done.1.slabs
  132.8 0.0 copy-start.4
  132.8 1.2 copy-done.4
  134.0 113.8 %relation_gradient.1 = bf16[64,32,256]{2,1,0:T(8,128)(2,1)S(1)} custom-call(s32[1]{0:T(128)} %get-tuple-element.10.count_in, s32[640]{0:T(1024)S(1)} %get-tuple-element.11.pairs, s32[64,256]{1,0:T(8,128)S(1)} %pad.4.segments, bf16[64,80,256]{2,1,0:T(8,128)(2,1)S(1)} %all-to-all-done.1.slabs, f32[512,224,256]{2,1,0:T(8,128)} %get-tuple-element.12.made, ...), custom_call_target="tpu_custom_call" | custom-call | flops 20000000000 | bytes 80000000 | tf_op jit(solution)/shard_map/relation_gradient/pallas_call | solution.py:404
  247.8 0.0 copy-start.2
  247.8 1.0 copy-done.2
  248.8 9.8 %all-to-all-start.2 = ((bf16[64,32,256]{2,1,0:T(8,128)(2,1)}), bf16[64,32,256]{2,1,0:T(8,128)(2,1)S(1)}, u32[]{:S(2)}, u32[]{:S(2)}) async-start(bf16[64,32,256]{2,1,0:T(8,128)(2,1)} %copy-done.2), calls=%async_computation.2 | async-start | bytes 2097152 | tf_op jit(solution)/shard_map/all_to_all | solution.py:475
  258.6 15.7 %all-to-all-done.2.grads = bf16[64,32,256]{2,1,0:T(8,128)(2,1)S(1)} async-done(((bf16[64,32,256]{2,1,0:T(8,128)(2,1)}), bf16[64,32,256]{2,1,0:T(8,128)(2,1)S(1)}, u32[]{:S(2)}, u32[]{:S(2)}) %all-to-all-start.2) | async-done | bytes 1048608 | tf_op jit(solution)/shard_map/all_to_all | solution.py:475
  274.3 0.0 copy-start
  274.3 2.2 copy-done
  276.5 0.0 copy-start.1
  276.5 2.2 copy-done.1
  278.7 1.3 unproject.3
  280.0 4.0 %collective-permute-start = (bf16[224,1024]{1,0:T(8,128)(2,1)S(1)}, bf16[224,1024]{1,0:T(8,128)(2,1)S(1)}, u32[]{:S(2)}, u32[]{:S(2)}) collective-permute-start(bf16[224,1024]{1,0:T(8,128)(2,1)S(1)} %unproject.3), channel_id=1, source_target_pairs={{0,1},{1,0},{2,3},{3,2},{4,5},{5,4},{6,7},{7,6},{8,9},{9,8},{10,11... | collective-permute-start | bytes 1376264 | tf_op jit(solution)/shard_map/ppermute | solution.py:478
  284.0 1.3 unproject.2
  285.4 0.1 collective-permute-done
  285.5 0.9 add_convert_fusion
  (2 shorter events, 0.0 us)
Async XLA Ops:
  6.7 29.1 %all-to-all-start = ((bf16[64,32,256]{2,1,0:T(8,128)(2,1)}), bf16[64,32,256]{2,1,0:T(8,128)(2,1)S(1)}, u32[]{:S(2)}, u32[]{:S(2)}) async-start(bf16[64,32,256]{2,1,0:T(8,128)(2,1)} %bitcast.7), calls=%async_computation | async-start | bytes 2097152 | tf_op jit(solution)/shard_map/all_to_all | solution.py:472
  35.8 1.0 copy-start.5
  36.8 5.2 %copy-start.7 = (s32[14336]{0:T(1024)S(1)}, s32[14336]{0:T(1024)}, u32[]{:S(2)}) copy-start(s32[14336]{0:T(1024)} %param.12) | copy-start | bytes 172036
  36.8 96.0 %all-to-all-start.1 = ((bf16[64,80,256]{2,1,0:T(8,128)(2,1)}), bf16[64,80,256]{2,1,0:T(8,128)(2,1)S(1)}, u32[]{:S(2)}, u32[]{:S(2)}) async-start(bf16[64,80,256]{2,1,0:T(8,128)(2,1)} %bitcast.6), calls=%async_computation.1 | async-start | bytes 5242880 | tf_op jit(solution)/shard_map/all_to_all | solution.py:473
  42.4 1.2 copy-start.6
  131.8 1.0 copy-start.3
  132.8 1.2 copy-start.4
  247.8 1.0 copy-start.2
  248.8 25.5 %all-to-all-start.2 = ((bf16[64,32,256]{2,1,0:T(8,128)(2,1)}), bf16[64,32,256]{2,1,0:T(8,128)(2,1)S(1)}, u32[]{:S(2)}, u32[]{:S(2)}) async-start(bf16[64,32,256]{2,1,0:T(8,128)(2,1)} %copy-done.2), calls=%async_computation.2 | async-start | bytes 2097152 | tf_op jit(solution)/shard_map/all_to_all | solution.py:475
  274.3 2.2 copy-start
  276.5 2.2 copy-start.1
  280.0 5.5 %collective-permute-start = (bf16[224,1024]{1,0:T(8,128)(2,1)S(1)}, bf16[224,1024]{1,0:T(8,128)(2,1)S(1)}, u32[]{:S(2)}, u32[]{:S(2)}) collective-permute-start(bf16[224,1024]{1,0:T(8,128)(2,1)S(1)} %unproject.3), channel_id=1, source_target_pairs={{0,1},{1,0},{2,3},{3,2},{4,5},{5,4},{6,7},{7,6},{8,9},{9,8},{10,11... | collective-permute-start | bytes 1376264 | tf_op jit(solution)/shard_map/ppermute | solution.py:478

commit v8 on v7

--- a/solution.py
+++ b/solution.py
@@ -18,8 +18,8 @@
 EXTRA = 16
 DOCS = 4
 PACK = 8
-LISTED = 8
-UNROLL = 4
+LISTED = 16
+UNROLL = 6
 LAG = 3 * UNROLL
 SLOTS = 4
 AHEAD = 2
@@ -438,23 +438,22 @@
     return relation_gradient(teacher, segments, made, scales, features, pairs, count)
 
 
-def unproject_kernel(part, grads, wq, wk, out):
+def unproject_kernel(grads, wq, wk, out):
     half = grads.shape[0] // 2
     rows, width = out.shape
-    columns = pl.ds(pl.multiple_of(part[0] * width, 256), width)
     total = jnp.zeros((width, grads.shape[2]), f32)
     for rel, weight in enumerate((wq, wk)):
         turned = grads[rel * half : (rel + 1) * half].reshape(half * WS, grads.shape[2])
-        total += jnp.dot(weight[columns], turned, preferred_element_type=f32)
+        total += jnp.dot(weight[...], turned, preferred_element_type=f32)
     out[...] = total.T[:rows].astype(out.dtype)
 
 
-def unproject(part, grads, wq, wk, rows, dtype):
-    width = wq.shape[0] // 2
+def unproject(grads, wq, wk, rows, dtype):
+    width = wq.shape[0]
     vmem = pl.BlockSpec(memory_space=pltpu.VMEM)
     return pl.pallas_call(
         unproject_kernel,
-        in_specs=[pl.BlockSpec(memory_space=pltpu.SMEM), vmem, vmem, vmem],
+        in_specs=[vmem, vmem, vmem],
         out_specs=vmem,
         out_shape=jax.ShapeDtypeStruct((rows, width), dtype),
         compiler_params=pltpu.CompilerParams(vmem_limit_bytes=32 * MIB),
@@ -462,7 +461,7 @@
             flops=4 * rows * width * wq.shape[1], bytes_accessed=6_000_000, transcendentals=0
         ),
         name="unproject",
-    )(part[None], grads, wq, wk)
+    )(grads, wq, wk)
 
 
 def shards(teacher_query, teacher_key, student_hidden, w_query, w_key, segment_ids, block_mask):
@@ -472,11 +471,18 @@
     student = lax.all_to_all(student.reshape(-1, *student.shape[2:]), "ctx", 0, 0, tiled=True)
     teacher = lax.all_to_all(teacher.reshape(-1, *teacher.shape[2:]), "ctx", 0, 0, tiled=True)
     turned = head_gradient(student, teacher, segment_ids, rows)
+    side = lax.axis_index("head")
+    width = w_query.shape[0] // 2
+    turned, side = lax.optimization_barrier((turned, side))
+    cut = [
+        [lax.dynamic_slice_in_dim(weight, part * width, width, 0) for weight in (w_query, w_key)]
+        for part in (1 - side, side)
+    ]
+    cut = lax.optimization_barrier(cut)
     back = lax.all_to_all(turned, "ctx", 0, 0, tiled=True)
-    side = lax.axis_index("head")
-    away = unproject(1 - side, back, w_query, w_key, rows, bf16)
+    away = unproject(back, *cut[0], rows, bf16)
     away = lax.ppermute(away, "head", [(0, 1), (1, 0)])
-    own = unproject(side, back, w_query, w_key, rows, f32)
+    own = unproject(back, *cut[1], rows, f32)
     return (own + away).astype(bf16)
 
 

time: 281 us -> 272 us (0.968); the launches traced: 286 us -> 268 us
  Pallas kernels: 216 us -> 198 us
  waiting for transfers between devices: 28.7 us -> 22.4 us
  local copies, waits for them, and re-layouts: 10.1 us -> 15.3 us
    pallas_call x1, Pallas kernels: 114 us -> 98.6 us  [relation_gradient(): pl.pallas_call(functools.partial(gradient_kernel, blocks), out_shape=jax....]
    all_to_all x1, waiting for transfers between devices: 15.7 us -> 9.4 us  [shards(): back = lax.all_to_all(turned, 'ctx', 0, 0, tiled=True)]
    dynamic_slice x0 -> x1, local copies, waits for them, and re-layouts: none -> 6.33 us  [shards(): lax.dynamic_slice_in_dim(weight, part * width, width, 0)]
    unnamed x16 -> x18, local copies, waits for them, and re-layouts: 9.73 us -> 8.57 us
  transfers between devices with their start and end apart: 4 -> 4, of which waited for: 3 -> 3; matrix products, arithmetic and copies ran while one was open for 0% -> 3% of each run, Pallas kernels for 33% -> 34%
where the time goes in v8:
time: 272 us; the launch traced here: 268 us
  Pallas kernels  198 us (73%)
  starting transfers between devices  30.9 us (11%)
  waiting for transfers between devices  22.4 us (8%)
  local copies, waits for them, and re-layouts  15.3 us (6%)
    pallas_call x1, Pallas kernels, relation_gradient(): pl.pallas_call(functools.partial(gradient_kernel, blocks), out_shape=jax....  98.6 us
    pallas_call x1, Pallas kernels, student_weights(): pl.pallas_call(functools.partial(student_kernel, blocks), out_shape=(jax....  86.1 us
    all_to_all x1, waiting for transfers between devices, shards(): lax.all_to_all(student.reshape(-1, *student.shape[2:]), 'ctx', 0, 0, tile...  12.9 us
    all_to_all x1, starting transfers between devices, shards(): lax.all_to_all(student.reshape(-1, *student.shape[2:]), 'ctx', 0, 0, tile...  12 us
    all_to_all x1, starting transfers between devices, shards(): back = lax.all_to_all(turned, 'ctx', 0, 0, tiled=True)  9.78 us
    all_to_all x1, waiting for transfers between devices, shards(): back = lax.all_to_all(turned, 'ctx', 0, 0, tiled=True)  9.4 us
    unnamed x18, local copies, waits for them, and re-layouts  8.57 us
    pallas_call x1, Pallas kernels, project(): pl.pallas_call(project_kernel, grid=(heads // PACK,), out_shape=jax.Shape...  6.64 us
  transfers between devices with their start and end apart: 4, of which 3 were waited for; matrix products, arithmetic and copies ran while one was open for 3% of the time, Pallas kernels for 34%

profile of v8, /device:TPU:1, one launch (start us, length us, event | category | flops | bytes accessed | tf_op | source)
XLA Modules:
  0.0 267.9 jit_solution(9372684835625927049)
XLA Ops:
  0.0 6.6 %project_student.1 = bf16[2,32,32,256]{3,2,1,0:T(8,128)(2,1)} custom-call(s32[1,7]{1,0:T(1,128)} %mask.1, bf16[224,2048]{1,0:T(8,128)(2,1)} %hidden.1, bf16[2048,1024]{1,0:T(8,128)(2,1)} %wq.1, bf16[2048,1024]{1,0:T(8,128)(2,1)} %wk.1), custom_call_target="tpu_custom_call" | custom-call | flops 1879048192 | bytes 10000000 | tf_op jit(solution)/shard_map/project_student/pallas_call | solution.py:57
  6.6 12.0 %all-to-all-start = ((bf16[64,32,256]{2,1,0:T(8,128)(2,1)}), bf16[64,32,256]{2,1,0:T(8,128)(2,1)S(1)}, u32[]{:S(2)}, u32[]{:S(2)}) async-start(bf16[64,32,256]{2,1,0:T(8,128)(2,1)} %bitcast.5), calls=%async_computation | async-start | bytes 2097152 | tf_op jit(solution)/shard_map/all_to_all | solution.py:471
  18.6 4.3 %turn_teacher.1 = bf16[2,32,80,256]{3,2,1,0:T(8,128)(2,1)} custom-call(bf16[224,2560]{1,0:T(8,128)(2,1)} %tq.1, bf16[224,2560]{1,0:T(8,128)(2,1)} %tk.1), custom_call_target="tpu_custom_call" | custom-call | bytes 5000000 | tf_op jit(solution)/shard_map/turn_teacher/pallas_call | solution.py:89
  22.9 12.9 %all-to-all-done.slabs_in = bf16[64,32,256]{2,1,0:T(8,128)(2,1)S(1)} async-done(((bf16[64,32,256]{2,1,0:T(8,128)(2,1)}), bf16[64,32,256]{2,1,0:T(8,128)(2,1)S(1)}, u32[]{:S(2)}, u32[]{:S(2)}) %all-to-all-start) | async-done | bytes 1048608 | tf_op jit(solution)/shard_map/all_to_all | solution.py:471
  35.8 0.0 copy-start.6
  35.8 1.0 copy-done.6
  36.8 0.0 copy-start.8
  36.8 5.2 %all-to-all-start.1 = ((bf16[64,80,256]{2,1,0:T(8,128)(2,1)}), bf16[64,80,256]{2,1,0:T(8,128)(2,1)S(1)}, u32[]{:S(2)}, u32[]{:S(2)}) async-start(bf16[64,80,256]{2,1,0:T(8,128)(2,1)} %bitcast.4), calls=%async_computation.1 | async-start | bytes 5242880 | tf_op jit(solution)/shard_map/all_to_all | solution.py:472
  41.9 0.0 copy-done.8
  42.0 0.1 slice.6
  42.1 0.2 slice.7
  42.3 0.1 reshape.9
  42.4 0.0 copy-start.7
  42.4 1.2 copy-done.7
  43.6 86.1 %student_weights.1 = (f32[512,224,256]{2,1,0:T(8,128)}, f32[64,8,256]{2,1,0:T(8,128)S(1)}, bf16[64,32,256]{2,1,0:T(8,128)(2,1)S(1)}, s32[640]{0:T(1024)S(1)}, s32[1]{0:T(128)}) custom-call(s32[2,64]{1,0:T(2,128)S(1)} %pad_add_fusion.ends, s32[64,256]{1,0:T(8,128)S(1)} %pad.4.segments, bf16[64,32,256]{2,1,0:T(8,128)(2,1)S(1)} %copy-done.7), custom_call_target="tpu_custom_call" | custom-call | flops 10000000000 | bytes 80000000 | tf_op jit(solution)/shard_map/student_weights/pallas_call | solution.py:273
  129.7 0.0 copy-start.4
  129.7 1.0 copy-done.4
  130.7 0.0 all-to-all-done.1.slabs
  130.7 0.0 copy-start.5
  130.7 1.2 copy-done.5
  131.9 98.6 %relation_gradient.1 = bf16[64,32,256]{2,1,0:T(8,128)(2,1)S(1)} custom-call(s32[1]{0:T(128)} %get-tuple-element.16.count_in, s32[640]{0:T(1024)S(1)} %get-tuple-element.17.pairs, s32[64,256]{1,0:T(8,128)S(1)} %pad.4.segments, bf16[64,80,256]{2,1,0:T(8,128)(2,1)S(1)} %all-to-all-done.1.slabs, f32[512,224,256]{2,1,0:T(8,128)} %get-tuple-element.18.made, ...), custom_call_target="tpu_custom_call" | custom-call | flops 20000000000 | bytes 80000000 | tf_op jit(solution)/shard_map/relation_gradient/pallas_call | solution.py:404
  230.5 0.0 copy-start.3
  230.5 1.0 copy-done.3
  231.5 9.8 %all-to-all-start.2 = ((bf16[64,32,256]{2,1,0:T(8,128)(2,1)}), bf16[64,32,256]{2,1,0:T(8,128)(2,1)S(1)}, u32[]{:S(2)}, u32[]{:S(2)}) async-start(bf16[64,32,256]{2,1,0:T(8,128)(2,1)} %copy-done.3), calls=%async_computation.2 | async-start | bytes 2097152 | tf_op jit(solution)/shard_map/all_to_all | solution.py:482
  241.3 6.3 %constant_dynamic-slice_fusion = (bf16[1024,1024]{1,0:T(8,128)(2,1)S(1)}, bf16[1024,1024]{1,0:T(8,128)(2,1)}, bf16[1024,1024]{1,0:T(8,128)(2,1)}, bf16[1024,1024]{1,0:T(8,128)(2,1)}) fusion(bf16[2048,1024]{1,0:T(8,128)(2,1)} %wk.1, s32[]{:T(128)S(6)} %select_n.9, s32[]{:T(128)S(6)} %select_n.8, bf16[2048,1024]{1,0:T(8,128)(2,1)} %wq.1), kind=kLoop, calls=%fused_computation.2 | loop fusion | bytes 16777224 | tf_op jit(solution)/shard_map/dynamic_slice | solution.py:478
  247.6 9.4 %all-to-all-done.2.grads = bf16[64,32,256]{2,1,0:T(8,128)(2,1)S(1)} async-done(((bf16[64,32,256]{2,1,0:T(8,128)(2,1)}), bf16[64,32,256]{2,1,0:T(8,128)(2,1)S(1)}, u32[]{:S(2)}, u32[]{:S(2)}) %all-to-all-start.2) | async-done | bytes 1048608 | tf_op jit(solution)/shard_map/all_to_all | solution.py:482
  257.0 0.0 copy-start.1
  257.0 1.6 copy-done.1
  258.6 0.0 copy-start.2
  258.6 1.6 copy-done.2
  260.2 0.0 copy-start
  260.2 1.3 unproject.3
  261.5 4.0 %collective-permute-start = (bf16[224,1024]{1,0:T(8,128)(2,1)S(1)}, bf16[224,1024]{1,0:T(8,128)(2,1)S(1)}, u32[]{:S(2)}, u32[]{:S(2)}) collective-permute-start(bf16[224,1024]{1,0:T(8,128)(2,1)S(1)} %unproject.3), channel_id=1, source_target_pairs={{0,1},{1,0},{2,3},{3,2},{4,5},{5,4},{6,7},{7,6},{8,9},{9,8},{10,11... | collective-permute-start | bytes 1376264 | tf_op jit(solution)/shard_map/ppermute | solution.py:484
  265.5 0.0 copy-done
  265.5 1.3 unproject.2
  266.9 0.1 collective-permute-done
  267.0 0.9 add_convert_fusion
  (2 shorter events, 0.0 us)
Async XLA Ops:
  6.6 29.1 %all-to-all-start = ((bf16[64,32,256]{2,1,0:T(8,128)(2,1)}), bf16[64,32,256]{2,1,0:T(8,128)(2,1)S(1)}, u32[]{:S(2)}, u32[]{:S(2)}) async-start(bf16[64,32,256]{2,1,0:T(8,128)(2,1)} %bitcast.5), calls=%async_computation | async-start | bytes 2097152 | tf_op jit(solution)/shard_map/all_to_all | solution.py:471
  35.8 1.0 copy-start.6
  36.8 5.2 %copy-start.8 = (s32[14336]{0:T(1024)S(1)}, s32[14336]{0:T(1024)}, u32[]{:S(2)}) copy-start(s32[14336]{0:T(1024)} %param.12) | copy-start | bytes 172036
  36.8 93.9 %all-to-all-start.1 = ((bf16[64,80,256]{2,1,0:T(8,128)(2,1)}), bf16[64,80,256]{2,1,0:T(8,128)(2,1)S(1)}, u32[]{:S(2)}, u32[]{:S(2)}) async-start(bf16[64,80,256]{2,1,0:T(8,128)(2,1)} %bitcast.4), calls=%async_computation.1 | async-start | bytes 5242880 | tf_op jit(solution)/shard_map/all_to_all | solution.py:472
  42.4 1.2 copy-start.7
  129.7 1.0 copy-start.4
  130.7 1.2 copy-start.5
  230.5 1.0 copy-start.3
  231.5 25.5 %all-to-all-start.2 = ((bf16[64,32,256]{2,1,0:T(8,128)(2,1)}), bf16[64,32,256]{2,1,0:T(8,128)(2,1)S(1)}, u32[]{:S(2)}, u32[]{:S(2)}) async-start(bf16[64,32,256]{2,1,0:T(8,128)(2,1)} %copy-done.3), calls=%async_computation.2 | async-start | bytes 2097152 | tf_op jit(solution)/shard_map/all_to_all | solution.py:482
  257.0 1.6 copy-start.1
  258.6 1.6 copy-start.2
  260.2 5.3 %copy-start = (bf16[1024,1024]{1,0:T(8,128)(2,1)S(1)}, bf16[1024,1024]{1,0:T(8,128)(2,1)}, u32[]{:S(2)}) copy-start(bf16[1024,1024]{1,0:T(8,128)(2,1)} %get-tuple-element.23.wq) | copy-start | bytes 6291460
  261.5 5.5 %collective-permute-start = (bf16[224,1024]{1,0:T(8,128)(2,1)S(1)}, bf16[224,1024]{1,0:T(8,128)(2,1)S(1)}, u32[]{:S(2)}, u32[]{:S(2)}) collective-permute-start(bf16[224,1024]{1,0:T(8,128)(2,1)S(1)} %unproject.3), channel_id=1, source_target_pairs={{0,1},{1,0},{2,3},{3,2},{4,5},{5,4},{6,7},{7,6},{8,9},{9,8},{10,11... | collective-permute-start | bytes 1376264 | tf_op jit(solution)/shard_map/ppermute | solution.py:484

commit v9 on v8

--- a/solution.py
+++ b/solution.py
@@ -18,8 +18,8 @@
 EXTRA = 16
 DOCS = 4
 PACK = 8
-LISTED = 16
-UNROLL = 6
+LISTED = 8
+UNROLL = 10
 LAG = 3 * UNROLL
 SLOTS = 4
 AHEAD = 2
@@ -217,7 +217,7 @@
     count_out[0] = count
     for place in range(LAG):
         pairs[place] = blocks | (blocks << 8)
-    for place in range(LAG + LISTED):
+    for place in range(LAG + UNROLL + LISTED):
         pairs[count + LAG + place] = blocks | (blocks << 8)
 
     @pl.when(jnp.logical_not(jnp.max(peak) * SCALE_S <= SAFE))

time: 272 us -> 254 us (0.934)
  Pallas kernels: 198 us -> 181 us
    pallas_call x1, Pallas kernels: 98.6 us -> 87.6 us  [relation_gradient(): pl.pallas_call(functools.partial(gradient_kernel, blocks), out_shape=jax....]
    pallas_call x1, Pallas kernels: 86.1 us -> 80 us  [student_weights(): pl.pallas_call(functools.partial(student_kernel, blocks), out_shape=(jax....]
where the time goes in v9:
time: 254 us; the launch traced here: 251 us
  Pallas kernels  181 us (71%)
  starting transfers between devices  30.9 us (12%)
  waiting for transfers between devices  22.4 us (9%)
  local copies, waits for them, and re-layouts  15.3 us (6%)
    pallas_call x1, Pallas kernels, relation_gradient(): pl.pallas_call(functools.partial(gradient_kernel, blocks), out_shape=jax....  87.6 us
    pallas_call x1, Pallas kernels, student_weights(): pl.pallas_call(functools.partial(student_kernel, blocks), out_shape=(jax....  80 us
    all_to_all x1, waiting for transfers between devices, shards(): lax.all_to_all(student.reshape(-1, *student.shape[2:]), 'ctx', 0, 0, tile...  12.9 us
    all_to_all x1, starting transfers between devices, shards(): lax.all_to_all(student.reshape(-1, *student.shape[2:]), 'ctx', 0, 0, tile...  12 us
    all_to_all x1, starting transfers between devices, shards(): back = lax.all_to_all(turned, 'ctx', 0, 0, tiled=True)  9.78 us
    all_to_all x1, waiting for transfers between devices, shards(): back = lax.all_to_all(turned, 'ctx', 0, 0, tiled=True)  9.4 us
    unnamed x18, local copies, waits for them, and re-layouts  8.57 us
    pallas_call x1, Pallas kernels, project(): pl.pallas_call(project_kernel, grid=(heads // PACK,), out_shape=jax.Shape...  6.64 us
  transfers between devices with their start and end apart: 4, of which 3 were waited for; matrix products, arithmetic and copies ran while one was open for 3% of the time, Pallas kernels for 34%

profile of v9, /device:TPU:1, one launch (start us, length us, event | category | flops | bytes accessed | tf_op | source)
XLA Modules:
  0.0 250.8 jit_solution(4116880460901602420)
XLA Ops:
  0.0 6.6 %project_student.1 = bf16[2,32,32,256]{3,2,1,0:T(8,128)(2,1)} custom-call(s32[1,7]{1,0:T(1,128)} %mask.1, bf16[224,2048]{1,0:T(8,128)(2,1)} %hidden.1, bf16[2048,1024]{1,0:T(8,128)(2,1)} %wq.1, bf16[2048,1024]{1,0:T(8,128)(2,1)} %wk.1), custom_call_target="tpu_custom_call" | custom-call | flops 1879048192 | bytes 10000000 | tf_op jit(solution)/shard_map/project_student/pallas_call | solution.py:57
  6.6 12.0 %all-to-all-start = ((bf16[64,32,256]{2,1,0:T(8,128)(2,1)}), bf16[64,32,256]{2,1,0:T(8,128)(2,1)S(1)}, u32[]{:S(2)}, u32[]{:S(2)}) async-start(bf16[64,32,256]{2,1,0:T(8,128)(2,1)} %bitcast.5), calls=%async_computation | async-start | bytes 2097152 | tf_op jit(solution)/shard_map/all_to_all | solution.py:471
  18.6 4.3 %turn_teacher.1 = bf16[2,32,80,256]{3,2,1,0:T(8,128)(2,1)} custom-call(bf16[224,2560]{1,0:T(8,128)(2,1)} %tq.1, bf16[224,2560]{1,0:T(8,128)(2,1)} %tk.1), custom_call_target="tpu_custom_call" | custom-call | bytes 5000000 | tf_op jit(solution)/shard_map/turn_teacher/pallas_call | solution.py:89
  22.9 12.9 %all-to-all-done.slabs_in = bf16[64,32,256]{2,1,0:T(8,128)(2,1)S(1)} async-done(((bf16[64,32,256]{2,1,0:T(8,128)(2,1)}), bf16[64,32,256]{2,1,0:T(8,128)(2,1)S(1)}, u32[]{:S(2)}, u32[]{:S(2)}) %all-to-all-start) | async-done | bytes 1048608 | tf_op jit(solution)/shard_map/all_to_all | solution.py:471
  35.8 0.0 copy-start.6
  35.8 1.0 copy-done.6
  36.8 0.0 copy-start.8
  36.8 5.2 %all-to-all-start.1 = ((bf16[64,80,256]{2,1,0:T(8,128)(2,1)}), bf16[64,80,256]{2,1,0:T(8,128)(2,1)S(1)}, u32[]{:S(2)}, u32[]{:S(2)}) async-start(bf16[64,80,256]{2,1,0:T(8,128)(2,1)} %bitcast.4), calls=%async_computation.1 | async-start | bytes 5242880 | tf_op jit(solution)/shard_map/all_to_all | solution.py:472
  41.9 0.0 copy-done.8
  42.0 0.1 slice.6
  42.1 0.2 slice.7
  42.3 0.1 reshape.9
  42.4 0.0 copy-start.7
  42.4 1.2 copy-done.7
  43.6 80.0 %student_weights.1 = (f32[512,224,256]{2,1,0:T(8,128)}, f32[64,8,256]{2,1,0:T(8,128)S(1)}, bf16[64,32,256]{2,1,0:T(8,128)(2,1)S(1)}, s32[640]{0:T(1024)S(1)}, s32[1]{0:T(128)}) custom-call(s32[2,64]{1,0:T(2,128)S(1)} %pad_add_fusion.ends, s32[64,256]{1,0:T(8,128)S(1)} %pad.4.segments, bf16[64,32,256]{2,1,0:T(8,128)(2,1)S(1)} %copy-done.7), custom_call_target="tpu_custom_call" | custom-call | flops 10000000000 | bytes 80000000 | tf_op jit(solution)/shard_map/student_weights/pallas_call | solution.py:273
  123.6 0.0 copy-start.4
  123.6 1.0 copy-done.4
  124.5 0.0 all-to-all-done.1.slabs
  124.5 0.0 copy-start.5
  124.6 1.2 copy-done.5
  125.8 87.6 %relation_gradient.1 = bf16[64,32,256]{2,1,0:T(8,128)(2,1)S(1)} custom-call(s32[1]{0:T(128)} %get-tuple-element.16.count_in, s32[640]{0:T(1024)S(1)} %get-tuple-element.17.pairs, s32[64,256]{1,0:T(8,128)S(1)} %pad.4.segments, bf16[64,80,256]{2,1,0:T(8,128)(2,1)S(1)} %all-to-all-done.1.slabs, f32[512,224,256]{2,1,0:T(8,128)} %get-tuple-element.18.made, ...), custom_call_target="tpu_custom_call" | custom-call | flops 20000000000 | bytes 80000000 | tf_op jit(solution)/shard_map/relation_gradient/pallas_call | solution.py:404
  213.4 0.0 copy-start.3
  213.4 1.0 copy-done.3
  214.4 9.8 %all-to-all-start.2 = ((bf16[64,32,256]{2,1,0:T(8,128)(2,1)}), bf16[64,32,256]{2,1,0:T(8,128)(2,1)S(1)}, u32[]{:S(2)}, u32[]{:S(2)}) async-start(bf16[64,32,256]{2,1,0:T(8,128)(2,1)} %copy-done.3), calls=%async_computation.2 | async-start | bytes 2097152 | tf_op jit(solution)/shard_map/all_to_all | solution.py:482
  224.2 6.3 %constant_dynamic-slice_fusion = (bf16[1024,1024]{1,0:T(8,128)(2,1)S(1)}, bf16[1024,1024]{1,0:T(8,128)(2,1)}, bf16[1024,1024]{1,0:T(8,128)(2,1)}, bf16[1024,1024]{1,0:T(8,128)(2,1)}) fusion(bf16[2048,1024]{1,0:T(8,128)(2,1)} %wk.1, s32[]{:T(128)S(6)} %select_n.9, s32[]{:T(128)S(6)} %select_n.8, bf16[2048,1024]{1,0:T(8,128)(2,1)} %wq.1), kind=kLoop, calls=%fused_computation.2 | loop fusion | bytes 16777224 | tf_op jit(solution)/shard_map/dynamic_slice | solution.py:478
  230.5 9.4 %all-to-all-done.2.grads = bf16[64,32,256]{2,1,0:T(8,128)(2,1)S(1)} async-done(((bf16[64,32,256]{2,1,0:T(8,128)(2,1)}), bf16[64,32,256]{2,1,0:T(8,128)(2,1)S(1)}, u32[]{:S(2)}, u32[]{:S(2)}) %all-to-all-start.2) | async-done | bytes 1048608 | tf_op jit(solution)/shard_map/all_to_all | solution.py:482
  239.9 0.0 copy-start.1
  239.9 1.6 copy-done.1
  241.5 0.0 copy-start.2
  241.5 1.6 copy-done.2
  243.1 0.0 copy-start
  243.1 1.3 unproject.3
  244.4 4.0 %collective-permute-start = (bf16[224,1024]{1,0:T(8,128)(2,1)S(1)}, bf16[224,1024]{1,0:T(8,128)(2,1)S(1)}, u32[]{:S(2)}, u32[]{:S(2)}) collective-permute-start(bf16[224,1024]{1,0:T(8,128)(2,1)S(1)} %unproject.3), channel_id=1, source_target_pairs={{0,1},{1,0},{2,3},{3,2},{4,5},{5,4},{6,7},{7,6},{8,9},{9,8},{10,11... | collective-permute-start | bytes 1376264 | tf_op jit(solution)/shard_map/ppermute | solution.py:484
  248.4 0.0 copy-done
  248.4 1.3 unproject.2
  249.7 0.1 collective-permute-done
  249.9 0.9 add_convert_fusion
  (2 shorter events, 0.0 us)
Async XLA Ops:
  6.6 29.1 %all-to-all-start = ((bf16[64,32,256]{2,1,0:T(8,128)(2,1)}), bf16[64,32,256]{2,1,0:T(8,128)(2,1)S(1)}, u32[]{:S(2)}, u32[]{:S(2)}) async-start(bf16[64,32,256]{2,1,0:T(8,128)(2,1)} %bitcast.5), calls=%async_computation | async-start | bytes 2097152 | tf_op jit(solution)/shard_map/all_to_all | solution.py:471
  35.8 1.0 copy-start.6
  36.8 5.2 %copy-start.8 = (s32[14336]{0:T(1024)S(1)}, s32[14336]{0:T(1024)}, u32[]{:S(2)}) copy-start(s32[14336]{0:T(1024)} %param.12) | copy-start | bytes 172036
  36.8 87.8 %all-to-all-start.1 = ((bf16[64,80,256]{2,1,0:T(8,128)(2,1)}), bf16[64,80,256]{2,1,0:T(8,128)(2,1)S(1)}, u32[]{:S(2)}, u32[]{:S(2)}) async-start(bf16[64,80,256]{2,1,0:T(8,128)(2,1)} %bitcast.4), calls=%async_computation.1 | async-start | bytes 5242880 | tf_op jit(solution)/shard_map/all_to_all | solution.py:472
  42.4 1.2 copy-start.7
  123.6 1.0 copy-start.4
  124.5 1.2 copy-start.5
  213.4 1.0 copy-start.3
  214.4 25.5 %all-to-all-start.2 = ((bf16[64,32,256]{2,1,0:T(8,128)(2,1)}), bf16[64,32,256]{2,1,0:T(8,128)(2,1)S(1)}, u32[]{:S(2)}, u32[]{:S(2)}) async-start(bf16[64,32,256]{2,1,0:T(8,128)(2,1)} %copy-done.3), calls=%async_computation.2 | async-start | bytes 2097152 | tf_op jit(solution)/shard_map/all_to_all | solution.py:482
  239.9 1.6 copy-start.1
  241.5 1.6 copy-start.2
  243.1 5.3 %copy-start = (bf16[1024,1024]{1,0:T(8,128)(2,1)S(1)}, bf16[1024,1024]{1,0:T(8,128)(2,1)}, u32[]{:S(2)}) copy-start(bf16[1024,1024]{1,0:T(8,128)(2,1)} %get-tuple-element.23.wq) | copy-start | bytes 6291460
  244.4 5.5 %collective-permute-start = (bf16[224,1024]{1,0:T(8,128)(2,1)S(1)}, bf16[224,1024]{1,0:T(8,128)(2,1)S(1)}, u32[]{:S(2)}, u32[]{:S(2)}) collective-permute-start(bf16[224,1024]{1,0:T(8,128)(2,1)S(1)} %unproject.3), channel_id=1, source_target_pairs={{0,1},{1,0},{2,3},{3,2},{4,5},{5,4},{6,7},{7,6},{8,9},{9,8},{10,11... | collective-permute-start | bytes 1376264 | tf_op jit(solution)/shard_map/ppermute | solution.py:484

commit v10 on v9

--- a/solution.py
+++ b/solution.py
@@ -19,7 +19,7 @@
 DOCS = 4
 PACK = 8
 LISTED = 8
-UNROLL = 10
+UNROLL = 16
 LAG = 3 * UNROLL
 SLOTS = 4
 AHEAD = 2
@@ -303,7 +303,7 @@
 
 
 def gradient_kernel(
-    blocks, count_in, pairs, segments, slabs, made, scales, features_in, out, features, result, keys, weights, rings, fetched, causal, sums, grad, sems, sem, out_sems
+    blocks, count_in, pairs, segments, slabs, made, scales, features_in, out, features, result, keys, weights, rings, fetched, causal, sums, grad, key_grad, sems, sem, out_sems
 ):
     rows, wide = causal.shape[1:]
     count = count_in[0]
@@ -313,7 +313,7 @@
 
     def fetch(turn):
         group = jnp.clip(turn - LAG // UNROLL, 0, made.shape[0] // UNROLL - 1)
-        slot = turn & (SLOTS - 1)
+        slot = lax.rem(turn, AHEAD + 1)
         group = made.at[pl.ds(group * UNROLL, UNROLL)]
         return pltpu.make_async_copy(group, fetched.at[slot], sems.at[slot])
 
@@ -322,6 +322,7 @@
 
     def prepare(block, peak):
         grad[block] = jnp.zeros((WS, wide), f32)
+        key_grad[block] = jnp.zeros((WS, wide), f32)
         return jnp.maximum(peak, fill(block, slabs[block], segments, keys, weights))
 
     peak = lax.fori_loop(0, blocks, prepare, jnp.zeros((1, wide), f32), unroll=4)
@@ -346,14 +347,14 @@
             coupling = student[low:high] * scale[1] - teacher[low:high] * scale[0]
             coupling = coupling.astype(bf16)
             key_side = features[readable(key), :, low:high]
-            grad[key, :, low:high] += lax.dot_general(
+            key_grad[key, :, low:high] += lax.dot_general(
                 query_side, coupling, (((1,), (1,)), ((), ())), preferred_element_type=f32
             )
             to_queries += jnp.dot(key_side, coupling, preferred_element_type=f32)
         grad[query] += to_queries
 
     def half(turn, parity):
-        slot = turn & (SLOTS - 1)
+        slot = lax.rem(turn, AHEAD + 1)
         fetch(turn).wait()
         fetch(turn + AHEAD).start()
         scale = [inverses(UNROLL * turn + step) for step in range(UNROLL)]
@@ -381,7 +382,7 @@
     size = blocks // pieces
 
     def finish(block, carry):
-        result[block] = grad[block].astype(bf16)
+        result[block] = (grad[block] + key_grad[block]).astype(bf16)
         return carry
 
     copies = []
@@ -412,11 +413,12 @@
             pltpu.VMEM((blocks, rows, DEPTH), bf16),
             pltpu.VMEM((blocks, DEPTH, wide), bf16),
             [pltpu.VMEM((2, UNROLL, rows, wide), f32)] * 2,
-            pltpu.VMEM((SLOTS, UNROLL, rows, wide), f32),
+            pltpu.VMEM((AHEAD + 1, UNROLL, rows, wide), f32),
             pltpu.VMEM((2, rows, wide), f32),
             pltpu.VMEM((blocks + 1, 8, wide), f32),
             pltpu.VMEM((blocks + 1, WS, wide), f32),
-            pltpu.SemaphoreType.DMA((SLOTS,)),
+            pltpu.VMEM((blocks + 1, WS, wide), f32),
+            pltpu.SemaphoreType.DMA((AHEAD + 1,)),
             pltpu.SemaphoreType.DMA,
             pltpu.SemaphoreType.DMA((4,)),
         ],

time: 254 us -> 269 us (1.059); the launches traced: 251 us -> 271 us
  Pallas kernels: 181 us -> 201 us
    pallas_call x1, Pallas kernels: 87.6 us -> 98.3 us  [relation_gradient(): pl.pallas_call(functools.partial(gradient_kernel, blocks), out_shape=jax....]
    pallas_call x1, Pallas kernels: 80 us -> 89.3 us  [student_weights(): pl.pallas_call(functools.partial(student_kernel, blocks), out_shape=(jax....]
  transfers between devices with their start and end apart: 4 -> 4, of which waited for: 3 -> 3; matrix products, arithmetic and copies ran while one was open for 3% -> 2% of each run, Pallas kernels for 34% -> 35%
where the time goes in v10:
time: 269 us; the launch traced here: 271 us
  Pallas kernels  201 us (75%)
  starting transfers between devices  30.9 us (11%)
  waiting for transfers between devices  22.4 us (8%)
  local copies, waits for them, and re-layouts  15.3 us (6%)
    pallas_call x1, Pallas kernels, relation_gradient(): pl.pallas_call(functools.partial(gradient_kernel, blocks), out_shape=jax....  98.3 us
    pallas_call x1, Pallas kernels, student_weights(): pl.pallas_call(functools.partial(student_kernel, blocks), out_shape=(jax....  89.3 us
    all_to_all x1, waiting for transfers between devices, shards(): lax.all_to_all(student.reshape(-1, *student.shape[2:]), 'ctx', 0, 0, tile...  12.9 us
    all_to_all x1, starting transfers between devices, shards(): lax.all_to_all(student.reshape(-1, *student.shape[2:]), 'ctx', 0, 0, tile...  12 us
    all_to_all x1, starting transfers between devices, shards(): back = lax.all_to_all(turned, 'ctx', 0, 0, tiled=True)  9.78 us
    all_to_all x1, waiting for transfers between devices, shards(): back = lax.all_to_all(turned, 'ctx', 0, 0, tiled=True)  9.41 us
    unnamed x18, local copies, waits for them, and re-layouts  8.57 us
    pallas_call x1, Pallas kernels, project(): pl.pallas_call(project_kernel, grid=(heads // PACK,), out_shape=jax.Shape...  6.64 us
  transfers between devices with their start and end apart: 4, of which 3 were waited for; matrix products, arithmetic and copies ran while one was open for 2% of the time, Pallas kernels for 35%

profile of v10, /device:TPU:1, one launch (start us, length us, event | category | flops | bytes accessed | tf_op | source)
XLA Modules:
  0.0 270.8 jit_solution(8966530546894519014)
XLA Ops:
  0.0 6.6 %project_student.1 = bf16[2,32,32,256]{3,2,1,0:T(8,128)(2,1)} custom-call(s32[1,7]{1,0:T(1,128)} %mask.1, bf16[224,2048]{1,0:T(8,128)(2,1)} %hidden.1, bf16[2048,1024]{1,0:T(8,128)(2,1)} %wq.1, bf16[2048,1024]{1,0:T(8,128)(2,1)} %wk.1), custom_call_target="tpu_custom_call" | custom-call | flops 1879048192 | bytes 10000000 | tf_op jit(solution)/shard_map/project_student/pallas_call | solution.py:57
  6.6 12.0 %all-to-all-start = ((bf16[64,32,256]{2,1,0:T(8,128)(2,1)}), bf16[64,32,256]{2,1,0:T(8,128)(2,1)S(1)}, u32[]{:S(2)}, u32[]{:S(2)}) async-start(bf16[64,32,256]{2,1,0:T(8,128)(2,1)} %bitcast.5), calls=%async_computation | async-start | bytes 2097152 | tf_op jit(solution)/shard_map/all_to_all | solution.py:473
  18.6 4.3 %turn_teacher.1 = bf16[2,32,80,256]{3,2,1,0:T(8,128)(2,1)} custom-call(bf16[224,2560]{1,0:T(8,128)(2,1)} %tq.1, bf16[224,2560]{1,0:T(8,128)(2,1)} %tk.1), custom_call_target="tpu_custom_call" | custom-call | bytes 5000000 | tf_op jit(solution)/shard_map/turn_teacher/pallas_call | solution.py:89
  22.9 12.9 %all-to-all-done.slabs_in = bf16[64,32,256]{2,1,0:T(8,128)(2,1)S(1)} async-done(((bf16[64,32,256]{2,1,0:T(8,128)(2,1)}), bf16[64,32,256]{2,1,0:T(8,128)(2,1)S(1)}, u32[]{:S(2)}, u32[]{:S(2)}) %all-to-all-start) | async-done | bytes 1048608 | tf_op jit(solution)/shard_map/all_to_all | solution.py:473
  35.8 0.0 copy-start.6
  35.8 1.0 copy-done.6
  36.8 0.0 copy-start.8
  36.8 5.2 %all-to-all-start.1 = ((bf16[64,80,256]{2,1,0:T(8,128)(2,1)}), bf16[64,80,256]{2,1,0:T(8,128)(2,1)S(1)}, u32[]{:S(2)}, u32[]{:S(2)}) async-start(bf16[64,80,256]{2,1,0:T(8,128)(2,1)} %bitcast.4), calls=%async_computation.1 | async-start | bytes 5242880 | tf_op jit(solution)/shard_map/all_to_all | solution.py:474
  41.9 0.0 copy-done.8
  42.0 0.1 slice.6
  42.1 0.2 slice.7
  42.3 0.1 reshape.9
  42.4 0.0 copy-start.7
  42.4 1.2 copy-done.7
  43.6 89.3 %student_weights.1 = (f32[512,224,256]{2,1,0:T(8,128)}, f32[64,8,256]{2,1,0:T(8,128)S(1)}, bf16[64,32,256]{2,1,0:T(8,128)(2,1)S(1)}, s32[640]{0:T(1024)S(1)}, s32[1]{0:T(128)}) custom-call(s32[2,64]{1,0:T(2,128)S(1)} %pad_add_fusion.ends, s32[64,256]{1,0:T(8,128)S(1)} %pad.4.segments, bf16[64,32,256]{2,1,0:T(8,128)(2,1)S(1)} %copy-done.7), custom_call_target="tpu_custom_call" | custom-call | flops 10000000000 | bytes 80000000 | tf_op jit(solution)/shard_map/student_weights/pallas_call | solution.py:273
  133.0 0.0 copy-start.4
  133.0 1.0 copy-done.4
  133.9 0.0 all-to-all-done.1.slabs
  133.9 0.0 copy-start.5
  133.9 1.2 copy-done.5
  135.2 98.3 %relation_gradient.1 = bf16[64,32,256]{2,1,0:T(8,128)(2,1)S(1)} custom-call(s32[1]{0:T(128)} %get-tuple-element.16.count_in, s32[640]{0:T(1024)S(1)} %get-tuple-element.17.pairs, s32[64,256]{1,0:T(8,128)S(1)} %pad.4.segments, bf16[64,80,256]{2,1,0:T(8,128)(2,1)S(1)} %all-to-all-done.1.slabs, f32[512,224,256]{2,1,0:T(8,128)} %get-tuple-element.18.made, ...), custom_call_target="tpu_custom_call" | custom-call | flops 20000000000 | bytes 80000000 | tf_op jit(solution)/shard_map/relation_gradient/pallas_call | solution.py:405
  233.4 0.0 copy-start.3
  233.4 1.0 copy-done.3
  234.4 9.8 %all-to-all-start.2 = ((bf16[64,32,256]{2,1,0:T(8,128)(2,1)}), bf16[64,32,256]{2,1,0:T(8,128)(2,1)S(1)}, u32[]{:S(2)}, u32[]{:S(2)}) async-start(bf16[64,32,256]{2,1,0:T(8,128)(2,1)} %copy-done.3), calls=%async_computation.2 | async-start | bytes 2097152 | tf_op jit(solution)/shard_map/all_to_all | solution.py:484
  244.2 6.3 %constant_dynamic-slice_fusion = (bf16[1024,1024]{1,0:T(8,128)(2,1)S(1)}, bf16[1024,1024]{1,0:T(8,128)(2,1)}, bf16[1024,1024]{1,0:T(8,128)(2,1)}, bf16[1024,1024]{1,0:T(8,128)(2,1)}) fusion(bf16[2048,1024]{1,0:T(8,128)(2,1)} %wk.1, s32[]{:T(128)S(6)} %select_n.9, s32[]{:T(128)S(6)} %select_n.8, bf16[2048,1024]{1,0:T(8,128)(2,1)} %wq.1), kind=kLoop, calls=%fused_computation.2 | loop fusion | bytes 16777224 | tf_op jit(solution)/shard_map/dynamic_slice | solution.py:480
  250.5 9.4 %all-to-all-done.2.grads = bf16[64,32,256]{2,1,0:T(8,128)(2,1)S(1)} async-done(((bf16[64,32,256]{2,1,0:T(8,128)(2,1)}), bf16[64,32,256]{2,1,0:T(8,128)(2,1)S(1)}, u32[]{:S(2)}, u32[]{:S(2)}) %all-to-all-start.2) | async-done | bytes 1048608 | tf_op jit(solution)/shard_map/all_to_all | solution.py:484
  260.0 0.0 copy-start.1
  260.0 1.6 copy-done.1
  261.6 0.0 copy-start.2
  261.6 1.6 copy-done.2
  263.1 0.0 copy-start
  263.1 1.3 unproject.3
  264.5 4.0 %collective-permute-start = (bf16[224,1024]{1,0:T(8,128)(2,1)S(1)}, bf16[224,1024]{1,0:T(8,128)(2,1)S(1)}, u32[]{:S(2)}, u32[]{:S(2)}) collective-permute-start(bf16[224,1024]{1,0:T(8,128)(2,1)S(1)} %unproject.3), channel_id=1, source_target_pairs={{0,1},{1,0},{2,3},{3,2},{4,5},{5,4},{6,7},{7,6},{8,9},{9,8},{10,11... | collective-permute-start | bytes 1376264 | tf_op jit(solution)/shard_map/ppermute | solution.py:486
  268.5 0.0 copy-done
  268.5 1.3 unproject.2
  269.8 0.1 collective-permute-done
  269.9 0.9 add_convert_fusion
  (2 shorter events, 0.0 us)
Async XLA Ops:
  6.6 29.1 %all-to-all-start = ((bf16[64,32,256]{2,1,0:T(8,128)(2,1)}), bf16[64,32,256]{2,1,0:T(8,128)(2,1)S(1)}, u32[]{:S(2)}, u32[]{:S(2)}) async-start(bf16[64,32,256]{2,1,0:T(8,128)(2,1)} %bitcast.5), calls=%async_computation | async-start | bytes 2097152 | tf_op jit(solution)/shard_map/all_to_all | solution.py:473
  35.8 1.0 copy-start.6
  36.8 5.2 %copy-start.8 = (s32[14336]{0:T(1024)S(1)}, s32[14336]{0:T(1024)}, u32[]{:S(2)}) copy-start(s32[14336]{0:T(1024)} %param.12) | copy-start | bytes 172036
  36.8 97.2 %all-to-all-start.1 = ((bf16[64,80,256]{2,1,0:T(8,128)(2,1)}), bf16[64,80,256]{2,1,0:T(8,128)(2,1)S(1)}, u32[]{:S(2)}, u32[]{:S(2)}) async-start(bf16[64,80,256]{2,1,0:T(8,128)(2,1)} %bitcast.4), calls=%async_computation.1 | async-start | bytes 5242880 | tf_op jit(solution)/shard_map/all_to_all | solution.py:474
  42.4 1.2 copy-start.7
  133.0 1.0 copy-start.4
  133.9 1.2 copy-start.5
  233.4 1.0 copy-start.3
  234.4 25.5 %all-to-all-start.2 = ((bf16[64,32,256]{2,1,0:T(8,128)(2,1)}), bf16[64,32,256]{2,1,0:T(8,128)(2,1)S(1)}, u32[]{:S(2)}, u32[]{:S(2)}) async-start(bf16[64,32,256]{2,1,0:T(8,128)(2,1)} %copy-done.3), calls=%async_computation.2 | async-start | bytes 2097152 | tf_op jit(solution)/shard_map/all_to_all | solution.py:484
  260.0 1.6 copy-start.1
  261.6 1.6 copy-start.2
  263.1 5.3 %copy-start = (bf16[1024,1024]{1,0:T(8,128)(2,1)S(1)}, bf16[1024,1024]{1,0:T(8,128)(2,1)}, u32[]{:S(2)}) copy-start(bf16[1024,1024]{1,0:T(8,128)(2,1)} %get-tuple-element.23.wq) | copy-start | bytes 6291460
  264.5 5.4 %collective-permute-start = (bf16[224,1024]{1,0:T(8,128)(2,1)S(1)}, bf16[224,1024]{1,0:T(8,128)(2,1)S(1)}, u32[]{:S(2)}, u32[]{:S(2)}) collective-permute-start(bf16[224,1024]{1,0:T(8,128)(2,1)S(1)} %unproject.3), channel_id=1, source_target_pairs={{0,1},{1,0},{2,3},{3,2},{4,5},{5,4},{6,7},{7,6},{8,9},{9,8},{10,11... | collective-permute-start | bytes 1376264 | tf_op jit(solution)/shard_map/ppermute | solution.py:486

commit v11 on v10

--- a/solution.py
+++ b/solution.py
@@ -325,7 +325,7 @@
         key_grad[block] = jnp.zeros((WS, wide), f32)
         return jnp.maximum(peak, fill(block, slabs[block], segments, keys, weights))
 
-    peak = lax.fori_loop(0, blocks, prepare, jnp.zeros((1, wide), f32), unroll=4)
+    peak = lax.fori_loop(0, blocks, prepare, jnp.zeros((1, wide), f32), unroll=8)
 
     @pl.when(jnp.logical_not(jnp.max(peak) * SCALE_T <= SAFE))
     def _():
@@ -458,7 +458,7 @@
         in_specs=[vmem, vmem, vmem],
         out_specs=vmem,
         out_shape=jax.ShapeDtypeStruct((rows, width), dtype),
-        compiler_params=pltpu.CompilerParams(vmem_limit_bytes=32 * MIB),
+        compiler_params=pltpu.CompilerParams(vmem_limit_bytes=12 * MIB),
         cost_estimate=pl.CostEstimate(
             flops=4 * rows * width * wq.shape[1], bytes_accessed=6_000_000, transcendentals=0
         ),

time: 269 us -> 253 us (0.941)
  Pallas kernels: 201 us -> 184 us
    pallas_call x1, Pallas kernels: 98.3 us -> 89.2 us  [relation_gradient(): pl.pallas_call(functools.partial(gradient_kernel, blocks), out_shape=jax....]
    pallas_call x1, Pallas kernels: 89.3 us -> 81.5 us  [student_weights(): pl.pallas_call(functools.partial(student_kernel, blocks), out_shape=(jax....]
  transfers between devices with their start and end apart: 4 -> 4, of which waited for: 3 -> 3; matrix products, arithmetic and copies ran while one was open for 2% -> 3% of each run, Pallas kernels for 35% -> 34%
where the time goes in v11:
time: 253 us; the launch traced here: 254 us
  Pallas kernels  184 us (73%)
  starting transfers between devices  30.9 us (12%)
  waiting for transfers between devices  22.4 us (9%)
  local copies, waits for them, and re-layouts  15.3 us (6%)
    pallas_call x1, Pallas kernels, relation_gradient(): pl.pallas_call(functools.partial(gradient_kernel, blocks), out_shape=jax....  89.2 us
    pallas_call x1, Pallas kernels, student_weights(): pl.pallas_call(functools.partial(student_kernel, blocks), out_shape=(jax....  81.5 us
    all_to_all x1, waiting for transfers between devices, shards(): lax.all_to_all(student.reshape(-1, *student.shape[2:]), 'ctx', 0, 0, tile...  12.9 us
    all_to_all x1, starting transfers between devices, shards(): lax.all_to_all(student.reshape(-1, *student.shape[2:]), 'ctx', 0, 0, tile...  12 us
    all_to_all x1, starting transfers between devices, shards(): back = lax.all_to_all(turned, 'ctx', 0, 0, tiled=True)  9.78 us
    all_to_all x1, waiting for transfers between devices, shards(): back = lax.all_to_all(turned, 'ctx', 0, 0, tiled=True)  9.4 us
    unnamed x18, local copies, waits for them, and re-layouts  8.57 us
    pallas_call x1, Pallas kernels, project(): pl.pallas_call(project_kernel, grid=(heads // PACK,), out_shape=jax.Shape...  6.64 us
  transfers between devices with their start and end apart: 4, of which 3 were waited for; matrix products, arithmetic and copies ran while one was open for 3% of the time, Pallas kernels for 34%

profile of v11, /device:TPU:1, one launch (start us, length us, event | category | flops | bytes accessed | tf_op | source)
XLA Modules:
  0.0 253.9 jit_solution(106156684837854688)
XLA Ops:
  0.0 6.6 %project_student.1 = bf16[2,32,32,256]{3,2,1,0:T(8,128)(2,1)} custom-call(s32[1,7]{1,0:T(1,128)} %mask.1, bf16[224,2048]{1,0:T(8,128)(2,1)} %hidden.1, bf16[2048,1024]{1,0:T(8,128)(2,1)} %wq.1, bf16[2048,1024]{1,0:T(8,128)(2,1)} %wk.1), custom_call_target="tpu_custom_call" | custom-call | flops 1879048192 | bytes 10000000 | tf_op jit(solution)/shard_map/project_student/pallas_call | solution.py:57
  6.6 12.0 %all-to-all-start = ((bf16[64,32,256]{2,1,0:T(8,128)(2,1)}), bf16[64,32,256]{2,1,0:T(8,128)(2,1)S(1)}, u32[]{:S(2)}, u32[]{:S(2)}) async-start(bf16[64,32,256]{2,1,0:T(8,128)(2,1)} %bitcast.5), calls=%async_computation | async-start | bytes 2097152 | tf_op jit(solution)/shard_map/all_to_all | solution.py:473
  18.6 4.3 %turn_teacher.1 = bf16[2,32,80,256]{3,2,1,0:T(8,128)(2,1)} custom-call(bf16[224,2560]{1,0:T(8,128)(2,1)} %tq.1, bf16[224,2560]{1,0:T(8,128)(2,1)} %tk.1), custom_call_target="tpu_custom_call" | custom-call | bytes 5000000 | tf_op jit(solution)/shard_map/turn_teacher/pallas_call | solution.py:89
  22.9 12.9 %all-to-all-done.slabs_in = bf16[64,32,256]{2,1,0:T(8,128)(2,1)S(1)} async-done(((bf16[64,32,256]{2,1,0:T(8,128)(2,1)}), bf16[64,32,256]{2,1,0:T(8,128)(2,1)S(1)}, u32[]{:S(2)}, u32[]{:S(2)}) %all-to-all-start) | async-done | bytes 1048608 | tf_op jit(solution)/shard_map/all_to_all | solution.py:473
  35.8 0.0 copy-start.6
  35.8 1.0 copy-done.6
  36.8 0.0 copy-start.8
  36.8 5.2 %all-to-all-start.1 = ((bf16[64,80,256]{2,1,0:T(8,128)(2,1)}), bf16[64,80,256]{2,1,0:T(8,128)(2,1)S(1)}, u32[]{:S(2)}, u32[]{:S(2)}) async-start(bf16[64,80,256]{2,1,0:T(8,128)(2,1)} %bitcast.4), calls=%async_computation.1 | async-start | bytes 5242880 | tf_op jit(solution)/shard_map/all_to_all | solution.py:474
  41.9 0.0 copy-done.8
  42.0 0.1 slice.6
  42.1 0.2 slice.7
  42.3 0.1 reshape.9
  42.4 0.0 copy-start.7
  42.4 1.2 copy-done.7
  43.6 81.5 %student_weights.1 = (f32[512,224,256]{2,1,0:T(8,128)}, f32[64,8,256]{2,1,0:T(8,128)S(1)}, bf16[64,32,256]{2,1,0:T(8,128)(2,1)S(1)}, s32[640]{0:T(1024)S(1)}, s32[1]{0:T(128)}) custom-call(s32[2,64]{1,0:T(2,128)S(1)} %pad_add_fusion.ends, s32[64,256]{1,0:T(8,128)S(1)} %pad.4.segments, bf16[64,32,256]{2,1,0:T(8,128)(2,1)S(1)} %copy-done.7), custom_call_target="tpu_custom_call" | custom-call | flops 10000000000 | bytes 80000000 | tf_op jit(solution)/shard_map/student_weights/pallas_call | solution.py:273
  125.2 0.0 copy-start.4
  125.2 1.0 copy-done.4
  126.1 0.0 all-to-all-done.1.slabs
  126.1 0.0 copy-start.5
  126.1 1.2 copy-done.5
  127.4 89.2 %relation_gradient.1 = bf16[64,32,256]{2,1,0:T(8,128)(2,1)S(1)} custom-call(s32[1]{0:T(128)} %get-tuple-element.16.count_in, s32[640]{0:T(1024)S(1)} %get-tuple-element.17.pairs, s32[64,256]{1,0:T(8,128)S(1)} %pad.4.segments, bf16[64,80,256]{2,1,0:T(8,128)(2,1)S(1)} %all-to-all-done.1.slabs, f32[512,224,256]{2,1,0:T(8,128)} %get-tuple-element.18.made, ...), custom_call_target="tpu_custom_call" | custom-call | flops 20000000000 | bytes 80000000 | tf_op jit(solution)/shard_map/relation_gradient/pallas_call | solution.py:405
  216.5 0.0 copy-start.3
  216.6 1.0 copy-done.3
  217.5 9.8 %all-to-all-start.2 = ((bf16[64,32,256]{2,1,0:T(8,128)(2,1)}), bf16[64,32,256]{2,1,0:T(8,128)(2,1)S(1)}, u32[]{:S(2)}, u32[]{:S(2)}) async-start(bf16[64,32,256]{2,1,0:T(8,128)(2,1)} %copy-done.3), calls=%async_computation.2 | async-start | bytes 2097152 | tf_op jit(solution)/shard_map/all_to_all | solution.py:484
  227.3 6.3 %constant_dynamic-slice_fusion = (bf16[1024,1024]{1,0:T(8,128)(2,1)S(1)}, bf16[1024,1024]{1,0:T(8,128)(2,1)}, bf16[1024,1024]{1,0:T(8,128)(2,1)}, bf16[1024,1024]{1,0:T(8,128)(2,1)}) fusion(bf16[2048,1024]{1,0:T(8,128)(2,1)} %wk.1, s32[]{:T(128)S(6)} %select_n.9, s32[]{:T(128)S(6)} %select_n.8, bf16[2048,1024]{1,0:T(8,128)(2,1)} %wq.1), kind=kLoop, calls=%fused_computation.2 | loop fusion | bytes 16777224 | tf_op jit(solution)/shard_map/dynamic_slice | solution.py:480
  233.7 9.4 %all-to-all-done.2.grads = bf16[64,32,256]{2,1,0:T(8,128)(2,1)S(1)} async-done(((bf16[64,32,256]{2,1,0:T(8,128)(2,1)}), bf16[64,32,256]{2,1,0:T(8,128)(2,1)S(1)}, u32[]{:S(2)}, u32[]{:S(2)}) %all-to-all-start.2) | async-done | bytes 1048608 | tf_op jit(solution)/shard_map/all_to_all | solution.py:484
  243.1 0.0 copy-start.1
  243.1 1.6 copy-done.1
  244.7 0.0 copy-start.2
  244.7 1.6 copy-done.2
  246.2 0.0 copy-start
  246.2 1.3 unproject.3
  247.6 4.0 %collective-permute-start = (bf16[224,1024]{1,0:T(8,128)(2,1)S(1)}, bf16[224,1024]{1,0:T(8,128)(2,1)S(1)}, u32[]{:S(2)}, u32[]{:S(2)}) collective-permute-start(bf16[224,1024]{1,0:T(8,128)(2,1)S(1)} %unproject.3), channel_id=1, source_target_pairs={{0,1},{1,0},{2,3},{3,2},{4,5},{5,4},{6,7},{7,6},{8,9},{9,8},{10,11... | collective-permute-start | bytes 1376264 | tf_op jit(solution)/shard_map/ppermute | solution.py:486
  251.6 0.0 copy-done
  251.6 1.3 unproject.2
  252.9 0.1 collective-permute-done
  253.0 0.9 add_convert_fusion
  (2 shorter events, 0.0 us)
Async XLA Ops:
  6.6 29.1 %all-to-all-start = ((bf16[64,32,256]{2,1,0:T(8,128)(2,1)}), bf16[64,32,256]{2,1,0:T(8,128)(2,1)S(1)}, u32[]{:S(2)}, u32[]{:S(2)}) async-start(bf16[64,32,256]{2,1,0:T(8,128)(2,1)} %bitcast.5), calls=%async_computation | async-start | bytes 2097152 | tf_op jit(solution)/shard_map/all_to_all | solution.py:473
  35.8 1.0 copy-start.6
  36.8 5.2 %copy-start.8 = (s32[14336]{0:T(1024)S(1)}, s32[14336]{0:T(1024)}, u32[]{:S(2)}) copy-start(s32[14336]{0:T(1024)} %param.12) | copy-start | bytes 172036
  36.8 89.4 %all-to-all-start.1 = ((bf16[64,80,256]{2,1,0:T(8,128)(2,1)}), bf16[64,80,256]{2,1,0:T(8,128)(2,1)S(1)}, u32[]{:S(2)}, u32[]{:S(2)}) async-start(bf16[64,80,256]{2,1,0:T(8,128)(2,1)} %bitcast.4), calls=%async_computation.1 | async-start | bytes 5242880 | tf_op jit(solution)/shard_map/all_to_all | solution.py:474
  42.4 1.2 copy-start.7
  125.2 1.0 copy-start.4
  126.1 1.2 copy-start.5
  216.5 1.0 copy-start.3
  217.5 25.5 %all-to-all-start.2 = ((bf16[64,32,256]{2,1,0:T(8,128)(2,1)}), bf16[64,32,256]{2,1,0:T(8,128)(2,1)S(1)}, u32[]{:S(2)}, u32[]{:S(2)}) async-start(bf16[64,32,256]{2,1,0:T(8,128)(2,1)} %copy-done.3), calls=%async_computation.2 | async-start | bytes 2097152 | tf_op jit(solution)/shard_map/all_to_all | solution.py:484
  243.1 1.6 copy-start.1
  244.7 1.6 copy-start.2
  246.2 5.3 %copy-start = (bf16[1024,1024]{1,0:T(8,128)(2,1)S(1)}, bf16[1024,1024]{1,0:T(8,128)(2,1)}, u32[]{:S(2)}) copy-start(bf16[1024,1024]{1,0:T(8,128)(2,1)} %get-tuple-element.23.wq) | copy-start | bytes 6291460
  247.6 5.5 %collective-permute-start = (bf16[224,1024]{1,0:T(8,128)(2,1)S(1)}, bf16[224,1024]{1,0:T(8,128)(2,1)S(1)}, u32[]{:S(2)}, u32[]{:S(2)}) collective-permute-start(bf16[224,1024]{1,0:T(8,128)(2,1)S(1)} %unproject.3), channel_id=1, source_target_pairs={{0,1},{1,0},{2,3},{3,2},{4,5},{5,4},{6,7},{7,6},{8,9},{9,8},{10,11... | collective-permute-start | bytes 1376264 | tf_op jit(solution)/shard_map/ppermute | solution.py:486

commit v12 on v10

--- a/solution.py
+++ b/solution.py
@@ -163,7 +163,7 @@
     key_block = jnp.minimum(key, blocks - 1)
     operand = weights[jnp.minimum(query, blocks - 1)]
     part = jnp.where(diagonal == 1, 0.0, sums[query])
-    for low, high in halves(rows):
+    for low, high in ((0, rows),):
         scores = jnp.dot(keys[key_block, low:high], operand, preferred_element_type=f32)
         made = jnp.exp(scores * scale + causal[diagonal, low:high])
         target[low:high] = made

time: 269 us -> 265 us (0.985)
  Pallas kernels: 201 us -> 195 us
    pallas_call x1, Pallas kernels: 89.3 us -> 85.5 us  [student_weights(): pl.pallas_call(functools.partial(student_kernel, blocks), out_shape=(jax....]
  transfers between devices with their start and end apart: 4 -> 4, of which waited for: 3 -> 3; matrix products, arithmetic and copies ran while one was open for 2% -> 3% of each run, Pallas kernels for 35% -> 34%
where the time goes in v12:
time: 265 us; the launch traced here: 264 us
  Pallas kernels  195 us (74%)
  starting transfers between devices  30.9 us (12%)
  waiting for transfers between devices  22.4 us (8%)
  local copies, waits for them, and re-layouts  15.3 us (6%)
    pallas_call x1, Pallas kernels, relation_gradient(): pl.pallas_call(functools.partial(gradient_kernel, blocks), out_shape=jax....  95.8 us
    pallas_call x1, Pallas kernels, student_weights(): pl.pallas_call(functools.partial(student_kernel, blocks), out_shape=(jax....  85.5 us
    all_to_all x1, waiting for transfers between devices, shards(): lax.all_to_all(student.reshape(-1, *student.shape[2:]), 'ctx', 0, 0, tile...  12.9 us
    all_to_all x1, starting transfers between devices, shards(): lax.all_to_all(student.reshape(-1, *student.shape[2:]), 'ctx', 0, 0, tile...  12 us
    all_to_all x1, starting transfers between devices, shards(): back = lax.all_to_all(turned, 'ctx', 0, 0, tiled=True)  9.78 us
    all_to_all x1, waiting for transfers between devices, shards(): back = lax.all_to_all(turned, 'ctx', 0, 0, tiled=True)  9.39 us
    unnamed x18, local copies, waits for them, and re-layouts  8.57 us
    pallas_call x1, Pallas kernels, project(): pl.pallas_call(project_kernel, grid=(heads // PACK,), out_shape=jax.Shape...  6.64 us
  transfers between devices with their start and end apart: 4, of which 3 were waited for; matrix products, arithmetic and copies ran while one was open for 3% of the time, Pallas kernels for 34%

profile of v12, /device:TPU:1, one launch (start us, length us, event | category | flops | bytes accessed | tf_op | source)
XLA Modules:
  0.0 264.4 jit_solution(16554799570304075205)
XLA Ops:
  0.0 6.6 %project_student.1 = bf16[2,32,32,256]{3,2,1,0:T(8,128)(2,1)} custom-call(s32[1,7]{1,0:T(1,128)} %mask.1, bf16[224,2048]{1,0:T(8,128)(2,1)} %hidden.1, bf16[2048,1024]{1,0:T(8,128)(2,1)} %wq.1, bf16[2048,1024]{1,0:T(8,128)(2,1)} %wk.1), custom_call_target="tpu_custom_call" | custom-call | flops 1879048192 | bytes 10000000 | tf_op jit(solution)/shard_map/project_student/pallas_call | solution.py:57
  6.6 12.0 %all-to-all-start = ((bf16[64,32,256]{2,1,0:T(8,128)(2,1)}), bf16[64,32,256]{2,1,0:T(8,128)(2,1)S(1)}, u32[]{:S(2)}, u32[]{:S(2)}) async-start(bf16[64,32,256]{2,1,0:T(8,128)(2,1)} %bitcast.5), calls=%async_computation | async-start | bytes 2097152 | tf_op jit(solution)/shard_map/all_to_all | solution.py:473
  18.6 4.3 %turn_teacher.1 = bf16[2,32,80,256]{3,2,1,0:T(8,128)(2,1)} custom-call(bf16[224,2560]{1,0:T(8,128)(2,1)} %tq.1, bf16[224,2560]{1,0:T(8,128)(2,1)} %tk.1), custom_call_target="tpu_custom_call" | custom-call | bytes 5000000 | tf_op jit(solution)/shard_map/turn_teacher/pallas_call | solution.py:89
  22.9 12.9 %all-to-all-done.slabs_in = bf16[64,32,256]{2,1,0:T(8,128)(2,1)S(1)} async-done(((bf16[64,32,256]{2,1,0:T(8,128)(2,1)}), bf16[64,32,256]{2,1,0:T(8,128)(2,1)S(1)}, u32[]{:S(2)}, u32[]{:S(2)}) %all-to-all-start) | async-done | bytes 1048608 | tf_op jit(solution)/shard_map/all_to_all | solution.py:473
  35.8 0.0 copy-start.6
  35.8 1.0 copy-done.6
  36.8 0.0 copy-start.8
  36.8 5.2 %all-to-all-start.1 = ((bf16[64,80,256]{2,1,0:T(8,128)(2,1)}), bf16[64,80,256]{2,1,0:T(8,128)(2,1)S(1)}, u32[]{:S(2)}, u32[]{:S(2)}) async-start(bf16[64,80,256]{2,1,0:T(8,128)(2,1)} %bitcast.4), calls=%async_computation.1 | async-start | bytes 5242880 | tf_op jit(solution)/shard_map/all_to_all | solution.py:474
  41.9 0.0 copy-done.8
  42.0 0.1 slice.6
  42.1 0.2 slice.7
  42.3 0.1 reshape.9
  42.4 0.0 copy-start.7
  42.4 1.2 copy-done.7
  43.6 85.5 %student_weights.1 = (f32[512,224,256]{2,1,0:T(8,128)}, f32[64,8,256]{2,1,0:T(8,128)S(1)}, bf16[64,32,256]{2,1,0:T(8,128)(2,1)S(1)}, s32[640]{0:T(1024)S(1)}, s32[1]{0:T(128)}) custom-call(s32[2,64]{1,0:T(2,128)S(1)} %pad_add_fusion.ends, s32[64,256]{1,0:T(8,128)S(1)} %pad.4.segments, bf16[64,32,256]{2,1,0:T(8,128)(2,1)S(1)} %copy-done.7), custom_call_target="tpu_custom_call" | custom-call | flops 10000000000 | bytes 80000000 | tf_op jit(solution)/shard_map/student_weights/pallas_call | solution.py:273
  129.1 0.0 copy-start.4
  129.1 1.0 copy-done.4
  130.0 0.0 all-to-all-done.1.slabs
  130.1 0.0 copy-start.5
  130.1 1.2 copy-done.5
  131.3 95.8 %relation_gradient.1 = bf16[64,32,256]{2,1,0:T(8,128)(2,1)S(1)} custom-call(s32[1]{0:T(128)} %get-tuple-element.16.count_in, s32[640]{0:T(1024)S(1)} %get-tuple-element.17.pairs, s32[64,256]{1,0:T(8,128)S(1)} %pad.4.segments, bf16[64,80,256]{2,1,0:T(8,128)(2,1)S(1)} %all-to-all-done.1.slabs, f32[512,224,256]{2,1,0:T(8,128)} %get-tuple-element.18.made, ...), custom_call_target="tpu_custom_call" | custom-call | flops 20000000000 | bytes 80000000 | tf_op jit(solution)/shard_map/relation_gradient/pallas_call | solution.py:405
  227.0 0.0 copy-start.3
  227.1 1.0 copy-done.3
  228.0 9.8 %all-to-all-start.2 = ((bf16[64,32,256]{2,1,0:T(8,128)(2,1)}), bf16[64,32,256]{2,1,0:T(8,128)(2,1)S(1)}, u32[]{:S(2)}, u32[]{:S(2)}) async-start(bf16[64,32,256]{2,1,0:T(8,128)(2,1)} %copy-done.3), calls=%async_computation.2 | async-start | bytes 2097152 | tf_op jit(solution)/shard_map/all_to_all | solution.py:484
  237.8 6.3 %constant_dynamic-slice_fusion = (bf16[1024,1024]{1,0:T(8,128)(2,1)S(1)}, bf16[1024,1024]{1,0:T(8,128)(2,1)}, bf16[1024,1024]{1,0:T(8,128)(2,1)}, bf16[1024,1024]{1,0:T(8,128)(2,1)}) fusion(bf16[2048,1024]{1,0:T(8,128)(2,1)} %wk.1, s32[]{:T(128)S(6)} %select_n.9, s32[]{:T(128)S(6)} %select_n.8, bf16[2048,1024]{1,0:T(8,128)(2,1)} %wq.1), kind=kLoop, calls=%fused_computation.2 | loop fusion | bytes 16777224 | tf_op jit(solution)/shard_map/dynamic_slice | solution.py:480
  244.2 9.4 %all-to-all-done.2.grads = bf16[64,32,256]{2,1,0:T(8,128)(2,1)S(1)} async-done(((bf16[64,32,256]{2,1,0:T(8,128)(2,1)}), bf16[64,32,256]{2,1,0:T(8,128)(2,1)S(1)}, u32[]{:S(2)}, u32[]{:S(2)}) %all-to-all-start.2) | async-done | bytes 1048608 | tf_op jit(solution)/shard_map/all_to_all | solution.py:484
  253.6 0.0 copy-start.1
  253.6 1.6 copy-done.1
  255.2 0.0 copy-start.2
  255.2 1.6 copy-done.2
  256.7 0.0 copy-start
  256.7 1.3 unproject.3
  258.1 4.0 %collective-permute-start = (bf16[224,1024]{1,0:T(8,128)(2,1)S(1)}, bf16[224,1024]{1,0:T(8,128)(2,1)S(1)}, u32[]{:S(2)}, u32[]{:S(2)}) collective-permute-start(bf16[224,1024]{1,0:T(8,128)(2,1)S(1)} %unproject.3), channel_id=1, source_target_pairs={{0,1},{1,0},{2,3},{3,2},{4,5},{5,4},{6,7},{7,6},{8,9},{9,8},{10,11... | collective-permute-start | bytes 1376264 | tf_op jit(solution)/shard_map/ppermute | solution.py:486
  262.1 0.0 copy-done
  262.1 1.3 unproject.2
  263.4 0.1 collective-permute-done
  263.5 0.9 add_convert_fusion
  (2 shorter events, 0.0 us)
Async XLA Ops:
  6.6 29.1 %all-to-all-start = ((bf16[64,32,256]{2,1,0:T(8,128)(2,1)}), bf16[64,32,256]{2,1,0:T(8,128)(2,1)S(1)}, u32[]{:S(2)}, u32[]{:S(2)}) async-start(bf16[64,32,256]{2,1,0:T(8,128)(2,1)} %bitcast.5), calls=%async_computation | async-start | bytes 2097152 | tf_op jit(solution)/shard_map/all_to_all | solution.py:473
  35.8 1.0 copy-start.6
  36.8 5.2 %copy-start.8 = (s32[14336]{0:T(1024)S(1)}, s32[14336]{0:T(1024)}, u32[]{:S(2)}) copy-start(s32[14336]{0:T(1024)} %param.12) | copy-start | bytes 172036
  36.8 93.3 %all-to-all-start.1 = ((bf16[64,80,256]{2,1,0:T(8,128)(2,1)}), bf16[64,80,256]{2,1,0:T(8,128)(2,1)S(1)}, u32[]{:S(2)}, u32[]{:S(2)}) async-start(bf16[64,80,256]{2,1,0:T(8,128)(2,1)} %bitcast.4), calls=%async_computation.1 | async-start | bytes 5242880 | tf_op jit(solution)/shard_map/all_to_all | solution.py:474
  42.4 1.2 copy-start.7
  129.1 1.0 copy-start.4
  130.1 1.2 copy-start.5
  227.0 1.0 copy-start.3
  228.0 25.5 %all-to-all-start.2 = ((bf16[64,32,256]{2,1,0:T(8,128)(2,1)}), bf16[64,32,256]{2,1,0:T(8,128)(2,1)S(1)}, u32[]{:S(2)}, u32[]{:S(2)}) async-start(bf16[64,32,256]{2,1,0:T(8,128)(2,1)} %copy-done.3), calls=%async_computation.2 | async-start | bytes 2097152 | tf_op jit(solution)/shard_map/all_to_all | solution.py:484
  253.6 1.6 copy-start.1
  255.2 1.6 copy-start.2
  256.7 5.3 %copy-start = (bf16[1024,1024]{1,0:T(8,128)(2,1)S(1)}, bf16[1024,1024]{1,0:T(8,128)(2,1)}, u32[]{:S(2)}) copy-start(bf16[1024,1024]{1,0:T(8,128)(2,1)} %get-tuple-element.23.wq) | copy-start | bytes 6291460
  258.1 5.5 %collective-permute-start = (bf16[224,1024]{1,0:T(8,128)(2,1)S(1)}, bf16[224,1024]{1,0:T(8,128)(2,1)S(1)}, u32[]{:S(2)}, u32[]{:S(2)}) collective-permute-start(bf16[224,1024]{1,0:T(8,128)(2,1)S(1)} %unproject.3), channel_id=1, source_target_pairs={{0,1},{1,0},{2,3},{3,2},{4,5},{5,4},{6,7},{7,6},{8,9},{9,8},{10,11... | collective-permute-start | bytes 1376264 | tf_op jit(solution)/shard_map/ppermute | solution.py:486
